TPU v7x, 128 devices: a whole 4x4x4 slice. The times are simulated.
128 devices in a mesh: cand: 8 (over z_hi, y), tp: 16 (over x, z_lo, core).
Axes of the slice: x: 4, y: 4, z: 4 (z_hi: 2, z_lo: 2; z = z_hi * 2 + z_lo), core: 2. Of those that a mesh axis runs over, the one named last changes fastest.
Arguments:
- tokens: bfloat16 [512, 4096], P(None, 'cand'), may hold values from -6 to 6
- attn_gain: float32 [4096], P('cand'), may hold values from 0.5 to 1.5
- ffn_gain: float32 [4096], P('cand'), may hold values from 0.5 to 1.5
- w_query: bfloat16 [4096, 4096], P('cand', 'tp'), may hold values from -40 to 40
- w_key: bfloat16 [4096, 1024], P('cand'), may hold values from -1 to 1
- w_value: bfloat16 [4096, 1024], P('cand'), may hold values from -0.09375 to 0.09375
- w_out: bfloat16 [4096, 4096], P('tp', 'cand'), may hold values from -0.09375 to 0.09375
- w_gate: bfloat16 [4096, 14336], P('cand', 'tp'), may hold values from -0.09375 to 0.09375
- w_up: bfloat16 [4096, 14336], P('cand', 'tp'), may hold values from -0.09375 to 0.09375
- w_down: bfloat16 [14336, 4096], P('tp', 'cand'), may hold values from -0.046875 to 0.046875
- doc_ids: int32 [512], replicated, may hold values from 0 to 3, never falling along the last dimension, each value on 1 to 256 neighbouring positions
- widths: int32 [8], replicated, may hold values from 16 to 12288, as said below
Outputs:
- grad_gate: bfloat16 [8, 4096, 12288], P('cand', None, 'tp')
- grad_up: bfloat16 [8, 4096, 12288], P('cand', None, 'tp')
- grad_down: bfloat16 [8, 12288, 4096], P('cand', 'tp')
Inputs may be any that keep to these rules, and one draw needn't show every extreme that they name: `widths`: each entry is a multiple of 16; some candidate keeps 12288 units.
All inputs are finite; a program needn't handle non-finite values.
Results may differ from a plain program's by a relative error of at most 0.035.
Values may be sent and summed in bfloat16 or wider, within the bound.
No kernel may reach another device: no remote copies, remote signals or barrier semaphores. Data moves between devices by JAX's collectives and lax.ppermute only.
A program may use at most 192 MiB of HBM per device.

v0:
```python
import jax
import jax.numpy as jnp
from jax import lax
from jax.sharding import PartitionSpec as P

D = 4096
HEADS = 32
KV_HEADS = 8
HEAD_DIM = 128
CAND_DEV = 768


EPSILON = 1e-05


def contract_rows(left, right):
    return lax.dot_general(
        left, right, (((0,), (0,)), ((), ())), preferred_element_type=jnp.float32
    )


def shards(
    tokens,
    attn_gain,
    ffn_gain,
    w_query,
    w_key,
    w_value,
    w_out,
    w_gate,
    w_up,
    w_down,
    doc_ids,
    widths,
):
    cand_index = lax.axis_index("cand")
    tp_index = lax.axis_index("tp")
    tp_count = lax.axis_size("tp")
    tok_count = tokens.shape[0]
    row_count = tok_count // tp_count
    slot_count = CAND_DEV
    wide_in = tokens.astype(jnp.float32)
    squares = lax.psum(jnp.sum(wide_in * wide_in, axis=1), "cand")
    normed = (wide_in * lax.rsqrt(squares / D + EPSILON)[:, None] * attn_gain[None, :]).astype(
        jnp.bfloat16
    )
    heads_dev = w_query.shape[1] // HEAD_DIM
    group_size = HEADS // KV_HEADS
    kv_index = tp_index * heads_dev // group_size
    key_cols = lax.dynamic_slice_in_dim(w_key, kv_index * HEAD_DIM, HEAD_DIM, 1)
    value_cols = lax.dynamic_slice_in_dim(w_value, kv_index * HEAD_DIM, HEAD_DIM, 1)
    query_part = jnp.dot(normed, w_query, preferred_element_type=jnp.float32)
    key_part = jnp.dot(normed, key_cols, preferred_element_type=jnp.float32)
    value_part = jnp.dot(normed, value_cols, preferred_element_type=jnp.float32)
    query_sum, key_sum, value_sum = lax.psum((query_part, key_part, value_part), "cand")
    query = query_sum.astype(jnp.bfloat16).reshape(tok_count, heads_dev, HEAD_DIM)
    key_rows = key_sum.astype(jnp.bfloat16)
    value_rows = value_sum.astype(jnp.bfloat16)
    scores = jnp.einsum(
        "qhd,kd->hqk", query, key_rows, preferred_element_type=jnp.float32
    ) * HEAD_DIM ** (-0.5)
    position = lax.iota(jnp.int32, tok_count)
    allowed = (position[None, :] <= position[:, None]) & (doc_ids[None, :] == doc_ids[:, None])
    scores = jnp.where(allowed[None], scores, -1e30)
    peak_score = jnp.max(scores, axis=-1, keepdims=True)
    expo = jnp.exp(scores - peak_score)
    weights_bf = (expo / jnp.sum(expo, axis=-1, keepdims=True)).astype(jnp.bfloat16)
    attended = jnp.einsum("hqk,kd->qhd", weights_bf, value_rows, preferred_element_type=jnp.float32)
    attended = attended.astype(jnp.bfloat16).reshape(tok_count, heads_dev * HEAD_DIM)
    attn_total = lax.psum(jnp.dot(attended, w_out, preferred_element_type=jnp.float32), "tp")
    residual = (wide_in + attn_total).astype(jnp.bfloat16)
    wide_res = residual.astype(jnp.float32)
    res_squares = lax.psum(jnp.sum(wide_res * wide_res, axis=1), "cand")
    ffn_in = (wide_res * lax.rsqrt(res_squares / D + EPSILON)[:, None] * ffn_gain[None, :]).astype(
        jnp.bfloat16
    )
    gate_part = jnp.dot(ffn_in, w_gate, preferred_element_type=jnp.float32)
    up_part = jnp.dot(ffn_in, w_up, preferred_element_type=jnp.float32)
    gate_sum, up_sum = lax.psum((gate_part, up_part), "cand")
    sigmoid_gate = jax.nn.sigmoid(gate_sum)
    activated = gate_sum * sigmoid_gate
    hidden = (activated * up_sum).astype(jnp.bfloat16)
    out_part = jnp.dot(hidden, w_down, preferred_element_type=jnp.float32)
    target_block = lax.psum(out_part, "tp").astype(jnp.bfloat16)
    target_all = lax.all_gather(target_block, "cand", axis=1, tiled=True)
    target = lax.dynamic_slice_in_dim(target_all, tp_index * row_count, row_count, 0)
    ffn_all = lax.all_gather(ffn_in, "cand", axis=1, tiled=True)
    slot_ids = lax.iota(jnp.int32, slot_count)
    cand_width = jnp.sum(jnp.where(lax.iota(jnp.int32, widths.shape[0]) == cand_index, widths, 0))
    live_slots = cand_width // tp_count
    keep_mask = (slot_ids < live_slots)[None, :]
    hidden_sel = hidden[:, :slot_count]
    used_hidden = jnp.where(keep_mask, hidden_sel, jnp.zeros((), jnp.bfloat16))
    down_local = w_down[:slot_count]
    down_all = lax.all_gather(down_local, "cand", axis=1, tiled=True)
    pred_part = jnp.dot(used_hidden, down_all, preferred_element_type=jnp.float32)
    predicted = lax.psum_scatter(pred_part, "tp", scatter_dimension=0, tiled=True)
    grad_rows = (predicted - target.astype(jnp.float32)).astype(jnp.bfloat16)
    grad_all = lax.all_gather(grad_rows, "tp", axis=0, tiled=True)
    back_sum = lax.dot_general(
        grad_all, down_all, (((1,), (1,)), ((), ())), preferred_element_type=jnp.float32
    )
    gate_sel = gate_sum[:, :slot_count]
    sigmoid_sel = sigmoid_gate[:, :slot_count]
    slope = sigmoid_sel * (1.0 + gate_sel * (1.0 - sigmoid_sel))
    gate_term = jnp.where(keep_mask, back_sum * up_sum[:, :slot_count] * slope, 0.0).astype(
        jnp.bfloat16
    )
    up_term = jnp.where(keep_mask, back_sum * activated[:, :slot_count], 0.0).astype(jnp.bfloat16)
    gate_grad = contract_rows(ffn_all, gate_term).astype(jnp.bfloat16)
    up_grad = contract_rows(ffn_all, up_term).astype(jnp.bfloat16)
    down_grad = contract_rows(used_hidden, grad_all).astype(jnp.bfloat16)
    return (gate_grad[None], up_grad[None], down_grad[None])


def solution(mesh):
    in_specs = (
        P(None, "cand"),
        P("cand"),
        P("cand"),
        P("cand", "tp"),
        P("cand", None),
        P("cand", None),
        P("tp", "cand"),
        P("cand", "tp"),
        P("cand", "tp"),
        P("tp", "cand"),
        P(),
        P(),
    )
    out_specs = (P("cand", None, "tp"), P("cand", None, "tp"), P("cand", "tp", None))
    return jax.shard_map(shards, mesh=mesh, in_specs=in_specs, out_specs=out_specs, check_vma=False)
```

profile of v0, /device:TPU:1, one launch (start us, length us, event | category | flops | bytes accessed | tf_op | source)
XLA Modules:
  0.0 796.0 jit_solution(9030950723977695880)
XLA Ops:
  9.5 22.4 %psum.63 = f32[512]{0:T(512)S(1)} all-reduce(f32[512]{0:T(512)S(1)} %fusion.15), channel_id=1, replica_groups=mesh['cand'=8,'tp'=16] {'cand'}, use_global_device_ids=true, to_apply=%region_1.0 | all-reduce | flops 512 | bytes 4096 | tf_op jit(solution)/shard_map/psum | solution.py:43
  31.9 1.5 fusion.79
  33.8 1.3 fusion.51
  35.1 64.0 %all-reduce.10 = (bf16[512,256]{1,0:T(8,128)(2,1)S(1)}, bf16[512,128]{1,0:T(8,128)(2,1)S(1)}, bf16[512,128]{0,1:T(8,128)(2,1)S(1)}) all-reduce(f32[512,256]{1,0:T(8,128)S(1)} %fusion.79, f32[512,128]{1,0:T(8,128)S(1)} %fusion.48, f32[512,128]{0,1:T(8,128)S(1)} %fusion.51), channel_id=1, replica_groups=mesh['cand'=8,'tp'=16] {'cand'}, use_global_device_ids=true, to_apply=%region_4.5 | all-reduce | flops 262144 | bytes 1572864 | tf_op jit(solution)/shard_map/psum | solution.py:55
  101.2 1.3 fusion.89
  102.6 135.5 %all-reduce.7.cloned.1.call-done = f32[512,512]{1,0:T(8,128)} async-done(((f32[512,512]{1,0:T(8,128)}), f32[512,512]{1,0:T(8,128)}) %all-reduce.7.cloned.1.call-update) | async-done | bytes 1048592 | tf_op jit(solution)/shard_map/psum | solution.py:70
  238.1 1.5 fusion.12
  239.6 20.2 %psum.68 = f32[512]{0:T(512)S(1)} all-reduce(f32[512]{0:T(512)S(1)} %fusion.12), channel_id=1, replica_groups=mesh['cand'=8,'tp'=16] {'cand'}, use_global_device_ids=true, to_apply=%region_9.10 | all-reduce | flops 512 | bytes 4096 | tf_op jit(solution)/shard_map/psum | solution.py:73
  260.1 1.9 fusion.90
  262.0 1.9 fusion.91
  266.1 97.4 %all-reduce.9.cloned.1.call-done = (f32[512,896]{1,0:T(8,128)}, f32[512,896]{1,0:T(8,128)}) async-done(((f32[512,896]{1,0:T(8,128)}, f32[512,896]{1,0:T(8,128)}), (f32[512,896]{1,0:T(8,128)}, f32[512,896]{1,0:T(8,128)})) %all-reduce.9.cloned.1.call-update) | async-done | bytes 3670032 | tf_op jit(solution)/shard_map/psum | solution.py:79
  363.5 4.4 fusion.83
  368.6 68.7 %all-reduce.11 = bf16[512,512]{1,0:T(8,128)(2,1)} all-reduce(f32[512,512]{1,0:T(8,128)S(1)} %fusion.92), channel_id=1, replica_groups=mesh['cand'=8,'tp'=16] {'tp'}, use_global_device_ids=true, to_apply=%region_14.15 | all-reduce | flops 262144 | bytes 1572864 | tf_op jit(solution)/shard_map/psum | solution.py:84
  440.5 34.3 %all-gather.7.cloned.1.call-done = bf16[768,4096]{1,0:T(8,128)(2,1)} async-done(((bf16[768,512]{1,0:T(8,128)(2,1)}), bf16[768,4096]{1,0:T(8,128)(2,1)}) %all-gather.7.cloned.1.call-update) | async-done | bytes 6291472 | tf_op jit(solution)/shard_map/all_gather | solution.py:95
  474.8 8.4 %fusion.30 = f32[512,4096]{1,0:T(8,128)} fusion(bf16[768,4096]{1,0:T(8,128)(2,1)} %all-gather.7.cloned.1.call-done, bf16[512,896]{1,0:T(8,128)(2,1)S(1)} %get-tuple-element.9, pred[768]{0:T(1024)(128)(4,1)S(1)} %iota_compare_fusion.1), kind=kOutput, calls=%fused_computation.47 | convolution fusion | flops 3221618688 | bytes 15467520 | tf_op jit(solution)/shard_map/dot_general | solution.py:96
  483.2 71.4 %all-gather.9.cloned.1.call-done = bf16[512,4096]{1,0:T(8,128)(2,1)} async-done(((bf16[512,512]{1,0:T(8,128)(2,1)}), bf16[512,4096]{1,0:T(8,128)(2,1)}) %all-gather.9.cloned.1.call-update) | async-done | bytes 4194320 | tf_op jit(solution)/shard_map/all_gather | solution.py:85
  554.6 98.3 %reduce-scatter.2.cloned.1.call-done = f32[32,4096]{1,0:T(8,128)} async-done(((f32[512,4096]{1,0:T(8,128)}), f32[32,4096]{1,0:T(8,128)}) %reduce-scatter.2.cloned.1.call-update) | async-done | bytes 524304 | tf_op jit(solution)/shard_map/reduce_scatter | solution.py:97
  653.0 1.9 subtract_convert_fusion
  655.6 38.7 %all-gather.11.cloned.1.call-done = bf16[512,4096]{1,0:T(8,128)(2,1)} async-done(((bf16[32,4096]{1,0:T(8,128)(2,1)}), bf16[512,4096]{1,0:T(8,128)(2,1)}) %all-gather.11.cloned.1.call-update) | async-done | bytes 4194320 | tf_op jit(solution)/shard_map/all_gather | solution.py:99
  694.3 7.7 fusion.3
  702.0 7.0 fusion.93
  709.0 64.7 %all-gather.5.cloned.1.call-done = bf16[512,4096]{1,0:T(8,128)(2,1)} async-done(((bf16[512,512]{1,0:T(8,128)(2,1)}), bf16[512,4096]{1,0:T(8,128)(2,1)}) %all-gather.5.cloned.1.call-update) | async-done | bytes 4194320 | tf_op jit(solution)/shard_map/all_gather | solution.py:87
  773.7 10.0 %fusion.1 = bf16[1,4096,768]{2,1,0:T(8,128)(2,1)} fusion(bf16[512,4096]{1,0:T(8,128)(2,1)} %all-gather.5.cloned.1.call-done, f32[512,896]{1,0:T(8,128)S(1)} %copy-done.5, f32[512,768]{1,0:T(8,128)} %fusion.93, f32[512,896]{1,0:T(8,128)} %get-tuple-element.7, f32[512,896]{1,0:T(8,128)} %get-tuple-element.10, pred[768]{0:T(1024)(128)(4,1)S(1)} %iota_compare_fusion.1), kind=kOutput, calls=%fused_computation.4 | convolution fusion | flops 3227516928 | bytes 16778240 | tf_op jit(solution)/shard_map/dot_general | solution.py:17
  783.7 5.4 fusion.2
  (60 shorter events, 9.4 us)
Async XLA Ops:
  7.2 26.2 %copy-start = (bf16[512,1024]{1,0:T(8,128)(2,1)S(1)}, bf16[512,1024]{1,0:T(8,128)(2,1)}, u32[]{:S(2)}) copy-start(bf16[512,1024]{1,0:T(8,128)(2,1)} %param.16) | copy-start | bytes 3145732
  7.2 26.2 %copy-start.3 = (bf16[512,512]{1,0:T(8,128)(2,1)S(1)}, bf16[512,512]{1,0:T(8,128)(2,1)}, u32[]{:S(2)}) copy-start(bf16[512,512]{1,0:T(8,128)(2,1)} %param.12) | copy-start | bytes 1572868
  7.2 26.2 %copy-start.14 = (f32[512]{0:T(512)S(1)}, f32[512]{0:T(512)}, u32[]{:S(2)}) copy-start(f32[512]{0:T(512)} %param.13) | copy-start | bytes 6148
  7.2 230.9 %all-reduce.7.cloned.1.call-start = ((), (), s32[]{:S(2)}) async-start(), calls=%async_computation.1 | async-start | bytes 2097152 | tf_op jit(solution)/shard_map/psum | solution.py:70
  100.0 1.2 copy-start.10
  101.2 158.6 %copy-start.11 = (f32[512]{0:T(512)S(1)}, f32[512]{0:T(512)}, u32[]{:S(2)}) copy-start(f32[512]{0:T(512)} %param.14) | copy-start | bytes 6148
  102.5 157.5 %copy-start.7 = (bf16[512,896]{1,0:T(8,128)(2,1)S(1)}, bf16[512,896]{1,0:T(8,128)(2,1)}, u32[]{:S(2)}) copy-start(bf16[512,896]{1,0:T(8,128)(2,1)} %param.19) | copy-start | bytes 2752516
  102.6 261.0 %all-reduce.9.cloned.1.call-start = ((), (), s32[]{:S(2)}) async-start(), calls=%async_computation.7 | async-start | bytes 7340032 | tf_op jit(solution)/shard_map/psum | solution.py:79
  238.1 21.7 %copy-start.4 = (f32[512,512]{1,0:T(8,128)S(1)}, f32[512,512]{1,0:T(8,128)}, u32[]{:S(2)}) copy-start(f32[512,512]{1,0:T(8,128)} %all-reduce.7.cloned.1.call-done) | copy-start | bytes 3145732
  260.0 3.9 copy-start.2
  260.0 2.0 copy-start.8
  263.9 1.2 copy-start.9
  264.0 210.8 %all-gather.7.cloned.1.call-start = ((), (), s32[]{:S(2)}) async-start(), calls=%async_computation.3 | async-start | bytes 7077888 | tf_op jit(solution)/shard_map/all_gather | solution.py:95
  266.1 288.5 %all-gather.9.cloned.1.call-start = ((), (), s32[]{:S(2)}) async-start(), calls=%async_computation.5 | async-start | bytes 4718592 | tf_op jit(solution)/shard_map/all_gather | solution.py:85
  367.9 69.5 %copy-start.15 = (s32[8]{0:T(128)S(1)}, s32[8]{0:T(128)}, u32[]{:S(2)}) copy-start(s32[8]{0:T(128)} %param.23) | copy-start | bytes 100
  437.3 215.6 %reduce-scatter.2.cloned.1.call-start = ((), (), s32[]{:S(2)}) async-start(), calls=%async_computation.4 | async-start | bytes 8912896 | tf_op jit(solution)/shard_map/reduce_scatter | solution.py:97
  483.2 211.1 %all-gather.11.cloned.1.call-start = ((), (), s32[]{:S(2)}) async-start(), calls=%async_computation.6 | async-start | bytes 4456448 | tf_op jit(solution)/shard_map/all_gather | solution.py:99
  654.8 118.9 %all-gather.5.cloned.1.call-start = ((), (), s32[]{:S(2)}) async-start(), calls=%async_computation.2 | async-start | bytes 4718592 | tf_op jit(solution)/shard_map/all_gather | solution.py:87
  694.3 7.7 copy-start.13
  702.0 71.7 %copy-start.5 = (f32[512,896]{1,0:T(8,128)S(1)}, f32[512,896]{1,0:T(8,128)}, u32[]{:S(2)}) copy-start(f32[512,896]{1,0:T(8,128)} %get-tuple-element.6) | copy-start | bytes 5505028
  773.7 10.0 %copy-start.6 = (f32[512,896]{1,0:T(8,128)S(1)}, f32[512,896]{1,0:T(8,128)}, u32[]{:S(2)}) copy-start(f32[512,896]{1,0:T(8,128)} %get-tuple-element.8) | copy-start | bytes 5505028
  773.7 10.0 %copy-start.12 = (bf16[512,4096]{1,0:T(8,128)(2,1)S(1)}, bf16[512,4096]{1,0:T(8,128)(2,1)}, u32[]{:S(2)}) copy-start(bf16[512,4096]{1,0:T(8,128)(2,1)} %all-gather.5.cloned.1.call-done) | copy-start | bytes 12582916
  773.7 10.0 %copy-start.16 = (f32[512,768]{1,0:T(8,128)S(1)}, f32[512,768]{1,0:T(8,128)}, u32[]{:S(2)}) copy-start(f32[512,768]{1,0:T(8,128)} %fusion.93) | copy-start | bytes 4718596
  783.7 5.4 copy-start.1
Sparse Core Ops, SparseCore 0:
  102.7 135.3 all-reduce.6
  264.1 99.3 all-reduce.8
  366.5 108.2 all-gather.6
  477.7 76.9 all-gather.8
  557.0 95.9 reduce-scatter.1
  655.2 39.0 all-gather.10
  696.7 76.9 all-gather.4
where the time goes:
time: 797 us; the launch traced here: 796 us
  waiting for transfers between devices  541 us (68%)
  blocking collectives  175 us (22%)
  matrix products  49.6 us (6%)
  between operations  16.8 us (2%)
  other arithmetic  10.9 us (1%)
    psum x1, waiting for transfers between devices, shards(): lax.psum(jnp.dot(attended, w_out, preferred_element_type=jnp.float32), 'tp')  135 us
    reduce_scatter x1, waiting for transfers between devices, shards(): lax.psum_scatter(pred_part, 'tp', scatter_dimension=0, tiled=True)  98.3 us
    psum x1, waiting for transfers between devices, shards(): gate_sum, up_sum = lax.psum((gate_part, up_part), 'cand')  97.4 us
    all_gather x1, waiting for transfers between devices, shards(): target_all = lax.all_gather(target_block, 'cand', axis=1, tiled=True)  71.4 us
    psum x1, blocking collectives, shards(): target_block = lax.psum(out_part, 'tp').astype(jnp.bfloat16)  68.7 us
    all_gather x1, waiting for transfers between devices, shards(): ffn_all = lax.all_gather(ffn_in, 'cand', axis=1, tiled=True)  64.7 us
    psum x1, blocking collectives, shards(): lax.psum((query_part, key_part, value_part), 'cand')  64 us
    all_gather x1, waiting for transfers between devices, shards(): grad_all = lax.all_gather(grad_rows, 'tp', axis=0, tiled=True)  38.7 us
  transfers between devices with their start and end apart: 7, of which 7 were waited for; matrix products, arithmetic and copies ran while one was open for 4% of the time, Pallas kernels for 0%

commit v1 on v0

v1 whole, which is shorter than its diff:
```python
import jax
import jax.numpy as jnp
from jax import lax
from jax.sharding import PartitionSpec as P

D = 4096
HEADS = 32
KV_HEADS = 8
HEAD_DIM = 128
CAND_DEV = 768
LANES = 128
EPSILON = 1e-05
BF = jnp.bfloat16
F32 = jnp.float32

CORE_PAIRS = [(i, i ^ 1) for i in range(16)]
SAME_CORE = [list(range(core, 16, 2)) for core in range(2)]


def two_parts(column):
    high = lax.reduce_precision(column, 8, 7)
    low = column - high
    pad = jnp.zeros((column.shape[0], LANES - 2), BF)
    return jnp.concatenate([high.astype(BF)[:, None], low.astype(BF)[:, None], pad], axis=1)


def exchange(blocks, axis, groups=None):
    return lax.all_to_all(blocks, axis, 0, 0, axis_index_groups=groups)


def sum_scatter(blocks, axis, groups=None):
    return jnp.sum(exchange(blocks, axis, groups).astype(F32), axis=0)


def gather_blocks(block, axis, count, groups=None):
    return exchange(jnp.broadcast_to(block[None], (count,) + block.shape), axis, groups)


def shards(
    tokens,
    attn_gain,
    ffn_gain,
    w_query,
    w_key,
    w_value,
    w_out,
    w_gate,
    w_up,
    w_down,
    doc_ids,
    widths,
):
    cand_index = lax.axis_index("cand")
    tp_index = lax.axis_index("tp")
    core = tp_index % 2
    cands = lax.axis_size("cand")
    tps = lax.axis_size("tp")
    chips = tps // 2
    tok_count = tokens.shape[0]
    width = tokens.shape[1]
    ff_dev = w_gate.shape[1]
    tok_cand = tok_count // cands
    tok_tp = tok_count // tps
    tok_half = tok_cand // 2

    down_all = lax.all_gather(w_down, "cand", axis=0)

    wide_in = tokens.astype(F32)
    scaled_in = (wide_in * attn_gain[None, :]).astype(BF)
    heads_dev = w_query.shape[1] // HEAD_DIM
    group_size = HEADS // KV_HEADS
    kv_index = tp_index * heads_dev // group_size
    key_cols = lax.dynamic_slice_in_dim(w_key, kv_index * HEAD_DIM, HEAD_DIM, 1)
    value_cols = lax.dynamic_slice_in_dim(w_value, kv_index * HEAD_DIM, HEAD_DIM, 1)
    parts = [
        jnp.dot(scaled_in, cols, preferred_element_type=F32).astype(BF)
        for cols in (w_query, key_cols, value_cols)
    ]
    parts.append(two_parts(jnp.sum(wide_in * wide_in, axis=1)))
    part = jnp.concatenate(parts, axis=1)
    total = sum_scatter(part.reshape(cands, tok_cand, part.shape[1]), "cand")
    qkv_width = part.shape[1] - LANES
    squares = total[:, qkv_width] + total[:, qkv_width + 1]
    qkv_rows = (total[:, :qkv_width] * lax.rsqrt(squares / D + EPSILON)[:, None]).astype(BF)
    qkv = gather_blocks(qkv_rows, "cand", cands).reshape(tok_count, qkv_width)
    q_width = heads_dev * HEAD_DIM
    query = qkv[:, :q_width].reshape(tok_count, heads_dev, HEAD_DIM)
    key_rows = qkv[:, q_width : q_width + HEAD_DIM]
    value_rows = qkv[:, q_width + HEAD_DIM :]

    scores = jnp.einsum(
        "qhd,kd->hqk", query, key_rows, preferred_element_type=F32
    ) * HEAD_DIM ** (-0.5)
    position = lax.iota(jnp.int32, tok_count)
    allowed = (position[None, :] <= position[:, None]) & (doc_ids[None, :] == doc_ids[:, None])
    scores = jnp.where(allowed[None], scores, -1e30)
    peak_score = jnp.max(scores, axis=-1, keepdims=True)
    expo = jnp.exp(scores - peak_score)
    weights_bf = (expo / jnp.sum(expo, axis=-1, keepdims=True)).astype(BF)
    attended = jnp.einsum("hqk,kd->qhd", weights_bf, value_rows, preferred_element_type=F32)
    attended = attended.astype(BF).reshape(tok_count, heads_dev * HEAD_DIM)
    out_part = jnp.dot(attended, w_out, preferred_element_type=F32).astype(BF)
    attn_rows = sum_scatter(out_part.reshape(tps, tok_tp, width), "tp")
    own_rows = lax.dynamic_slice_in_dim(tokens, tp_index * tok_tp, tok_tp, 0)
    residual_rows = (own_rows.astype(F32) + attn_rows).astype(BF)
    residual = gather_blocks(residual_rows, "tp", tps).reshape(tok_count, width)

    wide_res = residual.astype(F32)
    scaled_res = (wide_res * ffn_gain[None, :]).astype(BF)
    parts = [
        jnp.dot(scaled_res, cols, preferred_element_type=F32).astype(BF) for cols in (w_gate, w_up)
    ]
    parts.append(two_parts(jnp.sum(wide_res * wide_res, axis=1)))
    part = jnp.concatenate(parts, axis=1)
    total = sum_scatter(part.reshape(cands, tok_cand, part.shape[1]), "cand")
    squares = total[:, 2 * ff_dev] + total[:, 2 * ff_dev + 1]
    row_scale = lax.rsqrt(squares / D + EPSILON)
    gate_own = total[:, :ff_dev] * row_scale[:, None]
    up_own = total[:, ff_dev : 2 * ff_dev] * row_scale[:, None]
    hidden_own = (gate_own * jax.nn.sigmoid(gate_own) * up_own).astype(BF)

    sums_own = jnp.concatenate(
        [gate_own[:, :CAND_DEV].astype(BF), up_own[:, :CAND_DEV].astype(BF), two_parts(row_scale)], axis=1
    )
    sums_all = lax.all_gather(sums_own, "cand", axis=0)
    res_half = lax.dynamic_slice_in_dim(
        scaled_res.reshape(cands, 2, tok_half, width), core, 1, 1
    ).reshape(cands * tok_half, width)
    res_first = lax.all_gather(res_half, "cand", axis=0)
    res_second = lax.ppermute(res_first, "tp", CORE_PAIRS)

    live = widths // tps
    dropped = lax.iota(jnp.int32, ff_dev)[None, None, :] >= live[:, None, None]

    def dropped_output(half):
        rows = lax.dynamic_slice_in_dim(hidden_own, half * tok_half, tok_half, 0)
        rows = jnp.where(dropped, -rows[None], jnp.zeros((), BF)).reshape(cands * tok_half, ff_dev)
        return jnp.einsum("ru,fuk->frk", rows, down_all, preferred_element_type=F32).astype(BF)

    away = lax.ppermute(dropped_output(1 - core), "tp", CORE_PAIRS)
    pair_sum = (dropped_output(core).astype(F32) + away.astype(F32)).astype(BF)
    error_block = sum_scatter(pair_sum, "tp", SAME_CORE).astype(BF)
    grad_block = exchange(error_block.reshape(cands, tok_half, width), "cand")
    grad_first = gather_blocks(grad_block.reshape(cands * tok_half, width), "tp", chips, SAME_CORE)
    grad_second = lax.ppermute(grad_first, "tp", CORE_PAIRS)

    cand_live = jnp.sum(jnp.where(lax.iota(jnp.int32, widths.shape[0]) == cand_index, live, 0))
    keep_mask = (lax.iota(jnp.int32, CAND_DEV) < cand_live)[None, :]
    down_sel = down_all[:, :CAND_DEV]

    def terms(half, grad):
        sums = lax.dynamic_slice_in_dim(
            sums_all.reshape(cands, 2, tok_half, sums_all.shape[2]), half, 1, 1
        ).reshape(cands * tok_half, sums_all.shape[2]).astype(F32)
        gate_sel = sums[:, :CAND_DEV]
        up_sel = sums[:, CAND_DEV : 2 * CAND_DEV]
        scale = sums[:, 2 * CAND_DEV : 2 * CAND_DEV + 1] + sums[:, 2 * CAND_DEV + 1 : 2 * CAND_DEV + 2]
        sigmoid_sel = jax.nn.sigmoid(gate_sel)
        activated = gate_sel * sigmoid_sel
        slope = sigmoid_sel * (1.0 + gate_sel * (1.0 - sigmoid_sel))
        used = jnp.where(keep_mask, activated * up_sel, 0.0).astype(BF)
        back = jnp.einsum("fnk,fuk->nu", grad, down_sel, preferred_element_type=F32) * scale
        gate_term = jnp.where(keep_mask, back * up_sel * slope, 0.0).astype(BF)
        up_term = jnp.where(keep_mask, back * activated, 0.0).astype(BF)
        return used, gate_term, up_term

    first = terms(core, grad_first)
    second = terms(1 - core, grad_second)
    used, gate_term, up_term = (jnp.concatenate(pair, axis=0) for pair in zip(first, second))
    res_all = jnp.concatenate([res_first, res_second], axis=1)
    grad_all = jnp.concatenate([grad_first, grad_second], axis=1)

    def features_by_slots(term):
        grad = jnp.einsum("fnd,nu->fdu", res_all, term, preferred_element_type=F32)
        return grad.astype(BF).reshape(1, D, CAND_DEV)

    down_grad = jnp.einsum("nu,fnd->ufd", used, grad_all, preferred_element_type=F32)
    down_grad = down_grad.astype(BF).reshape(1, CAND_DEV, D)
    return features_by_slots(gate_term), features_by_slots(up_term), down_grad


def solution(mesh):
    in_specs = (
        P(None, "cand"),
        P("cand"),
        P("cand"),
        P("cand", "tp"),
        P("cand", None),
        P("cand", None),
        P("tp", "cand"),
        P("cand", "tp"),
        P("cand", "tp"),
        P("tp", "cand"),
        P(),
        P(),
    )
    out_specs = (P("cand", None, "tp"), P("cand", None, "tp"), P("cand", "tp", None))
    return jax.shard_map(shards, mesh=mesh, in_specs=in_specs, out_specs=out_specs, check_vma=False)
```

time: 797 us -> 337 us (0.42)
  waiting for transfers between devices: 541 us -> 136 us
  blocking collectives: 175 us -> 75.2 us
  starting transfers between devices: 0.47 us -> 27.1 us
  local copies, waits for them, and re-layouts: 2.12 us -> 20.5 us
    psum x2 -> x0, waiting for transfers between devices: 233 us -> none  [the longest x1 135 us: shards(): lax.psum(jnp.dot(attended, w_out, preferred_element_type=jnp.float32), 'tp')]
    psum x4 -> x0, blocking collectives: 175 us -> none  [the longest x1 68.7 us: shards(): target_block = lax.psum(out_part, 'tp').astype(jnp.bfloat16)]
    all_gather x4 -> x3, waiting for transfers between devices: 209 us -> 51.2 us  [the longest x1 28.6 us: shards(): sums_all = lax.all_gather(sums_own, 'cand', axis=0)]
    reduce_scatter x1 -> x0, waiting for transfers between devices: 98.3 us -> none  [shards(): lax.psum_scatter(pred_part, 'tp', scatter_dimension=0, tiled=True)]
    all_to_all x0 -> x4, waiting for transfers between devices: none -> 80.7 us  [exchange(): return lax.all_to_all(blocks, axis, 0, 0, axis_index_groups=groups)]
    all_to_all x0 -> x4, blocking collectives: none -> 75.2 us  [exchange(): return lax.all_to_all(blocks, axis, 0, 0, axis_index_groups=groups)]
    all_to_all x0 -> x4, starting transfers between devices: none -> 21.8 us  [exchange(): return lax.all_to_all(blocks, axis, 0, 0, axis_index_groups=groups)]
    unnamed x34 -> x37, local copies, waits for them, and re-layouts: 1.19 us -> 9.35 us
  transfers between devices with their start and end apart: 7 -> 10, of which waited for: 7 -> 7; matrix products, arithmetic and copies ran while one was open for 4% -> 18% of each run, Pallas kernels for 0% -> 0%
where the time goes in v1:
time: 337 us; the launch traced here: 335 us
  waiting for transfers between devices  136 us (40%)
  blocking collectives  75.2 us (22%)
  matrix products  55.9 us (17%)
  starting transfers between devices  27.1 us (8%)
  local copies, waits for them, and re-layouts  20.5 us (6%)
  between operations  14.3 us (4%)
  other arithmetic  5.94 us (2%)
    all_to_all x4, waiting for transfers between devices, exchange(): return lax.all_to_all(blocks, axis, 0, 0, axis_index_groups=groups)  80.7 us
    all_to_all x4, blocking collectives, exchange(): return lax.all_to_all(blocks, axis, 0, 0, axis_index_groups=groups)  75.2 us
    all_gather x1, waiting for transfers between devices, shards(): sums_all = lax.all_gather(sums_own, 'cand', axis=0)  28.6 us
    all_gather x1, waiting for transfers between devices, shards(): down_all = lax.all_gather(w_down, 'cand', axis=0)  22.6 us
    all_to_all x4, starting transfers between devices, exchange(): return lax.all_to_all(blocks, axis, 0, 0, axis_index_groups=groups)  21.8 us
    dot_general x2, matrix products, features_by_slots(): grad = jnp.einsum('fnd,nu->fdu', res_all, term, preferred_element_type=F32)  15.6 us
    dot_general x2, matrix products, dropped_output(): jnp.einsum('ru,fuk->frk', rows, down_all, preferred_element_type=F32)  14.1 us
    dot_general x2, matrix products, terms(): jnp.einsum('fnk,fuk->nu', grad, down_sel, preferred_element_type=F32)  9.84 us
  transfers between devices with their start and end apart: 10, of which 7 were waited for; matrix products, arithmetic and copies ran while one was open for 18% of the time, Pallas kernels for 0%

profile of v1, /device:TPU:1, one launch (start us, length us, event | category | flops | bytes accessed | tf_op | source)
XLA Modules:
  0.0 334.8 jit_solution(9791819041156157047)
XLA Ops:
  13.0 22.0 %all_to_all.40 = bf16[8,64,640]{2,1,0:T(8,128)(2,1)S(1)} all-to-all(bf16[8,64,640]{2,1,0:T(8,128)(2,1)S(1)} %concatenate.42), channel_id=1, replica_groups=mesh['cand'=8,'tp'=16] {'cand'}, dimensions={0} | all-to-all | bytes 1310720 | tf_op jit(solution)/shard_map/all_to_all | solution.py:28
  36.2 3.5 %all-to-all-start.1 = ((bf16[8,64,512]{2,1,0:T(8,128)(2,1)}), bf16[8,64,512]{2,1,0:T(8,128)(2,1)S(1)}, u32[]{:S(2)}, u32[]{:S(2)}) async-start(bf16[8,64,512]{2,1,0:T(8,128)(2,1)} %broadcast_in_dim.120), calls=%async_computation.1 | async-start | bytes 1048576 | tf_op jit(solution)/shard_map/all_to_all | solution.py:28
  40.0 11.6 %all-to-all-done.1 = bf16[8,64,512]{2,1,0:T(8,128)(2,1)S(1)} async-done(((bf16[8,64,512]{2,1,0:T(8,128)(2,1)}), bf16[8,64,512]{2,1,0:T(8,128)(2,1)S(1)}, u32[]{:S(2)}, u32[]{:S(2)}) %all-to-all-start.1) | async-done | bytes 524320 | tf_op jit(solution)/shard_map/all_to_all | solution.py:28
  54.9 10.4 %all-to-all-start.2 = ((bf16[16,32,512]{2,1,0:T(8,128)(2,1)}), bf16[16,32,512]{2,1,0:T(8,128)(2,1)S(1)}, u32[]{:S(2)}, u32[]{:S(2)}) async-start(bf16[16,32,512]{2,1,0:T(8,128)(2,1)} %bitcast.11), calls=%async_computation.2 | async-start | bytes 1048576 | tf_op jit(solution)/shard_map/all_to_all | solution.py:28
  65.3 9.8 %all-to-all-done.2 = bf16[16,32,512]{2,1,0:T(8,128)(2,1)S(1)} async-done(((bf16[16,32,512]{2,1,0:T(8,128)(2,1)}), bf16[16,32,512]{2,1,0:T(8,128)(2,1)S(1)}, u32[]{:S(2)}, u32[]{:S(2)}) %all-to-all-start.2) | async-done | bytes 524320 | tf_op jit(solution)/shard_map/all_to_all | solution.py:28
  75.3 14.6 %all_to_all.41 = bf16[16,32,512]{2,1,0:T(8,128)(2,1)S(1)} all-to-all(bf16[16,32,512]{2,1,0:T(8,128)(2,1)S(1)} %broadcast_in_dim.123), channel_id=1, replica_groups=mesh['cand'=8,'tp'=16] {'tp'}, dimensions={0} | all-to-all | bytes 1048576 | tf_op jit(solution)/shard_map/all_to_all | solution.py:28
  95.2 3.9 %all-to-all-start.4 = ((bf16[8,64,1920]{2,1,0:T(8,128)(2,1)}), bf16[8,64,1920]{2,1,0:T(8,128)(2,1)S(1)}, u32[]{:S(2)}, u32[]{:S(2)}) async-start(bf16[8,64,1920]{2,1,0:T(8,128)(2,1)} %concatenate.46), calls=%async_computation.4 | async-start | bytes 3932160 | tf_op jit(solution)/shard_map/all_to_all | solution.py:28
  99.9 29.4 %all-to-all-done.4 = bf16[8,64,1920]{2,1,0:T(8,128)(2,1)S(1)} async-done(((bf16[8,64,1920]{2,1,0:T(8,128)(2,1)}), bf16[8,64,1920]{2,1,0:T(8,128)(2,1)S(1)}, u32[]{:S(2)}, u32[]{:S(2)}) %all-to-all-start.4) | async-done | bytes 1966112 | tf_op jit(solution)/shard_map/all_to_all | solution.py:28
  130.2 22.6 %all-gather.8.cloned.1.call-done = bf16[7168,512]{1,0:T(8,128)(2,1)} async-done(((bf16[896,512]{1,0:T(8,128)(2,1)}), bf16[7168,512]{1,0:T(8,128)(2,1)}) %all-gather.8.cloned.1.call-update) | async-done | bytes 7340048 | tf_op jit(solution)/shard_map/all_gather | solution.py:66
  152.8 6.7 %convert_bitcast_fusion = bf16[8,256,512]{2,1,0:T(8,128)(2,1)} fusion(bf16[256,896,1]{1,0,2:T(8,128)(2,1)S(1)} %bitcast.117, bf16[8,896,512]{2,1,0:T(8,128)(2,1)} %bitcast.125), kind=kOutput, calls=%fused_computation.17 | convolution fusion | flops 1880096768 | bytes 9895936 | tf_op jit(solution)/shard_map/ru,fuk->frk/dot_general | solution.py:138
  164.7 7.4 %fusion.9 = bf16[8,256,512]{2,1,0:T(8,128)(2,1)} fusion(bf16[8,256,512]{2,1,0:T(8,128)(2,1)} %collective-permute-done.1, bf16[256,896,1]{1,0,2:T(8,128)(2,1)S(1)} %bitcast.116, bf16[8,896,512]{2,1,0:T(8,128)(2,1)} %bitcast.126), kind=kOutput, calls=%fused_computation.11 | convolution fusion | flops 1884291072 | bytes 11993088 | tf_op jit(solution)/shard_map/ru,fuk->frk/dot_general | solution.py:138
  172.1 4.0 %all-to-all-start.5 = ((bf16[8,256,512]{2,1,0:T(8,128)(2,1)}), bf16[8,256,512]{2,1,0:T(8,128)(2,1)S(1)}, u32[]{:S(2)}, u32[]{:S(2)}) async-start(bf16[8,256,512]{2,1,0:T(8,128)(2,1)} %fusion.9), calls=%async_computation.5 | async-start | bytes 4194304 | tf_op jit(solution)/shard_map/all_to_all | solution.py:28
  177.3 29.9 %all-to-all-done.5 = bf16[8,256,512]{2,1,0:T(8,128)(2,1)S(1)} async-done(((bf16[8,256,512]{2,1,0:T(8,128)(2,1)}), bf16[8,256,512]{2,1,0:T(8,128)(2,1)S(1)}, u32[]{:S(2)}, u32[]{:S(2)}) %all-to-all-start.5) | async-done | bytes 2097184 | tf_op jit(solution)/shard_map/all_to_all | solution.py:28
  207.6 12.5 %all_to_all.42 = bf16[8,32,512]{2,1,0:T(8,128)(2,1)S(1)} all-to-all(bf16[8,32,512]{2,1,0:T(8,128)(2,1)S(1)} %bitcast.111), channel_id=1, replica_groups=mesh['cand'=8,'tp'=16] {'cand'}, dimensions={0} | all-to-all | bytes 524288 | tf_op jit(solution)/shard_map/all_to_all | solution.py:28
  220.3 26.2 %all_to_all.43 = bf16[8,256,512]{2,1,0:T(8,128)(2,1)S(1)} all-to-all(bf16[8,256,512]{2,1,0:T(8,128)(2,1)S(1)} %broadcast_in_dim.130), channel_id=1, replica_groups={{0,2,4,6,8,10,12,14},{1,3,5,7,9,11,13,15},{16,18,20,22,24,26,28,30},{17..., dimensions={0} | all-to-all | bytes 4194304 | tf_op jit(solution)/shard_map/all_to_all | solution.py:28
  246.5 4.1 %collective-permute-start.2 = (bf16[8,256,512]{2,1,0:T(8,128)(2,1)S(1)}, bf16[8,256,512]{2,1,0:T(8,128)(2,1)}, u32[]{:S(2)}, u32[]{:S(2)}) collective-permute-start(bf16[8,256,512]{2,1,0:T(8,128)(2,1)S(1)} %all_to_all.43), channel_id=1, source_target_pairs={{0,1},{1,0},{2,3},{3,2},{4,5},{5,4},{6,7},{7,6},{8,9},{9,8},{10,11... | collective-permute-start | bytes 6291464 | tf_op jit(solution)/shard_map/ppermute | solution.py:145
  251.2 3.9 %copy.83 = bf16[8,256,512]{1,2,0:T(8,128)(2,1)} copy(bf16[8,256,512]{2,1,0:T(8,128)(2,1)} %all-gather.6.cloned.1.call-done) | data formatting | bytes 4194304 | tf_op jit(solution)/shard_map/all_gather | solution.py:129
  255.2 28.6 %all-gather.10.cloned.1.call-done = bf16[512,1664]{1,0:T(8,128)(2,1)} async-done(((bf16[64,1664]{1,0:T(8,128)(2,1)}), bf16[512,1664]{1,0:T(8,128)(2,1)}) %all-gather.10.cloned.1.call-update) | async-done | bytes 1703952 | tf_op jit(solution)/shard_map/all_gather | solution.py:125
  286.0 5.0 %fusion.23 = f32[256,768]{1,0:T(8,128)S(1)} fusion(bf16[8,256,512]{2,1,0:T(8,128)(2,1)S(1)} %all_to_all.43, bf16[8,896,512]{2,1,0:T(8,128)(2,1)} %bitcast.127, f32[256]{0:T(256)S(1)} %fusion.48), kind=kOutput, calls=%fused_computation.30 | convolution fusion | flops 1610809344 | bytes 9176064 | tf_op jit(solution)/shard_map/fnk,fuk->nu/dot_general | solution.py:162
  291.1 4.9 %select_convert_fusion.3 = (bf16[256,768]{1,0:T(8,128)(2,1)}, bf16[256,768]{1,0:T(8,128)(2,1)S(1)}, bf16[256,768]{1,0:T(8,128)(2,1)S(1)}, bf16[256,768]{1,0:T(8,...) fusion(f32[256,768]{1,0:T(8,128)S(1)} %fusion.23, pred[768]{0:T(1024)(128)(4,1)S(1)} %iota_compare_fusion.2, ...), kind=kOutput, calls=%fused_computation.60 | convolution fusion | flops 1617887232 | bytes 14682112 | tf_op jit(solution)/shard_map/fnk,fuk->nu/dot_general | solution.py:162
  295.9 7.8 %fusion.10 = bf16[768,8,512]{0,2,1:T(8,128)(2,1)} fusion(bf16[8,256,512]{2,1,0:T(8,128)(2,1)} %collective-permute-done.2, bf16[8,256,512]{2,1,0:T(8,128)(2,1)S(1)} %all_to_all.43, bf16[256,768]{1,0:T(8,128)(2,1)S(1)} %get-tuple-element.48, bf16[256,768]{1,0:T(8,128)(2,1)S(1)} %get-tuple-element.32), kind=kOutput, calls=%fused_computation.13 | convolution fusion | flops 3234332672 | bytes 11272192 | tf_op jit(solution)/shard_map/nu,fnd->ufd/dot_general | solution.py:177
  303.7 9.0 %copy.91 = bf16[1,768,4096]{2,1,0:T(8,128)(2,1)} copy(bf16[1,768,4096]{1,2,0:T(8,128)(2,1)} %bitcast.106) | data formatting | bytes 12582912
  312.7 7.8 %convolution_convert_fusion = bf16[8,512,768]{2,1,0:T(8,128)(2,1)} fusion(bf16[8,256,512]{1,2,0:T(8,128)(2,1)} %collective-permute-done, bf16[8,256,512]{1,2,0:T(8,128)(2,1)S(1)} %copy-done.2, bf16[256,768]{1,0:T(8,128)(2,1)S(1)} %copy-done.13, bf16[256,768]{1,0:T(8,128)(2,1)S(1)} %copy-done.12), kind=kOutput, calls=%fused_computation.14 | convolution fusion | flops 3234332672 | bytes 11272192 | tf_op jit(solution)/shard_map/fnd,nu->fdu/dot_general | solution.py:174
  320.5 7.8 %convolution_convert_fusion.1 = bf16[8,512,768]{2,1,0:T(8,128)(2,1)} fusion(bf16[8,256,512]{1,2,0:T(8,128)(2,1)} %collective-permute-done, bf16[8,256,512]{1,2,0:T(8,128)(2,1)S(1)} %copy-done.2, bf16[256,768]{1,0:T(8,128)(2,1)S(1)} %copy-done.11, bf16[256,768]{1,0:T(8,128)(2,1)S(1)} %get-tuple-element.29), kind=kOutput, calls=%fused_computation.15 | convolution fusion | flops 3234332672 | bytes 11272192 | tf_op jit(solution)/shard_map/fnd,nu->fdu/dot_general | solution.py:174
  (106 shorter events, 27.3 us)
Async XLA Ops:
  7.2 3.8 %copy-start.3 = (bf16[512,512]{1,0:T(8,128)(2,1)S(1)}, bf16[512,512]{1,0:T(8,128)(2,1)}, u32[]{:S(2)}) copy-start(bf16[512,512]{1,0:T(8,128)(2,1)} %param.12) | copy-start | bytes 1572868
  7.2 3.8 %copy-start.10 = (f32[512]{0:T(512)S(1)}, f32[512]{0:T(512)}, u32[]{:S(2)}) copy-start(f32[512]{0:T(512)} %param.13) | copy-start | bytes 6148
  7.2 5.0 %copy-start.9 = (bf16[512,256]{1,0:T(8,128)(2,1)S(1)}, bf16[512,256]{1,0:T(8,128)(2,1)}, u32[]{:S(2)}) copy-start(bf16[512,256]{1,0:T(8,128)(2,1)} %param.15) | copy-start | bytes 786436
  7.2 145.6 %all-gather.8.cloned.1.call-start = ((), (), s32[]{:S(2)}) async-start(), calls=%async_computation.9 | async-start | bytes 8257536 | tf_op jit(solution)/shard_map/all_gather | solution.py:66
  13.0 26.7 %copy-start.5 = (s32[512]{0:T(512)S(1)}, s32[512]{0:T(512)}, u32[]{:S(2)}) copy-start(s32[512]{0:T(512)} %param.22) | copy-start | bytes 6148
  36.2 15.4 %all-to-all-start.1 = ((bf16[8,64,512]{2,1,0:T(8,128)(2,1)}), bf16[8,64,512]{2,1,0:T(8,128)(2,1)S(1)}, u32[]{:S(2)}, u32[]{:S(2)}) async-start(bf16[8,64,512]{2,1,0:T(8,128)(2,1)} %broadcast_in_dim.120), calls=%async_computation.1 | async-start | bytes 1048576 | tf_op jit(solution)/shard_map/all_to_all | solution.py:28
  54.9 35.5 %copy-start.6 = (f32[512]{0:T(512)S(1)}, f32[512]{0:T(512)}, u32[]{:S(2)}) copy-start(f32[512]{0:T(512)} %param.14) | copy-start | bytes 6148
  54.9 20.2 %all-to-all-start.2 = ((bf16[16,32,512]{2,1,0:T(8,128)(2,1)}), bf16[16,32,512]{2,1,0:T(8,128)(2,1)S(1)}, u32[]{:S(2)}, u32[]{:S(2)}) async-start(bf16[16,32,512]{2,1,0:T(8,128)(2,1)} %bitcast.11), calls=%async_computation.2 | async-start | bytes 1048576 | tf_op jit(solution)/shard_map/all_to_all | solution.py:28
  65.3 25.2 %copy-start.8 = (bf16[512,896]{1,0:T(8,128)(2,1)S(1)}, bf16[512,896]{1,0:T(8,128)(2,1)}, u32[]{:S(2)}) copy-start(bf16[512,896]{1,0:T(8,128)(2,1)} %param.20) | copy-start | bytes 2752516
  95.2 4.0 %copy-start.7 = (s32[8]{0:T(128)S(1)}, s32[8]{0:T(128)}, u32[]{:S(2)}) copy-start(s32[8]{0:T(128)} %param.23) | copy-start | bytes 100
  95.2 34.1 %all-to-all-start.4 = ((bf16[8,64,1920]{2,1,0:T(8,128)(2,1)}), bf16[8,64,1920]{2,1,0:T(8,128)(2,1)S(1)}, u32[]{:S(2)}, u32[]{:S(2)}) async-start(bf16[8,64,1920]{2,1,0:T(8,128)(2,1)} %concatenate.46), calls=%async_computation.4 | async-start | bytes 3932160 | tf_op jit(solution)/shard_map/all_to_all | solution.py:28
  99.1 152.1 %all-gather.6.cloned.1.call-start = ((), (), s32[]{:S(2)}) async-start(), calls=%async_computation.8 | async-start | bytes 2359296 | tf_op jit(solution)/shard_map/all_gather | solution.py:129
  159.5 5.2 %collective-permute-start.1 = (bf16[8,256,512]{2,1,0:T(8,128)(2,1)}, bf16[8,256,512]{2,1,0:T(8,128)(2,1)}, u32[]{:S(2)}, u32[]{:S(2)}) collective-permute-start(bf16[8,256,512]{2,1,0:T(8,128)(2,1)} %convert_bitcast_fusion), channel_id=1, source_target_pairs={{0,1},{1,0},{2,3},{3,2},{4,5},{5,4},{6,7},{7,6},{8,9},{9,8},{10,11... | collective-permute-start | bytes 6291464 | tf_op jit(solution)/shard_map/ppermute | solution.py:140
  172.1 35.1 %all-to-all-start.5 = ((bf16[8,256,512]{2,1,0:T(8,128)(2,1)}), bf16[8,256,512]{2,1,0:T(8,128)(2,1)S(1)}, u32[]{:S(2)}, u32[]{:S(2)}) async-start(bf16[8,256,512]{2,1,0:T(8,128)(2,1)} %fusion.9), calls=%async_computation.5 | async-start | bytes 4194304 | tf_op jit(solution)/shard_map/all_to_all | solution.py:28
  176.1 107.6 %all-gather.10.cloned.1.call-start = ((), (), s32[]{:S(2)}) async-start(), calls=%async_computation.10 | async-start | bytes 1916928 | tf_op jit(solution)/shard_map/all_gather | solution.py:125
  246.5 44.6 %collective-permute-start.2 = (bf16[8,256,512]{2,1,0:T(8,128)(2,1)S(1)}, bf16[8,256,512]{2,1,0:T(8,128)(2,1)}, u32[]{:S(2)}, u32[]{:S(2)}) collective-permute-start(bf16[8,256,512]{2,1,0:T(8,128)(2,1)S(1)} %all_to_all.43), channel_id=1, source_target_pairs={{0,1},{1,0},{2,3},{3,2},{4,5},{5,4},{6,7},{7,6},{8,9},{9,8},{10,11... | collective-permute-start | bytes 6291464 | tf_op jit(solution)/shard_map/ppermute | solution.py:145
  255.2 57.5 %collective-permute-start = (bf16[8,256,512]{1,2,0:T(8,128)(2,1)}, bf16[8,256,512]{1,2,0:T(8,128)(2,1)}, u32[]{:S(2)}, u32[]{:S(2)}) collective-permute-start(bf16[8,256,512]{1,2,0:T(8,128)(2,1)} %copy.83), channel_id=1, source_target_pairs={{0,1},{1,0},{2,3},{3,2},{4,5},{5,4},{6,7},{7,6},{8,9},{9,8},{10,11... | collective-permute-start | bytes 6291464 | tf_op jit(solution)/shard_map/ppermute | solution.py:130
  285.3 5.7 %slice-start = ((s8[7340032]{0:T(1024)(128)(4,1)}), s8[4194304]{0:T(1024)(128)(4,1)S(1)}, s32[]{:S(2)}) async-start(s8[7340032]{0:T(1024)(128)(4,1)} %bitcast.128), calls=%async_computation.11 | async-start | bytes 8388608
  286.0 5.0 %slice-start.1 = ((s8[7340032]{0:T(1024)(128)(4,1)}), s8[3145728]{0:T(1024)(128)(4,1)S(1)}, s32[]{:S(2)}) async-start(s8[7340032]{0:T(1024)(128)(4,1)} %bitcast.128), calls=%async_computation.12 | async-start | bytes 6291456
  303.7 9.0 %copy-start.2 = (bf16[8,256,512]{1,2,0:T(8,128)(2,1)S(1)}, bf16[8,256,512]{1,2,0:T(8,128)(2,1)}, u32[]{:S(2)}) copy-start(bf16[8,256,512]{1,2,0:T(8,128)(2,1)} %copy.83) | copy-start | bytes 6291460
  303.7 9.0 %copy-start.12 = (bf16[256,768]{1,0:T(8,128)(2,1)S(1)}, bf16[256,768]{1,0:T(8,128)(2,1)}, u32[]{:S(2)}) copy-start(bf16[256,768]{1,0:T(8,128)(2,1)} %get-tuple-element.28) | copy-start | bytes 1179652
  303.7 9.0 %copy-start.13 = (bf16[256,768]{1,0:T(8,128)(2,1)S(1)}, bf16[256,768]{1,0:T(8,128)(2,1)}, u32[]{:S(2)}) copy-start(bf16[256,768]{1,0:T(8,128)(2,1)} %get-tuple-element.50) | copy-start | bytes 1179652
  312.7 7.8 %copy-start.11 = (bf16[256,768]{1,0:T(8,128)(2,1)S(1)}, bf16[256,768]{1,0:T(8,128)(2,1)}, u32[]{:S(2)}) copy-start(bf16[256,768]{1,0:T(8,128)(2,1)} %get-tuple-element.49) | copy-start | bytes 1179652
  320.5 7.8 %copy-start.1 = (bf16[512,1024]{1,0:T(8,128)(2,1)S(1)}, bf16[512,1024]{1,0:T(8,128)(2,1)}, u32[]{:S(2)}) copy-start(bf16[512,1024]{1,0:T(8,128)(2,1)} %param.16) | copy-start | bytes 3145732
  (2 other events, 3.6 us)
Sparse Core Ops, SparseCore 0:
  10.4 142.3 all-gather.7
  161.6 59.7 all-gather.5
  223.8 59.9 all-gather.9

commit v2 on v0

v2 whole, which is shorter than its diff:
```python
import functools

import jax
import jax.numpy as jnp
from jax import lax
from jax.experimental import pallas as pl
from jax.experimental.pallas import tpu as pltpu
from jax.sharding import PartitionSpec as P

D = 4096
HEADS = 32
KV_HEADS = 8
HEAD_DIM = 128
CAND_DEV = 768
LANES = 128
EPSILON = 1e-05
BF = jnp.bfloat16
F32 = jnp.float32

CORE_PAIRS = [(i, i ^ 1) for i in range(16)]
ACROSS_Z = [(i, i ^ 4) for i in range(8)]
SAME_Z = [[0, 1, 2, 3], [4, 5, 6, 7]]
SAME_CORE_ALL = [[c * 16 + t for c in range(8) for t in range(core, 16, 2)] for core in range(2)]
SAME_CORE = [list(range(core, 16, 2)) for core in range(2)]


def exchange(blocks, axis, groups=None):
    return lax.all_to_all(blocks, axis, 0, 0, axis_index_groups=groups)


def lanes_of(column):
    high = column.astype(BF).astype(F32)
    lane = lax.broadcasted_iota(jnp.int32, (column.shape[0], LANES), 1)
    return jnp.where(lane == 0, high, jnp.where(lane == 1, column - high, 0.0)).astype(BF)


def column_of(lanes):
    return lanes[:, 0:1].astype(F32) + lanes[:, 1:2].astype(F32)


def params(limit_mib):
    return pltpu.CompilerParams(
        dimension_semantics=("arbitrary",), vmem_limit_bytes=limit_mib << 20
    )


def cost(flops, bytes_accessed, transcendentals=0):
    return pl.CostEstimate(
        flops=flops, bytes_accessed=bytes_accessed, transcendentals=transcendentals
    )


def project_kernel(scalars, rows, gain, *refs):
    *weights, out, scaled_out = refs
    wide = rows[...].astype(F32)
    scaled = (wide * gain[...]).astype(BF)
    scaled_out[...] = scaled
    at = 0
    for weight in weights:
        width = weight.shape[1]
        out[:, at : at + width] = jnp.dot(
            scaled, weight[...], preferred_element_type=F32
        ).astype(BF)
        at += width
    out[:, at:] = lanes_of(jnp.sum(wide * wide, axis=1, keepdims=True))


def project(rows, gain, weights, widths, columns, limit_mib, name):
    count, depth = rows.shape
    out_width = sum(widths) + LANES
    tile = count // 2

    def weight_spec(i, width):
        return pl.BlockSpec((depth, width), lambda r, scalars: (0, scalars[i]))

    return pl.pallas_call(
        project_kernel,
        out_shape=[
            jax.ShapeDtypeStruct((count, out_width), BF),
            jax.ShapeDtypeStruct((count, depth), BF),
        ],
        grid_spec=pltpu.PrefetchScalarGridSpec(
            num_scalar_prefetch=1,
            grid=(2,),
            in_specs=[
                pl.BlockSpec((tile, depth), lambda r, scalars: (r, 0)),
                pl.BlockSpec((1, depth), lambda r, scalars: (0, 0)),
            ]
            + [weight_spec(i, width) for i, width in enumerate(widths)],
            out_specs=[
                pl.BlockSpec((tile, out_width), lambda r, scalars: (r, 0)),
                pl.BlockSpec((tile, depth), lambda r, scalars: (r, 0)),
            ],
        ),
        compiler_params=params(limit_mib),
        cost_estimate=cost(2 * count * depth * out_width, 2 * out_width * (count + depth)),
        name=name,
    )(jnp.stack(columns).astype(jnp.int32), rows, gain.reshape(1, depth), *weights)


def copies_kernel(body, scalars, *refs):
    *ins, out = refs
    value = body(*ins)
    for i in range(out.shape[0]):
        out[i] = value


def summed_copies(body, ins, in_specs, scalars, copies, rows, width, name):
    return pl.pallas_call(
        functools.partial(copies_kernel, body),
        out_shape=jax.ShapeDtypeStruct((copies, rows, width), BF),
        grid_spec=pltpu.PrefetchScalarGridSpec(
            num_scalar_prefetch=1,
            grid=(1,),
            in_specs=in_specs,
            out_specs=pl.BlockSpec((copies, rows, width), lambda i, scalars: (0, 0, 0)),
        ),
        compiler_params=params(12),
        cost_estimate=cost(0, 4 * copies * rows * width),
        name=name,
    )(scalars, *ins)


def whole(array):
    return pl.BlockSpec(array.shape, lambda i, scalars: (0,) * array.ndim)


def qkv_body(received):
    total = jnp.sum(received[...].astype(F32), axis=0)
    width = total.shape[1] - LANES
    squares = total[:, width : width + 1] + total[:, width + 1 : width + 2]
    return (total[:, :width] * lax.rsqrt(squares / D + EPSILON)).astype(BF)


def residual_body(received, rows):
    return (rows[...].astype(F32) + jnp.sum(received[...].astype(F32), axis=0)).astype(BF)


def sums_kernel(scalars, received, scaled_res, payload, minus_hidden):
    ff_dev = minus_hidden.shape[1]
    rows = received.shape[1]
    total = jnp.sum(received[...].astype(F32), axis=0)
    squares = total[:, 2 * ff_dev : 2 * ff_dev + 1] + total[:, 2 * ff_dev + 1 : 2 * ff_dev + 2]
    scale = lax.rsqrt(squares / D + EPSILON)
    gate = total[:, :ff_dev] * scale
    up = total[:, ff_dev : 2 * ff_dev] * scale
    minus_hidden[...] = (-(gate * jax.nn.sigmoid(gate) * up)).astype(BF)
    parts = (gate[:, :CAND_DEV].astype(BF), up[:, :CAND_DEV].astype(BF), lanes_of(scale), scaled_res)
    at = 0
    for part in parts:
        count = part.shape[0]
        for lane in range(0, part.shape[1], LANES):
            payload[at : at + count, :] = part[:, lane : lane + LANES]
            at += count


def gate_up_sums(scalars, received, scaled_res):
    _, rows, width = received.shape
    ff_dev = (width - LANES) // 2
    half, depth = scaled_res.shape[0] // 2, scaled_res.shape[1]
    payload_rows = rows * SUMS_TILES + half * (depth // LANES)
    return pl.pallas_call(
        sums_kernel,
        out_shape=[
            jax.ShapeDtypeStruct((payload_rows, LANES), BF),
            jax.ShapeDtypeStruct((rows, ff_dev), BF),
        ],
        grid_spec=pltpu.PrefetchScalarGridSpec(
            num_scalar_prefetch=1,
            grid=(1,),
            in_specs=[
                whole(received),
                pl.BlockSpec((half, depth), lambda i, scalars: (scalars[0], 0)),
            ],
            out_specs=[
                pl.BlockSpec((payload_rows, LANES), lambda i, scalars: (0, 0)),
                pl.BlockSpec((rows, ff_dev), lambda i, scalars: (0, 0)),
            ],
        ),
        compiler_params=params(20),
        cost_estimate=cost(0, 4 * received.size, rows * ff_dev),
        name="gate_up_sums",
    )(scalars, received, scaled_res)


LIVE_AT, LIVES_AT, Z_AT = 1, 2, 10
SUMS_TILES = 2 * CAND_DEV // LANES + 1


def dropped_kernel(scalars, own, other, down, down_rest, out, rows):
    cands, _, chunks, chunk, width = out.shape

    @pl.when(pl.program_id(0) == 0)
    def _():
        own_first = scalars[Z_AT] == 0
        unit = lax.broadcasted_iota(jnp.int32, (chunk, own.shape[1]), 1)
        for at in range(4):
            part = slice(at % 2 * chunk, (at % 2 + 1) * chunk)
            here, there = own[part, :].astype(F32), other[part, :].astype(F32)
            values = jnp.where(own_first == (at < 2), here, there)
            for c in range(8):
                kept = jnp.where(unit >= scalars[LIVES_AT + c], values, 0.0).astype(BF)
                rows[(c * 4 + at) * chunk : (c * 4 + at + 1) * chunk, :] = kept

    total = jnp.dot(rows[:, :CAND_DEV], down[0], preferred_element_type=F32)
    total += jnp.dot(rows[:, CAND_DEV:], down_rest[0], preferred_element_type=F32)
    out[:, 0] = total.astype(BF).reshape(cands, chunks, chunk, width)


def dropped_output(scalars, own, other, down_four, flip):
    tok_cand, ff_dev = own.shape
    width = down_four.shape[2]
    chunk = tok_cand // 2
    rest = ff_dev - CAND_DEV

    def block(i, scalars):
        return 2 * (1 - scalars[0] if flip else scalars[0]) + i

    return pl.pallas_call(
        dropped_kernel,
        out_shape=jax.ShapeDtypeStruct((8, 2, 4, chunk, width), BF),
        grid_spec=pltpu.PrefetchScalarGridSpec(
            num_scalar_prefetch=1,
            grid=(2,),
            in_specs=[
                whole(own),
                whole(other),
                pl.BlockSpec((1, CAND_DEV, width), lambda i, scalars: (block(i, scalars), 0, 0)),
                pl.BlockSpec(
                    (1, rest, width),
                    lambda i, scalars: (block(i, scalars), 2 * CAND_DEV // rest, 0),
                ),
            ],
            out_specs=pl.BlockSpec(
                (8, 1, 4, chunk, width), lambda i, scalars: (0, i, 0, 0, 0)
            ),
            scratch_shapes=[pltpu.VMEM((32 * chunk, ff_dev), BF)],
        ),
        compiler_params=params(60),
        cost_estimate=cost(4 * 32 * chunk * ff_dev * width, 4 * (ff_dev + 32 * chunk) * width),
        name="dropped_output",
    )(scalars, own, other, down_four, down_four)


def tiles_of(block, first, count, rows):
    tiles = [block[..., first + i * rows : first + (i + 1) * rows, :] for i in range(count)]
    return jnp.concatenate([tile.reshape(-1, LANES) for tile in tiles], axis=1)


def factors_kernel(rows, scalars, payload, gate_factor, up_factor, used_t):
    payload = payload[...]
    tiles = CAND_DEV // LANES
    gate = tiles_of(payload, 0, tiles, rows).astype(F32)
    up = tiles_of(payload, tiles * rows, tiles, rows).astype(F32)
    keep = lax.broadcasted_iota(jnp.int32, gate.shape, 1) < scalars[LIVE_AT]
    scale = jnp.where(keep, column_of(tiles_of(payload, 2 * tiles * rows, 1, rows)), 0.0)
    sigmoid = jax.nn.sigmoid(gate)
    activated = gate * sigmoid
    slope = sigmoid * (1.0 + gate * (1.0 - sigmoid))
    gate_factor[...] = up * slope * scale
    up_factor[...] = activated * scale
    used_t[...] = jnp.where(keep, activated * up, 0.0).T.astype(BF)


def factors(scalars, gathered, rows):
    cands, payload_rows, _ = gathered.shape
    tok_count = cands * rows
    half = tok_count // 2
    factor = jax.ShapeDtypeStruct((tok_count, CAND_DEV), F32)
    return pl.pallas_call(
        functools.partial(factors_kernel, rows),
        out_shape=[factor, factor, jax.ShapeDtypeStruct((CAND_DEV, tok_count), BF)],
        grid_spec=pltpu.PrefetchScalarGridSpec(
            num_scalar_prefetch=1,
            grid=(2,),
            in_specs=[
                pl.BlockSpec(
                    (cands // 2, payload_rows, LANES),
                    lambda i, scalars: ((scalars[0] + i) % 2, 0, 0),
                ),
            ],
            out_specs=[
                pl.BlockSpec((half, CAND_DEV), lambda i, scalars: (i, 0)),
                pl.BlockSpec((half, CAND_DEV), lambda i, scalars: (i, 0)),
                pl.BlockSpec((CAND_DEV, half), lambda i, scalars: (0, i)),
            ],
        ),
        compiler_params=params(28),
        cost_estimate=cost(0, 2 * gathered.size + 10 * tok_count * CAND_DEV, tok_count * CAND_DEV),
        name="factors",
    )(scalars, gathered)


def sum_error_kernel(received, out):
    value = jnp.sum(received[...].astype(F32), axis=1).astype(BF)
    for i in range(out.shape[0]):
        out[i] = value


def sum_error(received):
    groups, chips, rows, width = received.shape
    return pl.pallas_call(
        sum_error_kernel,
        out_shape=jax.ShapeDtypeStruct((chips, groups, rows, width), BF),
        grid=(4,),
        in_specs=[pl.BlockSpec((groups // 4, chips, rows, width), lambda i: (i, 0, 0, 0))],
        out_specs=pl.BlockSpec((chips, groups // 4, rows, width), lambda i: (0, i, 0, 0)),
        compiler_params=params(12),
        cost_estimate=cost(0, 4 * received.size),
        name="sum_error",
    )(received)


def contract(left, right, left_dim, right_dim):
    return lax.dot_general(
        left, right, (((left_dim,), (right_dim,)), ((), ())), preferred_element_type=F32
    )


def grad_rows_of(halves, z):
    rows = []
    for half in halves:
        block = half[0, :, z]
        rows += [block[chunk, y] for y in range(block.shape[1]) for chunk in range(block.shape[0])]
    return jnp.concatenate(rows, axis=0)


def back_product(scalars, halves, down):
    total = None
    for z in range(2):
        at = pl.multiple_of(jnp.where(scalars[Z_AT] == z, 0, CAND_DEV), CAND_DEV)
        product = contract(grad_rows_of(halves, z), down[0, pl.ds(at, CAND_DEV), :], 1, 1)
        total = product if total is None else total + product
    return total


def back_kernel(scalars, own_1, own_2, down, out):
    product = back_product(scalars, (own_1, own_2), down)

    @pl.when(pl.program_id(0) == 0)
    def _():
        out[...] = product

    @pl.when(pl.program_id(0) > 0)
    def _():
        out[...] += product


def half_specs(grad, block):
    chunks, z, y, rows, width = grad.shape[1:]

    def spec(flip):
        return pl.BlockSpec(
            (1, chunks // 2, z, y, rows, width),
            lambda i, scalars: (block(i), 1 - scalars[0] if flip else scalars[0], 0, 0, 0, 0),
        )

    return [spec(False), spec(True)]


def own_back(scalars, grad_own, down_four):
    _, chunks, z, y, rows, width = grad_own.shape
    tok_count = chunks * y * rows
    return pl.pallas_call(
        back_kernel,
        out_shape=jax.ShapeDtypeStruct((tok_count, CAND_DEV), F32),
        grid_spec=pltpu.PrefetchScalarGridSpec(
            num_scalar_prefetch=1,
            grid=(2,),
            in_specs=half_specs(grad_own, lambda i: i)
            + [
                pl.BlockSpec(
                    (1, 2 * CAND_DEV, width), lambda i, scalars: (2 * scalars[0] + i, 0, 0)
                )
            ],
            out_specs=pl.BlockSpec((tok_count, CAND_DEV), lambda i, scalars: (0, 0)),
        ),
        compiler_params=params(60),
        cost_estimate=cost(8 * tok_count * width * CAND_DEV, 10 << 20),
        name="own_back",
    )(scalars, grad_own, grad_own, down_four)


def gradient_kernel(
    scalars, own_1, own_2, other_1, other_2, down, res_1, res_2, start, gate_factor, up_factor, used_t, *refs
):
    gate_out, up_out, down_out, back, terms = refs
    step = pl.program_id(0)
    half, width = back.shape[0] // 2, own_1.shape[5]

    @pl.when(step == 0)
    def _():
        back[...] = start[...] + back_product(scalars, (other_1, other_2), down)

    @pl.when(step == 1)
    def _():
        total = back[...] + back_product(scalars, (other_1, other_2), down)
        terms[:, :CAND_DEV] = (total * gate_factor[...]).astype(BF)
        terms[:, CAND_DEV:] = (total * up_factor[...]).astype(BF)

    for at, halves in enumerate(((own_1, own_2), (other_1, other_2))):
        for z in range(2):

            @pl.when((step >= 2) & ((step - 2) // 4 == at) & ((step - 2) % 2 == z))
            def _(halves=halves, z=z):
                grad = grad_rows_of(halves, z)
                down_out[0] = jnp.dot(used_t[...], grad, preferred_element_type=F32).astype(BF)

    @pl.when(step >= 2)
    def _():
        tiles = width // LANES
        first = res_1.shape[1] - half * tiles
        res = [tiles_of(ref[0], first, tiles, half) for ref in (res_1, res_2)]
        res = jnp.concatenate(res, axis=0)
        both = contract(res, terms[...], 0, 0).astype(BF)
        gate_out[0] = both[:, :CAND_DEV]
        up_out[0] = both[:, CAND_DEV:]


def gradients(scalars, grad_own, grad_other, down_four, res_1, res_2, start, gate_factor, up_factor, used_t):
    _, chunks, z, y, rows, width = grad_own.shape
    tok_count = chunks * y * rows
    groups = 8

    def own_block(i):
        return jnp.clip((i - 2) // 2, 0, 1)

    def other_block(i):
        return jnp.where(i < 2, i, jnp.clip((i - 6) // 2, 0, 1))

    def late(i, scalars):
        at = jnp.maximum(i - 2, 0)
        core = jnp.where(at < 4, scalars[0], 1 - scalars[0])
        return at % 2 * 4 + 2 * core + at // 2 % 2

    res_spec = pl.BlockSpec((1,) + res_1.shape[1:], lambda i, scalars: (late(i, scalars), 0, 0))
    product = 2 * tok_count * groups * width * CAND_DEV
    return pl.pallas_call(
        gradient_kernel,
        out_shape=[
            jax.ShapeDtypeStruct((1, groups * width, CAND_DEV), BF),
            jax.ShapeDtypeStruct((1, groups * width, CAND_DEV), BF),
            jax.ShapeDtypeStruct((1, CAND_DEV, groups * width), BF),
        ],
        grid_spec=pltpu.PrefetchScalarGridSpec(
            num_scalar_prefetch=1,
            grid=(10,),
            in_specs=half_specs(grad_own, own_block)
            + half_specs(grad_other, other_block)
            + [
                pl.BlockSpec(
                    (1, 2 * CAND_DEV, width),
                    lambda i, scalars: (2 * (1 - scalars[0]) + jnp.minimum(i, 1), 0, 0),
                ),
                res_spec,
                res_spec,
                whole(start),
                whole(gate_factor),
                whole(up_factor),
                whole(used_t),
            ],
            out_specs=[
                pl.BlockSpec((1, width, CAND_DEV), lambda i, scalars: (0, late(i, scalars), 0)),
                pl.BlockSpec((1, width, CAND_DEV), lambda i, scalars: (0, late(i, scalars), 0)),
                pl.BlockSpec((1, CAND_DEV, width), lambda i, scalars: (0, 0, late(i, scalars))),
            ],
            scratch_shapes=[
                pltpu.VMEM((tok_count, CAND_DEV), F32),
                pltpu.VMEM((tok_count, 2 * CAND_DEV), BF),
            ],
        ),
        compiler_params=params(48),
        cost_estimate=cost(7 * product // 2, 40 << 20),
        name="gradients",
    )(
        scalars,
        grad_own,
        grad_own,
        grad_other,
        grad_other,
        down_four,
        res_1,
        res_2,
        start,
        gate_factor,
        up_factor,
        used_t,
    )


def shards(
    tokens,
    attn_gain,
    ffn_gain,
    w_query,
    w_key,
    w_value,
    w_out,
    w_gate,
    w_up,
    w_down,
    doc_ids,
    widths,
):
    cand_index = lax.axis_index("cand")
    tp_index = lax.axis_index("tp")
    core = (tp_index % 2).astype(jnp.int32)
    cands = lax.axis_size("cand")
    tps = lax.axis_size("tp")
    tok_count, width = tokens.shape
    ff_dev = w_gate.shape[1]
    tok_cand = tok_count // cands
    tok_tp = tok_count // tps
    nothing = jnp.zeros((1,), jnp.int32)

    down_across = lax.ppermute(w_down[:CAND_DEV], "cand", ACROSS_Z)

    heads_dev = w_query.shape[1] // HEAD_DIM
    kv_index = tp_index * heads_dev // (HEADS // KV_HEADS)
    zero = jnp.zeros_like(kv_index)
    q_width = heads_dev * HEAD_DIM
    part, _ = project(
        tokens,
        attn_gain,
        (w_query, w_key, w_value),
        (q_width, HEAD_DIM, HEAD_DIM),
        (zero, kv_index, kv_index),
        60,
        "project_qkv",
    )
    received = exchange(part.reshape(cands, tok_cand, part.shape[1]), "cand")
    received, down_across = lax.optimization_barrier((received, down_across))
    down_block = jnp.concatenate([w_down[:CAND_DEV], down_across, w_down[CAND_DEV:]], axis=0)
    down_four = lax.all_gather(down_block, "cand", axis=0, axis_index_groups=SAME_Z)
    qkv_width = part.shape[1] - LANES
    copies = summed_copies(
        qkv_body, (received,), [whole(received)], nothing, cands, tok_cand, qkv_width, "sum_qkv"
    )
    qkv = exchange(copies, "cand").reshape(tok_count, qkv_width)
    query = qkv[:, :q_width].reshape(tok_count, heads_dev, HEAD_DIM)
    key_rows = qkv[:, q_width : q_width + HEAD_DIM]
    value_rows = qkv[:, q_width + HEAD_DIM :]

    scores = jnp.einsum(
        "qhd,kd->hqk", query, key_rows, preferred_element_type=F32
    ) * HEAD_DIM ** (-0.5)
    position = lax.iota(jnp.int32, tok_count)
    allowed = (position[None, :] <= position[:, None]) & (doc_ids[None, :] == doc_ids[:, None])
    scores = jnp.where(allowed[None], scores, -1e30)
    peak_score = jnp.max(scores, axis=-1, keepdims=True)
    expo = jnp.exp(scores - peak_score)
    weights_bf = (expo / jnp.sum(expo, axis=-1, keepdims=True)).astype(BF)
    attended = jnp.einsum("hqk,kd->qhd", weights_bf, value_rows, preferred_element_type=F32)
    attended = attended.astype(BF).reshape(tok_count, heads_dev * HEAD_DIM)
    out_part = jnp.dot(attended, w_out, preferred_element_type=F32).astype(BF)
    received = exchange(out_part.reshape(tps, tok_tp, width), "tp")
    copies = summed_copies(
        residual_body,
        (received, tokens),
        [
            whole(received),
            pl.BlockSpec((tok_tp, width), lambda i, scalars: (scalars[0], 0)),
        ],
        tp_index.astype(jnp.int32)[None],
        tps,
        tok_tp,
        width,
        "sum_attention",
    )
    residual = exchange(copies, "tp").reshape(tok_count, width)

    part, scaled_res = project(
        residual, ffn_gain, (w_gate, w_up), (ff_dev, ff_dev), (zero, zero), 16, "project_gate_up"
    )
    received = exchange(part.reshape(cands, tok_cand, part.shape[1]), "cand")
    payload, minus_hidden = gate_up_sums(core[None], received, scaled_res)
    gathered = lax.all_gather(payload, "cand", axis=0)
    gathered_other = lax.ppermute(gathered, "tp", CORE_PAIRS)
    minus_hidden_across = lax.ppermute(minus_hidden, "cand", ACROSS_Z)

    live = (widths // tps).astype(jnp.int32)
    own_live = jnp.sum(jnp.where(lax.iota(jnp.int32, widths.shape[0]) == cand_index, live, 0))
    z_index = (cand_index // 4).astype(jnp.int32)
    scalars = jnp.concatenate([core[None], own_live[None], live, z_index[None]])
    for_other = dropped_output(scalars, minus_hidden, minus_hidden_across, down_four, True)
    away = lax.ppermute(for_other, "tp", CORE_PAIRS)
    mine = dropped_output(scalars, minus_hidden, minus_hidden_across, down_four, False)
    pair_sum = (mine.astype(F32) + away.astype(F32)).astype(BF)
    chunk = tok_cand // 2
    parts = pair_sum.reshape(cands * tps // 2, chunk, width)
    received = exchange(parts, ("cand", "tp"), SAME_CORE_ALL)
    copies = sum_error(received.reshape(cands, tps // 2, chunk, width))
    grad_own = exchange(copies, "tp", SAME_CORE).reshape(2, 4, 2, 4, chunk, width)
    grad_other = lax.ppermute(grad_own, "tp", CORE_PAIRS)

    start = own_back(scalars, grad_own, down_four)
    return tuple(
        gradients(
            scalars,
            grad_own,
            grad_other,
            down_four,
            gathered,
            gathered_other,
            start,
            *factors(scalars, gathered, tok_cand),
        )
    )


def solution(mesh):
    in_specs = (
        P(None, "cand"),
        P("cand"),
        P("cand"),
        P("cand", "tp"),
        P("cand", None),
        P("cand", None),
        P("tp", "cand"),
        P("cand", "tp"),
        P("cand", "tp"),
        P("tp", "cand"),
        P(),
        P(),
    )
    out_specs = (P("cand", None, "tp"), P("cand", None, "tp"), P("cand", "tp", None))
    return jax.shard_map(shards, mesh=mesh, in_specs=in_specs, out_specs=out_specs, check_vma=False)
```

time: 797 us -> 290 us (0.36)
  waiting for transfers between devices: 541 us -> 109 us
  blocking collectives: 175 us -> 67.3 us
  Pallas kernels: 0 us -> 50.4 us
  matrix products: 49.6 us -> 2.35 us
  starting transfers between devices: 0.47 us -> 30.7 us
    psum x2 -> x0, waiting for transfers between devices: 233 us -> none  [the longest x1 135 us: shards(): lax.psum(jnp.dot(attended, w_out, preferred_element_type=jnp.float32), 'tp')]
    psum x4 -> x0, blocking collectives: 175 us -> none  [the longest x1 68.7 us: shards(): target_block = lax.psum(out_part, 'tp').astype(jnp.bfloat16)]
    all_gather x4 -> x2, waiting for transfers between devices: 209 us -> 41.5 us  [the longest x1 41.5 us: shards(): gathered = lax.all_gather(payload, 'cand', axis=0)]
    reduce_scatter x1 -> x0, waiting for transfers between devices: 98.3 us -> none  [shards(): lax.psum_scatter(pred_part, 'tp', scatter_dimension=0, tiled=True)]
    all_to_all x0 -> x3, blocking collectives: none -> 67.3 us  [exchange(): return lax.all_to_all(blocks, axis, 0, 0, axis_index_groups=groups)]
    all_to_all x0 -> x4, waiting for transfers between devices: none -> 64.4 us  [exchange(): return lax.all_to_all(blocks, axis, 0, 0, axis_index_groups=groups)]
    pallas_call x0 -> x11, Pallas kernels: none -> 50.4 us  [the longest x1 21.7 us: gradients(): pl.pallas_call(gradient_kernel, out_shape=[jax.ShapeDtypeStruct((1, group...]
    dot_general x12 -> x1, matrix products: 47.5 us -> 0.32 us  [shards(): out_part = jnp.dot(attended, w_out, preferred_element_type=F32).astype(BF)]
  transfers between devices with their start and end apart: 7 -> 11, of which waited for: 7 -> 5; matrix products, arithmetic and copies ran while one was open for 4% -> 3% of each run, Pallas kernels for 0% -> 10%
where the time goes in v2:
time: 290 us; the launch traced here: 289 us
  waiting for transfers between devices  109 us (38%)
  blocking collectives  67.3 us (23%)
  Pallas kernels  50.4 us (17%)
  starting transfers between devices  30.7 us (11%)
  between operations  14.3 us (5%)
  local copies, waits for them, and re-layouts  8.84 us (3%)
  other arithmetic  6.45 us (2%)
    all_to_all x3, blocking collectives, exchange(): return lax.all_to_all(blocks, axis, 0, 0, axis_index_groups=groups)  67.3 us
    all_to_all x4, waiting for transfers between devices, exchange(): return lax.all_to_all(blocks, axis, 0, 0, axis_index_groups=groups)  64.4 us
    all_gather x1, waiting for transfers between devices, shards(): gathered = lax.all_gather(payload, 'cand', axis=0)  41.5 us
    all_to_all x4, starting transfers between devices, exchange(): return lax.all_to_all(blocks, axis, 0, 0, axis_index_groups=groups)  22.4 us
    pallas_call x1, Pallas kernels, gradients(): pl.pallas_call(gradient_kernel, out_shape=[jax.ShapeDtypeStruct((1, group...  21.7 us
    pallas_call x2, Pallas kernels, dropped_output(): pl.pallas_call(dropped_kernel, out_shape=jax.ShapeDtypeStruct((8, 2, 4, c...  11.3 us
    unnamed x34, local copies, waits for them, and re-layouts  7.44 us
    pallas_call x1, Pallas kernels, own_back(): pl.pallas_call(back_kernel, out_shape=jax.ShapeDtypeStruct((tok_count, CA...  5.94 us
  transfers between devices with their start and end apart: 11, of which 5 were waited for; matrix products, arithmetic and copies ran while one was open for 3% of the time, Pallas kernels for 10%

profile of v2, /device:TPU:1, one launch (start us, length us, event | category | flops | bytes accessed | tf_op | source)
XLA Modules:
  0.0 289.2 jit_solution(13707845404327986824)
XLA Ops:
  8.4 4.5 %collective-permute-start = (bf16[768,512]{1,0:T(8,128)(2,1)S(1)}, bf16[768,512]{1,0:T(8,128)(2,1)S(1)}, u32[]{:S(2)}, u32[]{:S(2)}) collective-permute-start(bf16[768,512]{1,0:T(8,128)(2,1)S(1)} %slice.16), channel_id=1, source_target_pairs={{0,64},{16,80},{32,96},{48,112},{64,0},{80,16},{96,32},{112,48},{1... | collective-permute-start | bytes 2359304 | tf_op jit(solution)/shard_map/ppermute | solution.py:516
  13.6 3.4 %project_qkv.1 = (bf16[512,640]{1,0:T(8,128)(2,1)}, bf16[512,512]{1,0:T(8,128)(2,1)}) custom-call(s32[3]{0:T(128)} %pad_add_fusion.1.scalars, bf16[512,512]{1,0:T(8,128)(2,1)} %refs_1_.4, f32[1,512]{1,0:T(1,128)} %bitcast.74, bf16[512,256]{1,0:T(8,128)(2,1)} %refs_0_.2, bf16[512,1024]{1,0:T(8,128)(2,1)} %refs_1_.3, bf16[512,1024]{1,0:T(8,128)(2,1)} %refs_2_.1), custom_call_target="tpu_custom_call" | custom-call | flops 335544320 | bytes 1310720 | tf_op jit(solution)/shard_map/project_qkv/pallas_call | solution.py:76
  17.0 4.2 %all-to-all-start = ((bf16[8,64,640]{2,1,0:T(8,128)(2,1)}), bf16[8,64,640]{2,1,0:T(8,128)(2,1)S(1)}, u32[]{:S(2)}, u32[]{:S(2)}) async-start(bf16[8,64,640]{2,1,0:T(8,128)(2,1)} %bitcast.70), calls=%async_computation | async-start | bytes 1310720 | tf_op jit(solution)/shard_map/all_to_all | solution.py:28
  21.2 16.0 %all-to-all-done.refs_0_ = bf16[8,64,640]{2,1,0:T(8,128)(2,1)S(1)} async-done(((bf16[8,64,640]{2,1,0:T(8,128)(2,1)}), bf16[8,64,640]{2,1,0:T(8,128)(2,1)S(1)}, u32[]{:S(2)}, u32[]{:S(2)}) %all-to-all-start) | async-done | bytes 655392 | tf_op jit(solution)/shard_map/all_to_all | solution.py:28
  39.5 6.6 %all-to-all-start.1 = ((bf16[8,64,512]{2,1,0:T(8,128)(2,1)}), bf16[8,64,512]{2,1,0:T(8,128)(2,1)S(1)}, u32[]{:S(2)}, u32[]{:S(2)}) async-start(bf16[8,64,512]{2,1,0:T(8,128)(2,1)} %sum_qkv.1), calls=%async_computation.1 | async-start | bytes 1048576 | tf_op jit(solution)/shard_map/all_to_all | solution.py:28
  46.3 10.9 %all-to-all-done.1 = bf16[8,64,512]{2,1,0:T(8,128)(2,1)S(1)} async-done(((bf16[8,64,512]{2,1,0:T(8,128)(2,1)}), bf16[8,64,512]{2,1,0:T(8,128)(2,1)S(1)}, u32[]{:S(2)}, u32[]{:S(2)}) %all-to-all-start.1) | async-done | bytes 524320 | tf_op jit(solution)/shard_map/all_to_all | solution.py:28
  59.8 15.8 %all_to_all.35.refs_0_ = bf16[16,32,512]{2,1,0:T(8,128)(2,1)S(1)} all-to-all(bf16[16,32,512]{2,1,0:T(8,128)(2,1)S(1)} %bitcast.66), channel_id=1, replica_groups=mesh['cand'=8,'tp'=16] {'tp'}, dimensions={0} | all-to-all | bytes 1048576 | tf_op jit(solution)/shard_map/all_to_all | solution.py:28
  75.6 13.5 %all_to_all.36 = bf16[16,32,512]{2,1,0:T(8,128)(2,1)S(1)} all-to-all(bf16[16,32,512]{2,1,0:T(8,128)(2,1)S(1)} %sum_attention.1), channel_id=1, replica_groups=mesh['cand'=8,'tp'=16] {'tp'}, dimensions={0} | all-to-all | bytes 1048576 | tf_op jit(solution)/shard_map/all_to_all | solution.py:28
  89.1 2.0 project_gate_up.1
  92.4 3.6 %all-to-all-start.4 = ((bf16[8,64,1920]{2,1,0:T(8,128)(2,1)}), bf16[8,64,1920]{2,1,0:T(8,128)(2,1)S(1)}, u32[]{:S(2)}, u32[]{:S(2)}) async-start(bf16[8,64,1920]{2,1,0:T(8,128)(2,1)} %bitcast.56), calls=%async_computation.4 | async-start | bytes 3932160 | tf_op jit(solution)/shard_map/all_to_all | solution.py:28
  96.1 37.5 %all-to-all-done.4.received = bf16[8,64,1920]{2,1,0:T(8,128)(2,1)S(1)} async-done(((bf16[8,64,1920]{2,1,0:T(8,128)(2,1)}), bf16[8,64,1920]{2,1,0:T(8,128)(2,1)S(1)}, u32[]{:S(2)}, u32[]{:S(2)}) %all-to-all-start.4) | async-done | bytes 1966112 | tf_op jit(solution)/shard_map/all_to_all | solution.py:28
  137.1 3.0 %collective-permute-done.1.other = bf16[64,896]{1,0:T(8,128)(2,1)S(1)} collective-permute-done((bf16[64,896]{1,0:T(8,128)(2,1)S(1)}, bf16[64,896]{1,0:T(8,128)(2,1)S(1)}, u32[]{:S(2)}, u32[]{:S(2)}) %collective-permute-start.1) | collective-permute-done | bytes 114720 | tf_op jit(solution)/shard_map/ppermute | solution.py:579
  140.8 5.6 %dropped_output.3 = bf16[8,2,4,32,512]{4,3,2,1,0:T(8,128)(2,1)} custom-call(s32[11]{0:T(128)} %pad_add_fusion.scalars, bf16[64,896]{1,0:T(8,128)(2,1)} %copy-done.6, bf16[64,896]{1,0:T(8,128)(2,1)} %copy-done.14, bf16[4,1664,512]{2,1,0:T(8,128)(2,1)} %bitcast.59, bf16[4,1664,512]{2,1,0:T(8,128)(2,1)} %bitcast.60), custom_call_target="tpu_custom_call" | custom-call | flops 1879048192 | bytes 3932160 | tf_op jit(solution)/shard_map/dropped_output/pallas_call | solution.py:219
  146.4 2.5 collective-permute-start.2
  149.0 5.6 %dropped_output.2 = bf16[8,2,4,32,512]{4,3,2,1,0:T(8,128)(2,1)} custom-call(s32[11]{0:T(128)} %pad_add_fusion.scalars, bf16[64,896]{1,0:T(8,128)(2,1)} %copy-done.6, bf16[64,896]{1,0:T(8,128)(2,1)} %copy-done.14, bf16[4,1664,512]{2,1,0:T(8,128)(2,1)} %bitcast.61, bf16[4,1664,512]{2,1,0:T(8,128)(2,1)} %bitcast.62), custom_call_target="tpu_custom_call" | custom-call | flops 1879048192 | bytes 3932160 | tf_op jit(solution)/shard_map/dropped_output/pallas_call | solution.py:219
  154.6 2.4 add_convert_fusion
  157.0 38.1 %all_to_all.37 = bf16[64,32,512]{2,1,0:T(8,128)(2,1)S(1)} all-to-all(bf16[64,32,512]{2,1,0:T(8,128)(2,1)S(1)} %bitcast.65), channel_id=1, replica_groups={{0,2,4,6,8,10,12,14,16,18,20,22,24,26,28,30,32,34,36,38,40,42,44,46,48,..., dimensions={0} | all-to-all | bytes 4194304 | tf_op jit(solution)/shard_map/all_to_all | solution.py:28
  195.1 1.9 sum_error.1
  197.0 8.1 %all-to-all-start.6 = ((bf16[8,8,32,512]{3,2,1,0:T(8,128)(2,1)}), bf16[8,8,32,512]{3,2,1,0:T(8,128)(2,1)}, u32[]{:S(2)}, u32[]{:S(2)}) async-start(bf16[8,8,32,512]{3,2,1,0:T(8,128)(2,1)} %sum_error.1), calls=%async_computation.6 | async-start | bytes 4194304 | tf_op jit(solution)/shard_map/all_to_all | solution.py:28
  205.1 41.5 %all-gather.7.cloned.1.call-done = bf16[14848,128]{1,0:T(8,128)(2,1)} async-done(((bf16[1856,128]{1,0:T(8,128)(2,1)}), bf16[14848,128]{1,0:T(8,128)(2,1)}) %all-gather.7.cloned.1.call-update) | async-done | bytes 3801104 | tf_op jit(solution)/shard_map/all_gather | solution.py:577
  247.5 2.1 copy-done.2
  249.5 1.8 factors.1
  252.2 5.9 %own_back.1.start = f32[512,768]{1,0:T(8,128)} custom-call(s32[11]{0:T(128)} %pad_add_fusion.scalars, bf16[2,4,2,4,32,512]{5,4,3,2,1,0:T(8,128)(2,1)} %bitcast.21.own_1.own_2, bf16[2,4,2,4,32,512]{5,4,3,2,1,0:T(8,128)(2,1)} %bitcast.21.own_1.own_2, bf16[4,1664,512]{2,1,0:T(8,128)(2,1)} %bitcast.63), custom_call_target="tpu_custom_call" | custom-call | flops 1610612736 | bytes 10485760 | tf_op jit(solution)/shard_map/own_back/pallas_call | solution.py:364
  260.7 21.7 %gradients.1 = (bf16[1,4096,768]{2,1,0:T(8,128)(2,1)}, bf16[1,4096,768]{2,1,0:T(8,128)(2,1)}, bf16[1,768,4096]{2,1,0:T(8,128)(2,1)}) custom-call(s32[11]{0:T(128)S(1)} %copy-done.8, bf16[2,4,2,4,32,512]{5,4,3,2,1,0:T(8,128)(2,1)} %bitcast.21.own_1.own_2, bf16[2,4,2,4,32,512]{5,4,3,2,1,0:T(8,128)(2,1)} %bitcast.21.own_1.own_2, ...), custom_call_target="tpu_custom_call" | custom-call | flops 11274289152 | bytes 41943040 | tf_op jit(solution)/shard_map/gradients/pallas_call | solution.py:438
  (63 shorter events, 16.8 us)
Async XLA Ops:
  7.2 52.2 %copy-start = (bf16[256,512]{1,0:T(8,128)(2,1)S(1)}, bf16[256,512]{1,0:T(8,128)(2,1)}, u32[]{:S(2)}) copy-start(bf16[256,512]{1,0:T(8,128)(2,1)} %param.18) | copy-start | bytes 786436
  8.4 28.8 %collective-permute-start = (bf16[768,512]{1,0:T(8,128)(2,1)S(1)}, bf16[768,512]{1,0:T(8,128)(2,1)S(1)}, u32[]{:S(2)}, u32[]{:S(2)}) collective-permute-start(bf16[768,512]{1,0:T(8,128)(2,1)S(1)} %slice.16), channel_id=1, source_target_pairs={{0,64},{16,80},{32,96},{48,112},{64,0},{80,16},{96,32},{112,48},{1... | collective-permute-start | bytes 2359304 | tf_op jit(solution)/shard_map/ppermute | solution.py:516
  13.6 23.6 %slice-start = ((bf16[896,512]{1,0:T(8,128)(2,1)}), bf16[128,512]{1,0:T(8,128)(2,1)S(1)}, s32[]{:S(2)}) async-start(bf16[896,512]{1,0:T(8,128)(2,1)} %param.21), calls=%async_computation.9 | async-start | bytes 262144 | tf_op jit(solution)/shard_map/slice | solution.py:533
  17.0 20.2 %all-to-all-start = ((bf16[8,64,640]{2,1,0:T(8,128)(2,1)}), bf16[8,64,640]{2,1,0:T(8,128)(2,1)S(1)}, u32[]{:S(2)}, u32[]{:S(2)}) async-start(bf16[8,64,640]{2,1,0:T(8,128)(2,1)} %bitcast.70), calls=%async_computation | async-start | bytes 1310720 | tf_op jit(solution)/shard_map/all_to_all | solution.py:28
  21.2 119.0 %all-gather.5.cloned.1.call-start = ((), (), s32[]{:S(2)}) async-start(), calls=%async_computation.7 | async-start | bytes 8519680 | tf_op jit(solution)/shard_map/all_gather | solution.py:534
  38.5 7.6 %copy-start.15 = (s32[512]{0:T(512)S(1)}, s32[512]{0:T(512)}, u32[]{:S(2)}) copy-start(s32[512]{0:T(512)} %param.22) | copy-start | bytes 6148
  39.5 17.6 %all-to-all-start.1 = ((bf16[8,64,512]{2,1,0:T(8,128)(2,1)}), bf16[8,64,512]{2,1,0:T(8,128)(2,1)S(1)}, u32[]{:S(2)}, u32[]{:S(2)}) async-start(bf16[8,64,512]{2,1,0:T(8,128)(2,1)} %sum_qkv.1), calls=%async_computation.1 | async-start | bytes 1048576 | tf_op jit(solution)/shard_map/all_to_all | solution.py:28
  59.4 16.2 %copy-start.3 = (bf16[512,512]{1,0:T(8,128)(2,1)S(1)}, bf16[512,512]{1,0:T(8,128)(2,1)}, u32[]{:S(2)}) copy-start(bf16[512,512]{1,0:T(8,128)(2,1)} %refs_1_.4) | copy-start | bytes 1572868
  59.7 29.4 %copy-start.9 = (bf16[512,896]{1,0:T(8,128)(2,1)S(1)}, bf16[512,896]{1,0:T(8,128)(2,1)}, u32[]{:S(2)}) copy-start(bf16[512,896]{1,0:T(8,128)(2,1)} %refs_0_.3) | copy-start | bytes 2752516
  59.7 29.4 %copy-start.10 = (bf16[512,896]{1,0:T(8,128)(2,1)S(1)}, bf16[512,896]{1,0:T(8,128)(2,1)}, u32[]{:S(2)}) copy-start(bf16[512,896]{1,0:T(8,128)(2,1)} %refs_1_.5) | copy-start | bytes 2752516
  59.7 29.4 %copy-start.13 = (f32[512]{0:T(512)S(1)}, f32[512]{0:T(512)}, u32[]{:S(2)}) copy-start(f32[512]{0:T(512)} %param.14) | copy-start | bytes 6148
  92.4 41.2 %all-to-all-start.4 = ((bf16[8,64,1920]{2,1,0:T(8,128)(2,1)}), bf16[8,64,1920]{2,1,0:T(8,128)(2,1)S(1)}, u32[]{:S(2)}, u32[]{:S(2)}) async-start(bf16[8,64,1920]{2,1,0:T(8,128)(2,1)} %bitcast.56), calls=%async_computation.4 | async-start | bytes 3932160 | tf_op jit(solution)/shard_map/all_to_all | solution.py:28
  96.0 39.2 %copy-start.16 = (s32[8]{0:T(128)S(1)}, s32[8]{0:T(128)}, u32[]{:S(2)}) copy-start(s32[8]{0:T(128)} %param.23) | copy-start | bytes 100
  96.0 150.6 %all-gather.7.cloned.1.call-start = ((), (), s32[]{:S(2)}) async-start(), calls=%async_computation.8 | async-start | bytes 4276224 | tf_op jit(solution)/shard_map/all_gather | solution.py:577
  134.9 5.3 %copy-start.6 = (bf16[64,896]{1,0:T(8,128)(2,1)}, bf16[64,896]{1,0:T(8,128)(2,1)S(1)}, u32[]{:S(2)}) copy-start(bf16[64,896]{1,0:T(8,128)(2,1)S(1)} %get-tuple-element.17.own) | copy-start | bytes 344068
  134.9 5.2 %collective-permute-start.1 = (bf16[64,896]{1,0:T(8,128)(2,1)S(1)}, bf16[64,896]{1,0:T(8,128)(2,1)S(1)}, u32[]{:S(2)}, u32[]{:S(2)}) collective-permute-start(bf16[64,896]{1,0:T(8,128)(2,1)S(1)} %get-tuple-element.17.own), channel_id=1, source_target_pairs={{0,64},{16,80},{32,96},{48,112},{64,0},{80,16},{96,32},{112,48},{1... | collective-permute-start | bytes 344072 | tf_op jit(solution)/shard_map/ppermute | solution.py:579
  146.4 8.2 %collective-permute-start.2 = (bf16[8,2,4,32,512]{4,3,2,1,0:T(8,128)(2,1)}, bf16[8,2,4,32,512]{4,3,2,1,0:T(8,128)(2,1)S(1)}, u32[]{:S(2)}, u32[]{:S(2)}) collective-permute-start(bf16[8,2,4,32,512]{4,3,2,1,0:T(8,128)(2,1)} %dropped_output.3), channel_id=1, source_target_pairs={{0,1},{1,0},{2,3},{3,2},{4,5},{5,4},{6,7},{7,6},{8,9},{9,8},{10,11... | collective-permute-start | bytes 6291464 | tf_op jit(solution)/shard_map/ppermute | solution.py:586
  197.0 50.5 %copy-start.7 = (s32[11]{0:T(128)S(1)}, s32[11]{0:T(128)}, u32[]{:S(2)}) copy-start(s32[11]{0:T(128)} %pad_add_fusion.scalars) | copy-start | bytes 136
  197.0 50.4 %all-to-all-start.6 = ((bf16[8,8,32,512]{3,2,1,0:T(8,128)(2,1)}), bf16[8,8,32,512]{3,2,1,0:T(8,128)(2,1)}, u32[]{:S(2)}, u32[]{:S(2)}) async-start(bf16[8,8,32,512]{3,2,1,0:T(8,128)(2,1)} %sum_error.1), calls=%async_computation.6 | async-start | bytes 4194304 | tf_op jit(solution)/shard_map/all_to_all | solution.py:28
  246.6 11.5 %collective-permute-start.4 = (bf16[8,1856,128]{2,1,0:T(8,128)(2,1)}, bf16[8,1856,128]{2,1,0:T(8,128)(2,1)}, u32[]{:S(2)}, u32[]{:S(2)}) collective-permute-start(bf16[8,1856,128]{2,1,0:T(8,128)(2,1)} %bitcast.53), channel_id=1, source_target_pairs={{0,1},{1,0},{2,3},{3,2},{4,5},{5,4},{6,7},{7,6},{8,9},{9,8},{10,11... | collective-permute-start | bytes 11403272 | tf_op jit(solution)/shard_map/ppermute | solution.py:578
  247.4 10.7 %collective-permute-start.3 = (bf16[2,4,2,4,32,512]{5,4,3,2,1,0:T(8,128)(2,1)}, bf16[2,4,2,4,32,512]{5,4,3,2,1,0:T(8,128)(2,1)}, u32[]{:S(2)}, u32[]{:S(2)}) collective-permute-start(bf16[2,4,2,4,32,512]{5,4,3,2,1,0:T(8,128)(2,1)} %bitcast.21.own_1.own_2), channel_id=1, source_target_pairs={{0,1},{1,0},{2,3},{3,2},{4,5},{5,4},{6,7},{7,6},{8,9},{9,8},{10,11... | collective-permute-start | bytes 6291464 | tf_op jit(solution)/shard_map/ppermute | solution.py:594
  247.5 2.1 copy-start.2
  252.2 5.9 %copy-start.8 = (s32[11]{0:T(128)S(1)}, s32[11]{0:T(128)}, u32[]{:S(2)}) copy-start(s32[11]{0:T(128)} %pad_add_fusion.scalars) | copy-start | bytes 136
  260.7 21.7 %copy-start.1 = (bf16[256,512]{1,0:T(8,128)(2,1)S(1)}, bf16[256,512]{1,0:T(8,128)(2,1)}, u32[]{:S(2)}) copy-start(bf16[256,512]{1,0:T(8,128)(2,1)} %param.18) | copy-start | bytes 786436
  (5 other events, 5.3 us)
Sparse Core Ops, SparseCore 0:
  38.7 93.0 all-gather.4
  135.0 111.5 all-gather.6

commit v3 on v2

v3 whole, which is shorter than its diff:
```python
import functools

import jax
import jax.numpy as jnp
from jax import lax
from jax.experimental import pallas as pl
from jax.experimental.pallas import tpu as pltpu
from jax.sharding import PartitionSpec as P

D = 4096
HEADS = 32
KV_HEADS = 8
HEAD_DIM = 128
CAND_DEV = 768
LANES = 128
EPSILON = 1e-05
BF = jnp.bfloat16
F32 = jnp.float32

VMEM = pl.BlockSpec(memory_space=pltpu.VMEM)
CORE_PAIRS = [(i, i ^ 1) for i in range(16)]
ACROSS_Z = [(i, i ^ 4) for i in range(8)]
SAME_Z = [[0, 1, 2, 3], [4, 5, 6, 7]]
SAME_CORE_ALL = [[c * 16 + t for c in range(8) for t in range(core, 16, 2)] for core in range(2)]
SAME_CORE = [list(range(core, 16, 2)) for core in range(2)]


def exchange(blocks, axis, groups=None):
    return lax.all_to_all(blocks, axis, 0, 0, axis_index_groups=groups)


def lanes_of(column):
    high = column.astype(BF).astype(F32)
    lane = lax.broadcasted_iota(jnp.int32, (column.shape[0], LANES), 1)
    return jnp.where(lane == 0, high, jnp.where(lane == 1, column - high, 0.0)).astype(BF)


def column_of(lanes):
    return lanes[:, 0:1].astype(F32) + lanes[:, 1:2].astype(F32)


def params(limit_mib):
    return pltpu.CompilerParams(
        dimension_semantics=("arbitrary",), vmem_limit_bytes=limit_mib << 20
    )


def cost(flops, bytes_accessed, transcendentals=0):
    return pl.CostEstimate(
        flops=flops, bytes_accessed=bytes_accessed, transcendentals=transcendentals
    )


def project_kernel(scalars, rows, gain, *refs):
    *weights, out, scaled_out = refs
    wide = rows[...].astype(F32)
    scaled = (wide * gain[...]).astype(BF)
    scaled_out[...] = scaled
    at = 0
    for weight in weights:
        width = weight.shape[1]
        out[:, at : at + width] = jnp.dot(
            scaled, weight[...], preferred_element_type=F32
        ).astype(BF)
        at += width
    out[:, at:] = lanes_of(jnp.sum(wide * wide, axis=1, keepdims=True))


def project(rows, gain, weights, widths, columns, limit_mib, name):
    count, depth = rows.shape
    out_width = sum(widths) + LANES
    tile = count // 2

    def weight_spec(i, width):
        return pl.BlockSpec((depth, width), lambda r, scalars: (0, scalars[i]))

    return pl.pallas_call(
        project_kernel,
        out_shape=[
            jax.ShapeDtypeStruct((count, out_width), BF),
            jax.ShapeDtypeStruct((count, depth), BF),
        ],
        grid_spec=pltpu.PrefetchScalarGridSpec(
            num_scalar_prefetch=1,
            grid=(2,),
            in_specs=[
                pl.BlockSpec((tile, depth), lambda r, scalars: (r, 0)),
                pl.BlockSpec((1, depth), lambda r, scalars: (0, 0)),
            ]
            + [weight_spec(i, width) for i, width in enumerate(widths)],
            out_specs=[
                pl.BlockSpec((tile, out_width), lambda r, scalars: (r, 0)),
                pl.BlockSpec((tile, depth), lambda r, scalars: (r, 0)),
            ],
        ),
        compiler_params=params(limit_mib),
        cost_estimate=cost(2 * count * depth * out_width, 2 * out_width * (count + depth)),
        name=name,
    )(jnp.stack(columns).astype(jnp.int32), rows, gain.reshape(1, depth), *weights)


def copies_kernel(body, scalars, *refs):
    *ins, out = refs
    value = body(*ins)
    for i in range(out.shape[0]):
        out[i] = value


def summed_copies(body, ins, in_specs, scalars, copies, rows, width, name):
    return pl.pallas_call(
        functools.partial(copies_kernel, body),
        out_shape=jax.ShapeDtypeStruct((copies, rows, width), BF),
        grid_spec=pltpu.PrefetchScalarGridSpec(
            num_scalar_prefetch=1,
            grid=(1,),
            in_specs=in_specs,
            out_specs=pl.BlockSpec((copies, rows, width), lambda i, scalars: (0, 0, 0)),
        ),
        compiler_params=params(12),
        cost_estimate=cost(0, 4 * copies * rows * width),
        name=name,
    )(scalars, *ins)


def whole(array):
    return pl.BlockSpec(array.shape, lambda i, scalars: (0,) * array.ndim)


def to_vmem_kernel(blocks, out):
    out[pl.program_id(0)] = blocks[0]


def to_vmem(blocks):
    return pl.pallas_call(
        to_vmem_kernel,
        out_shape=jax.ShapeDtypeStruct(blocks.shape, blocks.dtype),
        grid=(blocks.shape[0],),
        in_specs=[pl.BlockSpec((1,) + blocks.shape[1:], lambda i: (i, 0, 0))],
        out_specs=VMEM,
        compiler_params=params(12),
        cost_estimate=cost(0, 4 * blocks.size),
        name="to_vmem",
    )(blocks)


def qkv_body(received):
    total = jnp.sum(received[...].astype(F32), axis=0)
    width = total.shape[1] - LANES
    squares = total[:, width : width + 1] + total[:, width + 1 : width + 2]
    return (total[:, :width] * lax.rsqrt(squares / D + EPSILON)).astype(BF)


def residual_body(received, rows):
    return (rows[...].astype(F32) + jnp.sum(received[...].astype(F32), axis=0)).astype(BF)


def sums_kernel(scalars, received, scaled_res, res_across, payload, minus_hidden):
    ff_dev = minus_hidden.shape[1]
    rows = received.shape[1]
    total = jnp.sum(received[...].astype(F32), axis=0)
    squares = total[:, 2 * ff_dev : 2 * ff_dev + 1] + total[:, 2 * ff_dev + 1 : 2 * ff_dev + 2]
    scale = lax.rsqrt(squares / D + EPSILON)
    gate = total[:, :ff_dev] * scale
    up = total[:, ff_dev : 2 * ff_dev] * scale
    minus_hidden[...] = (-(gate * jax.nn.sigmoid(gate) * up)).astype(BF)
    parts = (gate[:, :CAND_DEV].astype(BF), up[:, :CAND_DEV].astype(BF), lanes_of(scale), scaled_res, res_across)
    at = 0
    for part in parts:
        count = part.shape[0]
        for lane in range(0, part.shape[1], LANES):
            payload[at : at + count, :] = part[:, lane : lane + LANES]
            at += count


def gate_up_sums(scalars, received, scaled_res, res_across):
    _, rows, width = received.shape
    ff_dev = (width - LANES) // 2
    half, depth = scaled_res.shape[0] // 2, scaled_res.shape[1]
    payload_rows = rows * SUMS_TILES + 2 * half * (depth // LANES)
    return pl.pallas_call(
        sums_kernel,
        out_shape=[
            jax.ShapeDtypeStruct((payload_rows, LANES), BF),
            jax.ShapeDtypeStruct((rows, ff_dev), BF),
        ],
        grid_spec=pltpu.PrefetchScalarGridSpec(
            num_scalar_prefetch=1,
            grid=(1,),
            in_specs=[
                whole(received),
                pl.BlockSpec((half, depth), lambda i, scalars: (scalars[0], 0)),
                whole(res_across),
            ],
            out_specs=[
                pl.BlockSpec((payload_rows, LANES), lambda i, scalars: (0, 0)),
                pl.BlockSpec((rows, ff_dev), lambda i, scalars: (0, 0)),
            ],
        ),
        compiler_params=params(20),
        cost_estimate=cost(0, 4 * received.size, rows * ff_dev),
        name="gate_up_sums",
    )(scalars, received, scaled_res, res_across)


LIVE_AT, LIVES_AT, Z_AT = 1, 2, 10
SUMS_TILES = 2 * CAND_DEV // LANES + 1


def dropped_kernel(flip, scalars, own, other, down, out, rows):
    cands, _, chunks, chunk, width = out.shape

    @pl.when(pl.program_id(0) == 0)
    def _():
        own_first = scalars[Z_AT] == 0
        unit = lax.broadcasted_iota(jnp.int32, (chunk, own.shape[1]), 1)
        for at in range(4):
            part = slice(at % 2 * chunk, (at % 2 + 1) * chunk)
            here, there = own[part, :].astype(F32), other[part, :].astype(F32)
            values = jnp.where(own_first == (at < 2), here, there)
            for c in range(8):
                kept = jnp.where(unit >= scalars[LIVES_AT + c], values, 0.0).astype(BF)
                rows[(c * 4 + at) * chunk : (c * 4 + at + 1) * chunk, :] = kept

    block = 2 * (1 - scalars[0] if flip else scalars[0]) + pl.program_id(0)
    total = jnp.dot(rows[...], down[block], preferred_element_type=F32)
    out[:, 0] = total.astype(BF).reshape(cands, chunks, chunk, width)


def dropped_output(scalars, own, other, down_four, flip):
    tok_cand, ff_dev = own.shape
    width = down_four.shape[2]
    chunk = tok_cand // 2

    return pl.pallas_call(
        functools.partial(dropped_kernel, flip),
        out_shape=jax.ShapeDtypeStruct((8, 2, 4, chunk, width), BF),
        grid_spec=pltpu.PrefetchScalarGridSpec(
            num_scalar_prefetch=1,
            grid=(2,),
            in_specs=[
                whole(own),
                whole(other),
                VMEM,
            ],
            out_specs=pl.BlockSpec(
                (8, 1, 4, chunk, width), lambda i, scalars: (0, i, 0, 0, 0)
            ),
            scratch_shapes=[pltpu.VMEM((32 * chunk, ff_dev), BF)],
        ),
        compiler_params=params(20),
        cost_estimate=cost(4 * 32 * chunk * ff_dev * width, 4 * (ff_dev + 32 * chunk) * width),
        name="dropped_output",
    )(scalars, own, other, down_four)


def tiles_of(block, first, count, rows):
    tiles = [block[..., first + i * rows : first + (i + 1) * rows, :] for i in range(count)]
    return jnp.concatenate([tile.reshape(-1, LANES) for tile in tiles], axis=1)


def factors_kernel(rows, scalars, own_sums, across_sums, gate_factor, up_factor, used_t):
    own_z = (scalars[0] + pl.program_id(0)) % 2 == scalars[Z_AT]
    payload = jnp.where(own_z, own_sums[...].astype(F32), across_sums[...].astype(F32))
    tiles = CAND_DEV // LANES
    gate = tiles_of(payload, 0, tiles, rows)
    up = tiles_of(payload, tiles * rows, tiles, rows)
    keep = lax.broadcasted_iota(jnp.int32, gate.shape, 1) < scalars[LIVE_AT]
    scale = jnp.where(keep, column_of(tiles_of(payload, 2 * tiles * rows, 1, rows)), 0.0)
    sigmoid = jax.nn.sigmoid(gate)
    activated = gate * sigmoid
    slope = sigmoid * (1.0 + gate * (1.0 - sigmoid))
    at = pl.program_id(0)
    half = gate.shape[0]
    gate_factor[pl.ds(at * half, half), :] = (up * slope * scale).astype(BF)
    up_factor[pl.ds(at * half, half), :] = (activated * scale).astype(BF)
    turned = jnp.where(keep, activated * up, 0.0).T.astype(BF)
    used_t[:, pl.ds(pl.multiple_of(at * half, half), half)] = turned


def factors(scalars, own_sums, across_sums, rows):
    groups = own_sums.shape[0]
    half = groups * rows
    tok_count = 2 * half
    factor = jax.ShapeDtypeStruct((tok_count, CAND_DEV), BF)
    return pl.pallas_call(
        functools.partial(factors_kernel, rows),
        out_shape=[factor, factor, jax.ShapeDtypeStruct((CAND_DEV, tok_count), BF)],
        grid_spec=pltpu.PrefetchScalarGridSpec(
            num_scalar_prefetch=1,
            grid=(2,),
            in_specs=[
                pl.BlockSpec((groups, rows * SUMS_TILES, LANES), lambda i, scalars: (0, 0, 0)),
            ]
            + [
                pl.BlockSpec((groups, rows * SUMS_TILES, LANES), lambda i, scalars: (0, 0, 0)),
            ],
            out_specs=[VMEM] * 3,
        ),
        compiler_params=params(24),
        cost_estimate=cost(0, 14 * tok_count * CAND_DEV, tok_count * CAND_DEV),
        name="factors",
    )(scalars, own_sums, across_sums)


def sum_error_kernel(received, out):
    value = jnp.sum(received[...].astype(F32), axis=1).astype(BF)
    for i in range(out.shape[0]):
        out[i] = value


def sum_error(received):
    groups, chips, rows, width = received.shape
    return pl.pallas_call(
        sum_error_kernel,
        out_shape=jax.ShapeDtypeStruct((chips, groups, rows, width), BF),
        grid=(4,),
        in_specs=[pl.BlockSpec((groups // 4, chips, rows, width), lambda i: (i, 0, 0, 0))],
        out_specs=pl.BlockSpec((chips, groups // 4, rows, width), lambda i: (0, i, 0, 0)),
        compiler_params=params(12),
        cost_estimate=cost(0, 4 * received.size),
        name="sum_error",
    )(received)


def contract(left, right, left_dim, right_dim):
    return lax.dot_general(
        left, right, (((left_dim,), (right_dim,)), ((), ())), preferred_element_type=F32
    )


def grad_rows_of(scalars, grad, block, z):
    rows = []
    for half in (scalars[0], 1 - scalars[0]):
        for y in range(grad.shape[3]):
            rows += [grad[block, 2 * half + i, z, y] for i in range(2)]
    return jnp.concatenate(rows, axis=0)


def back_product(scalars, grad, own_four, across_four, core):
    total = None
    for z, down in ((scalars[Z_AT], own_four), (1 - scalars[Z_AT], across_four)):
        rows = [grad_rows_of(scalars, grad, block, z) for block in range(2)]
        units = [down[2 * core + block, :CAND_DEV] for block in range(2)]
        product = contract(jnp.concatenate(rows, axis=1), jnp.concatenate(units, axis=1), 1, 1)
        total = product if total is None else total + product
    return total


def back_kernel(scalars, grad, own_four, across_four, out):
    out[...] = back_product(scalars, grad, own_four, across_four, scalars[0])


def own_back(scalars, grad_own, own_four, across_four):
    _, chunks, z, y, rows, width = grad_own.shape
    tok_count = chunks * y * rows
    return pl.pallas_call(
        back_kernel,
        out_shape=jax.ShapeDtypeStruct((tok_count, CAND_DEV), F32),
        in_specs=[pl.BlockSpec(memory_space=pltpu.SMEM), VMEM, VMEM, VMEM],
        out_specs=VMEM,
        compiler_params=pltpu.CompilerParams(vmem_limit_bytes=16 << 20),
        cost_estimate=cost(8 * tok_count * width * CAND_DEV, 10 << 20),
        name="own_back",
    )(scalars, grad_own, own_four, across_four)


def res_order_kernel(half, first_row, scalars, first, second, out):
    at = pl.program_id(0)
    tiles = out.shape[2] // LANES
    for part in range(2):
        z = jnp.where(scalars[Z_AT] == 0, part, 1 - part)
        start = first_row + part * half * tiles
        for row, ref in ((0, first), (half, second)):
            out[4 * z + at, row : row + half, :] = tiles_of(ref[0], start, tiles, half)


def res_order(scalars, gathered, gathered_other, first_row, half, width):
    blocks = gathered.shape[0]
    spec = pl.BlockSpec((1,) + gathered.shape[1:], lambda i, scalars: (i, 0, 0))
    return pl.pallas_call(
        functools.partial(res_order_kernel, half, first_row),
        out_shape=jax.ShapeDtypeStruct((2 * blocks, 2 * half, width), BF),
        grid_spec=pltpu.PrefetchScalarGridSpec(
            num_scalar_prefetch=1, grid=(blocks,), in_specs=[spec, spec], out_specs=VMEM
        ),
        compiler_params=params(16),
        cost_estimate=cost(0, 4 * gathered.size + 8 * blocks * half * width),
        name="res_order",
    )(scalars, gathered, gathered_other)


def gradient_kernel(
    scalars, own, other, own_four, across_four, res, start, gate_factor, up_factor, used_t, gate_out, up_out, down_out, terms
):
    step = pl.program_id(0)

    @pl.when(step == 0)
    def _():
        total = start[...] + back_product(scalars, other, own_four, across_four, 1 - scalars[0])
        terms[:, :CAND_DEV] = (total * gate_factor[...].astype(F32)).astype(BF)
        terms[:, CAND_DEV:] = (total * up_factor[...].astype(F32)).astype(BF)

    for at, grad in enumerate((own, other)):

        @pl.when((step >= 1) & (step < 5) & ((step - 1) // 2 == at))
        def _(grad=grad):
            z = (step - 1) % 2
            rows = [grad_rows_of(scalars, grad, block, z) for block in range(2)]
            rows = jnp.concatenate(rows, axis=1)
            down_out[0] = jnp.dot(used_t[...], rows, preferred_element_type=F32).astype(BF)

    @pl.when(step >= 5)
    def _():
        both = contract(res[jnp.maximum(step - 5, 0)], terms[...], 0, 0).astype(BF)
        gate_out[0] = both[:, :CAND_DEV]
        up_out[0] = both[:, CAND_DEV:]


def gradients(
    scalars, grad_own, grad_other, own_four, across_four, res, start, gate_factor, up_factor, used_t
):
    groups, tok_count, width = res.shape

    def late_pair(i, scalars):
        at = jnp.clip(i - 1, 0, 3)
        return at % 2 * 2 + jnp.where(at < 2, scalars[0], 1 - scalars[0])

    out = jax.ShapeDtypeStruct((1, groups * width, CAND_DEV), BF)
    out_spec = pl.BlockSpec((1, width, CAND_DEV), lambda i, scalars: (0, jnp.maximum(i - 5, 0), 0))
    product = 2 * tok_count * groups * width * CAND_DEV
    return pl.pallas_call(
        gradient_kernel,
        out_shape=[out, out, jax.ShapeDtypeStruct((1, CAND_DEV, groups * width), BF)],
        grid_spec=pltpu.PrefetchScalarGridSpec(
            num_scalar_prefetch=1,
            grid=(5 + groups,),
            in_specs=[VMEM] * 9,
            out_specs=[
                out_spec,
                out_spec,
                pl.BlockSpec(
                    (1, CAND_DEV, 2 * width), lambda i, scalars: (0, 0, late_pair(i, scalars))
                ),
            ],
            scratch_shapes=[pltpu.VMEM((tok_count, 2 * CAND_DEV), BF)],
        ),
        compiler_params=params(28),
        cost_estimate=cost(7 * product // 2, 40 << 20),
        name="gradients",
    )(
        scalars,
        grad_own,
        grad_other,
        own_four,
        across_four,
        res,
        start,
        gate_factor,
        up_factor,
        used_t,
    )


def shards(
    tokens,
    attn_gain,
    ffn_gain,
    w_query,
    w_key,
    w_value,
    w_out,
    w_gate,
    w_up,
    w_down,
    doc_ids,
    widths,
):
    cand_index = lax.axis_index("cand")
    tp_index = lax.axis_index("tp")
    core = (tp_index % 2).astype(jnp.int32)
    cands = lax.axis_size("cand")
    tps = lax.axis_size("tp")
    tok_count, width = tokens.shape
    ff_dev = w_gate.shape[1]
    tok_cand = tok_count // cands
    tok_tp = tok_count // tps
    nothing = jnp.zeros((1,), jnp.int32)

    own_four = lax.all_gather(w_down, "cand", axis=0, axis_index_groups=SAME_Z)
    down_across = lax.ppermute(w_down[:CAND_DEV], "cand", ACROSS_Z)

    heads_dev = w_query.shape[1] // HEAD_DIM
    kv_index = tp_index * heads_dev // (HEADS // KV_HEADS)
    zero = jnp.zeros_like(kv_index)
    q_width = heads_dev * HEAD_DIM
    part, _ = project(
        tokens,
        attn_gain,
        (w_query, w_key, w_value),
        (q_width, HEAD_DIM, HEAD_DIM),
        (zero, kv_index, kv_index),
        60,
        "project_qkv",
    )
    received = exchange(part.reshape(cands, tok_cand, part.shape[1]), "cand")
    received, down_across = lax.optimization_barrier((received, down_across))
    across_four = lax.all_gather(down_across, "cand", axis=0, axis_index_groups=SAME_Z)
    qkv_width = part.shape[1] - LANES
    copies = summed_copies(
        qkv_body, (received,), [whole(received)], nothing, cands, tok_cand, qkv_width, "sum_qkv"
    )
    qkv = exchange(copies, "cand").reshape(tok_count, qkv_width)
    query = qkv[:, :q_width].reshape(tok_count, heads_dev, HEAD_DIM)
    key_rows = qkv[:, q_width : q_width + HEAD_DIM]
    value_rows = qkv[:, q_width + HEAD_DIM :]

    scores = jnp.einsum(
        "qhd,kd->hqk", query, key_rows, preferred_element_type=F32
    ) * HEAD_DIM ** (-0.5)
    position = lax.iota(jnp.int32, tok_count)
    allowed = (position[None, :] <= position[:, None]) & (doc_ids[None, :] == doc_ids[:, None])
    scores = jnp.where(allowed[None], scores, -1e30)
    peak_score = jnp.max(scores, axis=-1, keepdims=True)
    expo = jnp.exp(scores - peak_score)
    weights_bf = (expo / jnp.sum(expo, axis=-1, keepdims=True)).astype(BF)
    attended = jnp.einsum("hqk,kd->qhd", weights_bf, value_rows, preferred_element_type=F32)
    attended = attended.astype(BF).reshape(tok_count, heads_dev * HEAD_DIM)
    out_part = jnp.dot(attended, w_out, preferred_element_type=F32).astype(BF)
    received = exchange(out_part.reshape(tps, tok_tp, width), "tp")
    copies = summed_copies(
        residual_body,
        (received, tokens),
        [
            whole(received),
            pl.BlockSpec((tok_tp, width), lambda i, scalars: (scalars[0], 0)),
        ],
        tp_index.astype(jnp.int32)[None],
        tps,
        tok_tp,
        width,
        "sum_attention",
    )
    residual = exchange(copies, "tp").reshape(tok_count, width)

    residual, own_four = lax.optimization_barrier((residual, own_four))
    own_four = to_vmem(own_four)
    part, scaled_res = project(
        residual, ffn_gain, (w_gate, w_up), (ff_dev, ff_dev), (zero, zero), 16, "project_gate_up"
    )
    tok_half = tok_count // 2
    res_half = lax.dynamic_slice_in_dim(scaled_res, core * tok_half, tok_half, 0)
    res_across = lax.ppermute(res_half, "cand", ACROSS_Z)
    received = exchange(part.reshape(cands, tok_cand, part.shape[1]), "cand")
    received, own_four, res_across = lax.optimization_barrier((received, own_four, res_across))
    payload, minus_hidden = gate_up_sums(core[None], received, scaled_res, res_across)
    sums_rows = tok_cand * SUMS_TILES
    sums_across = lax.ppermute(payload[:sums_rows], "cand", ACROSS_Z)
    minus_hidden_across = lax.ppermute(minus_hidden, "cand", ACROSS_Z)

    live = (widths // tps).astype(jnp.int32)
    own_live = jnp.sum(jnp.where(lax.iota(jnp.int32, widths.shape[0]) == cand_index, live, 0))
    z_index = (cand_index // 4).astype(jnp.int32)
    scalars = jnp.concatenate([core[None], own_live[None], live, z_index[None]])
    minus_hidden, across_four = lax.optimization_barrier((minus_hidden, across_four))
    for_other = dropped_output(scalars, minus_hidden, minus_hidden_across, own_four, True)
    away = lax.ppermute(for_other, "tp", CORE_PAIRS)
    mine = dropped_output(scalars, minus_hidden, minus_hidden_across, own_four, False)
    pair_sum = (mine.astype(F32) + away.astype(F32)).astype(BF)
    pair_sum, sums_across = lax.optimization_barrier((pair_sum, sums_across))
    payload = jnp.concatenate([payload, sums_across], axis=0)
    gathered = lax.all_gather(payload, "cand", axis=0, axis_index_groups=SAME_Z)
    chunk = tok_cand // 2
    parts = pair_sum.reshape(cands * tps // 2, chunk, width)
    received = exchange(parts, ("cand", "tp"), SAME_CORE_ALL)
    copies = sum_error(received.reshape(cands, tps // 2, chunk, width))
    gathered_other = lax.ppermute(gathered, "tp", CORE_PAIRS)
    grad_own = exchange(copies, "tp", SAME_CORE).reshape(2, 4, 2, 4, chunk, width)
    grad_other = lax.ppermute(grad_own, "tp", CORE_PAIRS)

    res = res_order(scalars, gathered, gathered_other, sums_rows, tok_half, width)
    factor = factors(scalars, gathered[:, :sums_rows], gathered[:, -sums_rows:], tok_cand)
    across_four = to_vmem(across_four)
    grad_own, across_four, *factor = lax.optimization_barrier((grad_own, across_four, *factor))
    start = own_back(scalars, grad_own, own_four, across_four)
    return tuple(
        gradients(
            scalars, grad_own, grad_other, own_four, across_four, res, start, *factor
        )
    )


def solution(mesh):
    in_specs = (
        P(None, "cand"),
        P("cand"),
        P("cand"),
        P("cand", "tp"),
        P("cand", None),
        P("cand", None),
        P("tp", "cand"),
        P("cand", "tp"),
        P("cand", "tp"),
        P("tp", "cand"),
        P(),
        P(),
    )
    out_specs = (P("cand", None, "tp"), P("cand", None, "tp"), P("cand", "tp", None))
    return jax.shard_map(shards, mesh=mesh, in_specs=in_specs, out_specs=out_specs, check_vma=False)
```

time: 290 us -> 275 us (0.948)
  waiting for transfers between devices: 109 us -> 73.8 us
  blocking collectives: 67.3 us -> 88.5 us
  Pallas kernels: 50.4 us -> 43.6 us
  starting transfers between devices: 30.7 us -> 36 us
    all_gather x2 -> x3, waiting for transfers between devices: 41.5 us -> 17.5 us  [the longest x1 17.5 us: shards(): gathered = lax.all_gather(payload, 'cand', axis=0, axis_index_groups=SAME_Z)]
    all_to_all x4 -> x3, waiting for transfers between devices: 64.4 us -> 42.7 us  [exchange(): return lax.all_to_all(blocks, axis, 0, 0, axis_index_groups=groups)]
    all_to_all x3 -> x4, blocking collectives: 67.3 us -> 88.5 us  [exchange(): return lax.all_to_all(blocks, axis, 0, 0, axis_index_groups=groups)]
    ppermute x0 -> x2, waiting for transfers between devices: none -> 9.11 us  [the longest x1 5.95 us: shards(): res_across = lax.ppermute(res_half, 'cand', ACROSS_Z)]
    pallas_call x1, Pallas kernels: 5.94 us -> 2.38 us  [own_back(): pl.pallas_call(back_kernel, out_shape=jax.ShapeDtypeStruct((tok_count, CA...]
    pallas_call x3 -> x6, Pallas kernels: 33 us -> 29.8 us  [the longest x1 17 us: gradients(): pl.pallas_call(gradient_kernel, out_shape=[out, out, jax.ShapeDtypeStruct...]
    ppermute x0 -> x2, starting transfers between devices: none -> 3.06 us  [the longest x1 2.98 us: shards(): res_across = lax.ppermute(res_half, 'cand', ACROSS_Z)]
    unnamed x34 -> x32, local copies, waits for them, and re-layouts: 7.44 us -> 10 us
  transfers between devices with their start and end apart: 11 -> 13, of which waited for: 5 -> 7; matrix products, arithmetic and copies ran while one was open for 3% -> 3% of each run, Pallas kernels for 10% -> 8%
where the time goes in v3:
time: 275 us; the launch traced here: 274 us
  blocking collectives  88.5 us (32%)
  waiting for transfers between devices  73.8 us (27%)
  Pallas kernels  43.6 us (16%)
  starting transfers between devices  36 us (13%)
  between operations  14.1 us (5%)
  local copies, waits for them, and re-layouts  11.5 us (4%)
  other arithmetic  4.02 us (1%)
    all_to_all x4, blocking collectives, exchange(): return lax.all_to_all(blocks, axis, 0, 0, axis_index_groups=groups)  88.5 us
    all_to_all x3, waiting for transfers between devices, exchange(): return lax.all_to_all(blocks, axis, 0, 0, axis_index_groups=groups)  42.7 us
    all_to_all x3, starting transfers between devices, exchange(): return lax.all_to_all(blocks, axis, 0, 0, axis_index_groups=groups)  23.1 us
    all_gather x1, waiting for transfers between devices, shards(): gathered = lax.all_gather(payload, 'cand', axis=0, axis_index_groups=SAME_Z)  17.5 us
    pallas_call x1, Pallas kernels, gradients(): pl.pallas_call(gradient_kernel, out_shape=[out, out, jax.ShapeDtypeStruct...  17 us
    unnamed x32, local copies, waits for them, and re-layouts  10 us
    pallas_call x2, Pallas kernels, dropped_output(): pl.pallas_call(functools.partial(dropped_kernel, flip), out_shape=jax.Sha...  8.71 us
    ppermute x1, waiting for transfers between devices, shards(): res_across = lax.ppermute(res_half, 'cand', ACROSS_Z)  5.95 us
  transfers between devices with their start and end apart: 13, of which 7 were waited for; matrix products, arithmetic and copies ran while one was open for 3% of the time, Pallas kernels for 8%

profile of v3, /device:TPU:1, one launch (start us, length us, event | category | flops | bytes accessed | tf_op | source)
XLA Modules:
  0.0 273.9 jit_solution(7760789677449660737)
XLA Ops:
  9.1 4.5 %collective-permute-start = (bf16[768,512]{1,0:T(8,128)(2,1)S(1)}, bf16[768,512]{1,0:T(8,128)(2,1)S(1)}, u32[]{:S(2)}, u32[]{:S(2)}) collective-permute-start(bf16[768,512]{1,0:T(8,128)(2,1)S(1)} %slice.21), channel_id=1, source_target_pairs={{0,64},{16,80},{32,96},{48,112},{64,0},{80,16},{96,32},{112,48},{1... | collective-permute-start | bytes 2359304 | tf_op jit(solution)/shard_map/ppermute | solution.py:490
  14.2 3.3 %project_qkv.1 = (bf16[512,640]{1,0:T(8,128)(2,1)}, bf16[512,512]{1,0:T(8,128)(2,1)}) custom-call(s32[3]{0:T(128)} %pad_add_fusion.1.scalars, bf16[512,512]{1,0:T(8,128)(2,1)} %refs_1_.4, f32[1,512]{1,0:T(1,128)} %bitcast.74, bf16[512,256]{1,0:T(8,128)(2,1)} %refs_0_.2, bf16[512,1024]{1,0:T(8,128)(2,1)} %refs_1_.3, bf16[512,1024]{1,0:T(8,128)(2,1)} %refs_2_.1), custom_call_target="tpu_custom_call" | custom-call | flops 335544320 | bytes 1310720 | tf_op jit(solution)/shard_map/project_qkv/pallas_call | solution.py:77
  17.5 19.5 %all_to_all.35.refs_0_ = bf16[8,64,640]{2,1,0:T(8,128)(2,1)S(1)} all-to-all(bf16[8,64,640]{2,1,0:T(8,128)(2,1)} %bitcast.70), channel_id=1, replica_groups=mesh['cand'=8,'tp'=16] {'cand'}, dimensions={0} | all-to-all | bytes 1310720 | tf_op jit(solution)/shard_map/all_to_all | solution.py:29
  38.9 7.5 %all-to-all-start.1 = ((bf16[8,64,512]{2,1,0:T(8,128)(2,1)}), bf16[8,64,512]{2,1,0:T(8,128)(2,1)S(1)}, u32[]{:S(2)}, u32[]{:S(2)}) async-start(bf16[8,64,512]{2,1,0:T(8,128)(2,1)} %sum_qkv.1), calls=%async_computation.1 | async-start | bytes 1048576 | tf_op jit(solution)/shard_map/all_to_all | solution.py:29
  46.6 14.1 %all-to-all-done.1 = bf16[8,64,512]{2,1,0:T(8,128)(2,1)S(1)} async-done(((bf16[8,64,512]{2,1,0:T(8,128)(2,1)}), bf16[8,64,512]{2,1,0:T(8,128)(2,1)S(1)}, u32[]{:S(2)}, u32[]{:S(2)}) %all-to-all-start.1) | async-done | bytes 524320 | tf_op jit(solution)/shard_map/all_to_all | solution.py:29
  63.3 16.4 %all_to_all.36.refs_0_ = bf16[16,32,512]{2,1,0:T(8,128)(2,1)S(1)} all-to-all(bf16[16,32,512]{2,1,0:T(8,128)(2,1)S(1)} %bitcast.66), channel_id=1, replica_groups=mesh['cand'=8,'tp'=16] {'tp'}, dimensions={0} | all-to-all | bytes 1048576 | tf_op jit(solution)/shard_map/all_to_all | solution.py:29
  79.8 13.5 %all_to_all.37 = bf16[16,32,512]{2,1,0:T(8,128)(2,1)S(1)} all-to-all(bf16[16,32,512]{2,1,0:T(8,128)(2,1)S(1)} %sum_attention.1), channel_id=1, replica_groups=mesh['cand'=8,'tp'=16] {'tp'}, dimensions={0} | all-to-all | bytes 1048576 | tf_op jit(solution)/shard_map/all_to_all | solution.py:29
  93.3 2.1 project_gate_up.1
  96.6 6.3 %all-to-all-start.4 = ((bf16[8,64,1920]{2,1,0:T(8,128)(2,1)}), bf16[8,64,1920]{2,1,0:T(8,128)(2,1)S(1)}, u32[]{:S(2)}, u32[]{:S(2)}) async-start(bf16[8,64,1920]{2,1,0:T(8,128)(2,1)} %bitcast.62), calls=%async_computation.4 | async-start | bytes 3932160 | tf_op jit(solution)/shard_map/all_to_all | solution.py:29
  103.0 3.0 %collective-permute-start.1 = (bf16[256,512]{1,0:T(8,128)(2,1)S(1)}, bf16[256,512]{1,0:T(8,128)(2,1)S(1)}, u32[]{:S(2)}, u32[]{:S(2)}) collective-permute-start(bf16[256,512]{1,0:T(8,128)(2,1)S(1)} %constant_dynamic-slice_fusion), channel_id=1, source_target_pairs={{0,64},{16,80},{32,96},{48,112},{64,0},{80,16},{96,32},{112,48},{1... | collective-permute-start | bytes 786440 | tf_op jit(solution)/shard_map/ppermute | solution.py:552
  110.2 5.9 %collective-permute-done.1.res_across = bf16[256,512]{1,0:T(8,128)(2,1)S(1)} collective-permute-done((bf16[256,512]{1,0:T(8,128)(2,1)S(1)}, bf16[256,512]{1,0:T(8,128)(2,1)S(1)}, u32[]{:S(2)}, u32[]{:S(2)}) %collective-permute-start.1) | collective-permute-done | bytes 262176 | tf_op jit(solution)/shard_map/ppermute | solution.py:552
  116.1 16.7 %all-to-all-done.4.received = bf16[8,64,1920]{2,1,0:T(8,128)(2,1)S(1)} async-done(((bf16[8,64,1920]{2,1,0:T(8,128)(2,1)}), bf16[8,64,1920]{2,1,0:T(8,128)(2,1)S(1)}, u32[]{:S(2)}, u32[]{:S(2)}) %all-to-all-start.4) | async-done | bytes 1966112 | tf_op jit(solution)/shard_map/all_to_all | solution.py:29
  135.5 3.8 %collective-permute-done.2.other = bf16[64,896]{1,0:T(8,128)(2,1)S(1)} collective-permute-done((bf16[64,896]{1,0:T(8,128)(2,1)}, bf16[64,896]{1,0:T(8,128)(2,1)S(1)}, u32[]{:S(2)}, u32[]{:S(2)}) %collective-permute-start.2) | collective-permute-done | bytes 114720 | tf_op jit(solution)/shard_map/ppermute | solution.py:558
  141.4 4.3 %dropped_output.3 = bf16[8,2,4,32,512]{4,3,2,1,0:T(8,128)(2,1)S(1)} custom-call(s32[11]{0:T(128)S(1)} %pad_add_fusion.scalars, bf16[64,896]{1,0:T(8,128)(2,1)} %get-tuple-element.37.own, bf16[64,896]{1,0:T(8,128)(2,1)S(1)} %collective-permute-done.2.other, bf16[4,896,512]{2,1,0:T(8,128)(2,1)S(1)} %copy-done.3), custom_call_target="tpu_custom_call" | custom-call | flops 1879048192 | bytes 3932160 | tf_op jit(solution)/shard_map/dropped_output/pallas_call | solution.py:234
  145.7 2.8 %collective-permute-start.3 = (bf16[8,2,4,32,512]{4,3,2,1,0:T(8,128)(2,1)S(1)}, bf16[8,2,4,32,512]{4,3,2,1,0:T(8,128)(2,1)S(1)}, u32[]{:S(2)}, u32[]{:S(2)}) collective-permute-start(bf16[8,2,4,32,512]{4,3,2,1,0:T(8,128)(2,1)S(1)} %dropped_output.3), channel_id=1, source_target_pairs={{0,1},{1,0},{2,3},{3,2},{4,5},{5,4},{6,7},{7,6},{8,9},{9,8},{10,11... | collective-permute-start | bytes 6291464 | tf_op jit(solution)/shard_map/ppermute | solution.py:566
  148.7 4.4 %dropped_output.2 = bf16[8,2,4,32,512]{4,3,2,1,0:T(8,128)(2,1)S(1)} custom-call(s32[11]{0:T(128)S(1)} %pad_add_fusion.scalars, bf16[64,896]{1,0:T(8,128)(2,1)} %get-tuple-element.37.own, bf16[64,896]{1,0:T(8,128)(2,1)S(1)} %collective-permute-done.2.other, bf16[4,896,512]{2,1,0:T(8,128)(2,1)S(1)} %copy-done.3), custom_call_target="tpu_custom_call" | custom-call | flops 1879048192 | bytes 3932160 | tf_op jit(solution)/shard_map/dropped_output/pallas_call | solution.py:234
  153.9 3.2 %collective-permute-done.4 = bf16[832,128]{1,0:T(8,128)(2,1)S(1)} collective-permute-done((bf16[832,128]{1,0:T(8,128)(2,1)S(1)}, bf16[832,128]{1,0:T(8,128)(2,1)S(1)}, u32[]{:S(2)}, u32[]{:S(2)}) %collective-permute-start.4) | collective-permute-done | bytes 213024 | tf_op jit(solution)/shard_map/ppermute | solution.py:557
  158.1 39.1 %all_to_all.38 = bf16[64,32,512]{2,1,0:T(8,128)(2,1)S(1)} all-to-all(bf16[64,32,512]{2,1,0:T(8,128)(2,1)S(1)} %bitcast.65), channel_id=1, replica_groups={{0,2,4,6,8,10,12,14,16,18,20,22,24,26,28,30,32,34,36,38,40,42,44,46,48,..., dimensions={0} | all-to-all | bytes 4194304 | tf_op jit(solution)/shard_map/all_to_all | solution.py:29
  199.1 9.3 %all-to-all-start.6 = ((bf16[8,8,32,512]{3,2,1,0:T(8,128)(2,1)}), bf16[8,8,32,512]{3,2,1,0:T(8,128)(2,1)S(1)}, u32[]{:S(2)}, u32[]{:S(2)}) async-start(bf16[8,8,32,512]{3,2,1,0:T(8,128)(2,1)} %sum_error.1), calls=%async_computation.6 | async-start | bytes 4194304 | tf_op jit(solution)/shard_map/all_to_all | solution.py:29
  208.4 17.5 %all-gather.11.cloned.1.call-done = bf16[14848,128]{1,0:T(8,128)(2,1)} async-done(((bf16[3712,128]{1,0:T(8,128)(2,1)}), bf16[14848,128]{1,0:T(8,128)(2,1)}) %all-gather.11.cloned.1.call-update) | async-done | bytes 3801104 | tf_op jit(solution)/shard_map/all_gather | solution.py:571
  226.3 11.9 %all-to-all-done.6 = bf16[8,8,32,512]{3,2,1,0:T(8,128)(2,1)S(1)} async-done(((bf16[8,8,32,512]{3,2,1,0:T(8,128)(2,1)}), bf16[8,8,32,512]{3,2,1,0:T(8,128)(2,1)S(1)}, u32[]{:S(2)}, u32[]{:S(2)}) %all-to-all-start.6) | async-done | bytes 2097184 | tf_op jit(solution)/shard_map/all_to_all | solution.py:29
  244.3 2.4 own_back.1.start
  246.7 3.6 %res_order.1.res = bf16[8,512,512]{2,1,0:T(8,128)(2,1)S(1)} custom-call(s32[11]{0:T(128)S(1)} %pad_add_fusion.scalars, bf16[4,3712,128]{2,1,0:T(8,128)(2,1)S(1)} %bitcast.59, bf16[4,3712,128]{2,1,0:T(8,128)(2,1)} %collective-permute-done.6.second), custom_call_target="tpu_custom_call" | custom-call | bytes 11796480 | tf_op jit(solution)/shard_map/res_order/pallas_call | solution.py:380
  250.3 17.0 %gradients.1 = (bf16[1,4096,768]{2,1,0:T(8,128)(2,1)}, bf16[1,4096,768]{2,1,0:T(8,128)(2,1)}, bf16[1,768,4096]{2,1,0:T(8,128)(2,1)}) custom-call(s32[11]{0:T(128)S(1)} %pad_add_fusion.scalars, bf16[2,4,2,4,32,512]{5,4,3,2,1,0:T(8,128)(2,1)S(1)} %bitcast.56, bf16[2,4,2,4,32,512]{5,4,3,2,1,0:T(8,128)(2,1)S(1)} %collective-permute-done.5.other, ...), custom_call_target="tpu_custom_call" | custom-call | flops 11274289152 | bytes 41943040 | tf_op jit(solution)/shard_map/gradients/pallas_call | solution.py:431
  (71 shorter events, 27.8 us)
Async XLA Ops:
  7.2 55.7 %copy-start = (bf16[256,512]{1,0:T(8,128)(2,1)S(1)}, bf16[256,512]{1,0:T(8,128)(2,1)}, u32[]{:S(2)}) copy-start(bf16[256,512]{1,0:T(8,128)(2,1)} %param.18) | copy-start | bytes 786436
  7.2 86.1 %all-gather.7.cloned.1.call-start = ((), (), s32[]{:S(2)}) async-start(), calls=%async_computation.7 | async-start | bytes 4587520 | tf_op jit(solution)/shard_map/all_gather | solution.py:489
  7.9 127.6 %all-gather.9.cloned.1.call-start = ((), (), s32[]{:S(2)}) async-start(), calls=%async_computation.8 | async-start | bytes 3932160 | tf_op jit(solution)/shard_map/all_gather | solution.py:507
  9.1 27.9 %collective-permute-start = (bf16[768,512]{1,0:T(8,128)(2,1)S(1)}, bf16[768,512]{1,0:T(8,128)(2,1)S(1)}, u32[]{:S(2)}, u32[]{:S(2)}) collective-permute-start(bf16[768,512]{1,0:T(8,128)(2,1)S(1)} %slice.21), channel_id=1, source_target_pairs={{0,64},{16,80},{32,96},{48,112},{64,0},{80,16},{96,32},{112,48},{1... | collective-permute-start | bytes 2359304 | tf_op jit(solution)/shard_map/ppermute | solution.py:490
  17.5 28.9 %copy-start.14 = (s32[512]{0:T(512)S(1)}, s32[512]{0:T(512)}, u32[]{:S(2)}) copy-start(s32[512]{0:T(512)} %param.22) | copy-start | bytes 6148
  38.9 21.8 %all-to-all-start.1 = ((bf16[8,64,512]{2,1,0:T(8,128)(2,1)}), bf16[8,64,512]{2,1,0:T(8,128)(2,1)S(1)}, u32[]{:S(2)}, u32[]{:S(2)}) async-start(bf16[8,64,512]{2,1,0:T(8,128)(2,1)} %sum_qkv.1), calls=%async_computation.1 | async-start | bytes 1048576 | tf_op jit(solution)/shard_map/all_to_all | solution.py:29
  62.9 16.8 %copy-start.8 = (bf16[512,512]{1,0:T(8,128)(2,1)S(1)}, bf16[512,512]{1,0:T(8,128)(2,1)}, u32[]{:S(2)}) copy-start(bf16[512,512]{1,0:T(8,128)(2,1)} %refs_1_.4) | copy-start | bytes 1572868
  63.2 30.0 %copy-start.10 = (bf16[512,896]{1,0:T(8,128)(2,1)S(1)}, bf16[512,896]{1,0:T(8,128)(2,1)}, u32[]{:S(2)}) copy-start(bf16[512,896]{1,0:T(8,128)(2,1)} %refs_0_.3) | copy-start | bytes 2752516
  63.3 30.0 %copy-start.11 = (bf16[512,896]{1,0:T(8,128)(2,1)S(1)}, bf16[512,896]{1,0:T(8,128)(2,1)}, u32[]{:S(2)}) copy-start(bf16[512,896]{1,0:T(8,128)(2,1)} %refs_1_.5) | copy-start | bytes 2752516
  63.3 30.0 %copy-start.12 = (f32[512]{0:T(512)S(1)}, f32[512]{0:T(512)}, u32[]{:S(2)}) copy-start(f32[512]{0:T(512)} %param.14) | copy-start | bytes 6148
  96.6 36.2 %all-to-all-start.4 = ((bf16[8,64,1920]{2,1,0:T(8,128)(2,1)}), bf16[8,64,1920]{2,1,0:T(8,128)(2,1)S(1)}, u32[]{:S(2)}, u32[]{:S(2)}) async-start(bf16[8,64,1920]{2,1,0:T(8,128)(2,1)} %bitcast.62), calls=%async_computation.4 | async-start | bytes 3932160 | tf_op jit(solution)/shard_map/all_to_all | solution.py:29
  102.9 123.0 %all-gather.11.cloned.1.call-start = ((), (), s32[]{:S(2)}) async-start(), calls=%async_computation.9 | async-start | bytes 4751360 | tf_op jit(solution)/shard_map/all_gather | solution.py:571
  103.0 13.1 %collective-permute-start.1 = (bf16[256,512]{1,0:T(8,128)(2,1)S(1)}, bf16[256,512]{1,0:T(8,128)(2,1)S(1)}, u32[]{:S(2)}, u32[]{:S(2)}) collective-permute-start(bf16[256,512]{1,0:T(8,128)(2,1)S(1)} %constant_dynamic-slice_fusion), channel_id=1, source_target_pairs={{0,64},{16,80},{32,96},{48,112},{64,0},{80,16},{96,32},{112,48},{1... | collective-permute-start | bytes 786440 | tf_op jit(solution)/shard_map/ppermute | solution.py:552
  110.2 23.9 %copy-start.15 = (s32[8]{0:T(128)S(1)}, s32[8]{0:T(128)}, u32[]{:S(2)}) copy-start(s32[8]{0:T(128)} %param.23) | copy-start | bytes 100
  134.0 5.4 %collective-permute-start.2 = (bf16[64,896]{1,0:T(8,128)(2,1)}, bf16[64,896]{1,0:T(8,128)(2,1)S(1)}, u32[]{:S(2)}, u32[]{:S(2)}) collective-permute-start(bf16[64,896]{1,0:T(8,128)(2,1)} %get-tuple-element.37.own), channel_id=1, source_target_pairs={{0,64},{16,80},{32,96},{48,112},{64,0},{80,16},{96,32},{112,48},{1... | collective-permute-start | bytes 344072 | tf_op jit(solution)/shard_map/ppermute | solution.py:558
  139.4 2.0 copy-start.3
  145.7 7.3 %collective-permute-start.3 = (bf16[8,2,4,32,512]{4,3,2,1,0:T(8,128)(2,1)S(1)}, bf16[8,2,4,32,512]{4,3,2,1,0:T(8,128)(2,1)S(1)}, u32[]{:S(2)}, u32[]{:S(2)}) collective-permute-start(bf16[8,2,4,32,512]{4,3,2,1,0:T(8,128)(2,1)S(1)} %dropped_output.3), channel_id=1, source_target_pairs={{0,1},{1,0},{2,3},{3,2},{4,5},{5,4},{6,7},{7,6},{8,9},{9,8},{10,11... | collective-permute-start | bytes 6291464 | tf_op jit(solution)/shard_map/ppermute | solution.py:566
  148.6 8.5 %collective-permute-start.4 = (bf16[832,128]{1,0:T(8,128)(2,1)S(1)}, bf16[832,128]{1,0:T(8,128)(2,1)S(1)}, u32[]{:S(2)}, u32[]{:S(2)}) collective-permute-start(bf16[832,128]{1,0:T(8,128)(2,1)S(1)} %slice.25), channel_id=1, source_target_pairs={{0,64},{16,80},{32,96},{48,112},{64,0},{80,16},{96,32},{112,48},{1... | collective-permute-start | bytes 638984 | tf_op jit(solution)/shard_map/ppermute | solution.py:557
  199.1 39.1 %all-to-all-start.6 = ((bf16[8,8,32,512]{3,2,1,0:T(8,128)(2,1)}), bf16[8,8,32,512]{3,2,1,0:T(8,128)(2,1)S(1)}, u32[]{:S(2)}, u32[]{:S(2)}) async-start(bf16[8,8,32,512]{3,2,1,0:T(8,128)(2,1)} %sum_error.1), calls=%async_computation.6 | async-start | bytes 4194304 | tf_op jit(solution)/shard_map/all_to_all | solution.py:29
  225.9 20.8 %collective-permute-start.6 = (bf16[4,3712,128]{2,1,0:T(8,128)(2,1)}, bf16[4,3712,128]{2,1,0:T(8,128)(2,1)}, u32[]{:S(2)}, u32[]{:S(2)}) collective-permute-start(bf16[4,3712,128]{2,1,0:T(8,128)(2,1)} %bitcast.57), channel_id=1, source_target_pairs={{0,1},{1,0},{2,3},{3,2},{4,5},{5,4},{6,7},{7,6},{8,9},{9,8},{10,11... | collective-permute-start | bytes 11403272 | tf_op jit(solution)/shard_map/ppermute | solution.py:576
  238.2 4.0 %copy-start.5 = (bf16[14848,128]{1,0:T(8,128)(2,1)S(1)}, bf16[14848,128]{1,0:T(8,128)(2,1)}, u32[]{:S(2)}) copy-start(bf16[14848,128]{1,0:T(8,128)(2,1)} %all-gather.11.cloned.1.call-done) | copy-start | bytes 11403268
  238.2 12.1 %collective-permute-start.5 = (bf16[2,4,2,4,32,512]{5,4,3,2,1,0:T(8,128)(2,1)S(1)}, bf16[2,4,2,4,32,512]{5,4,3,2,1,0:T(8,128)(2,1)S(1)}, u32[]{:S(2)}, u32[]{:S(2)}) collective-permute-start(bf16[2,4,2,4,32,512]{5,4,3,2,1,0:T(8,128)(2,1)S(1)} %bitcast.54), channel_id=1, source_target_pairs={{0,1},{1,0},{2,3},{3,2},{4,5},{5,4},{6,7},{7,6},{8,9},{9,8},{10,11... | collective-permute-start | bytes 6291464 | tf_op jit(solution)/shard_map/ppermute | solution.py:578
  242.3 2.0 copy-start.4
  250.3 17.0 %copy-start.1 = (bf16[256,512]{1,0:T(8,128)(2,1)S(1)}, bf16[256,512]{1,0:T(8,128)(2,1)}, u32[]{:S(2)}) copy-start(bf16[256,512]{1,0:T(8,128)(2,1)} %param.18) | copy-start | bytes 786436
  (5 other events, 7.9 us)
Sparse Core Ops, SparseCore 0:
  9.7 58.6 all-gather.6
  70.6 50.5 all-gather.8
  158.2 67.6 all-gather.10

commit v4 on v3

--- a/solution.py
+++ b/solution.py
@@ -137,7 +137,7 @@
         grid=(blocks.shape[0],),
         in_specs=[pl.BlockSpec((1,) + blocks.shape[1:], lambda i: (i, 0, 0))],
         out_specs=VMEM,
-        compiler_params=params(12),
+        compiler_params=params(8),
         cost_estimate=cost(0, 4 * blocks.size),
         name="to_vmem",
     )(blocks)
@@ -154,108 +154,90 @@
     return (rows[...].astype(F32) + jnp.sum(received[...].astype(F32), axis=0)).astype(BF)
 
 
-def sums_kernel(scalars, received, scaled_res, res_across, payload, minus_hidden):
+def put_tiles(out, parts):
+    at = 0
+    for part in parts:
+        count = part.shape[0]
+        for lane in range(0, part.shape[1], LANES):
+            out[at : at + count, :] = part[:, lane : lane + LANES]
+            at += count
+
+
+def sums_kernel(received, res_half, res_across, res_tiles, sums, minus_hidden):
     ff_dev = minus_hidden.shape[1]
-    rows = received.shape[1]
     total = jnp.sum(received[...].astype(F32), axis=0)
     squares = total[:, 2 * ff_dev : 2 * ff_dev + 1] + total[:, 2 * ff_dev + 1 : 2 * ff_dev + 2]
     scale = lax.rsqrt(squares / D + EPSILON)
     gate = total[:, :ff_dev] * scale
     up = total[:, ff_dev : 2 * ff_dev] * scale
-    minus_hidden[...] = (-(gate * jax.nn.sigmoid(gate) * up)).astype(BF)
-    parts = (gate[:, :CAND_DEV].astype(BF), up[:, :CAND_DEV].astype(BF), lanes_of(scale), scaled_res, res_across)
-    at = 0
-    for part in parts:
-        count = part.shape[0]
-        for lane in range(0, part.shape[1], LANES):
-            payload[at : at + count, :] = part[:, lane : lane + LANES]
-            at += count
-
-
-def gate_up_sums(scalars, received, scaled_res, res_across):
+    hidden = (-(gate * jax.nn.sigmoid(gate) * up)).astype(BF)
+    minus_hidden[...] = hidden
+    slots = [part[:, :CAND_DEV].astype(BF) for part in (gate, up)]
+    put_tiles(sums, slots + [lanes_of(scale), hidden[:, CAND_DEV:]])
+    put_tiles(res_tiles, (res_half, res_across))
+
+
+def gate_up_sums(received, res_half, res_across):
     _, rows, width = received.shape
     ff_dev = (width - LANES) // 2
-    half, depth = scaled_res.shape[0] // 2, scaled_res.shape[1]
-    payload_rows = rows * SUMS_TILES + 2 * half * (depth // LANES)
+    half, depth = res_half.shape
     return pl.pallas_call(
         sums_kernel,
         out_shape=[
-            jax.ShapeDtypeStruct((payload_rows, LANES), BF),
+            jax.ShapeDtypeStruct((2 * half * (depth // LANES), LANES), BF),
+            jax.ShapeDtypeStruct((rows * SUMS_TILES, LANES), BF),
             jax.ShapeDtypeStruct((rows, ff_dev), BF),
         ],
-        grid_spec=pltpu.PrefetchScalarGridSpec(
-            num_scalar_prefetch=1,
-            grid=(1,),
-            in_specs=[
-                whole(received),
-                pl.BlockSpec((half, depth), lambda i, scalars: (scalars[0], 0)),
-                whole(res_across),
-            ],
-            out_specs=[
-                pl.BlockSpec((payload_rows, LANES), lambda i, scalars: (0, 0)),
-                pl.BlockSpec((rows, ff_dev), lambda i, scalars: (0, 0)),
-            ],
-        ),
-        compiler_params=params(20),
+        compiler_params=pltpu.CompilerParams(vmem_limit_bytes=14 << 20),
         cost_estimate=cost(0, 4 * received.size, rows * ff_dev),
         name="gate_up_sums",
-    )(scalars, received, scaled_res, res_across)
+    )(received, res_half, res_across)
 
 
 LIVE_AT, LIVES_AT, Z_AT = 1, 2, 10
-SUMS_TILES = 2 * CAND_DEV // LANES + 1
-
-
-def dropped_kernel(flip, scalars, own, other, down, out, rows):
-    cands, _, chunks, chunk, width = out.shape
-
-    @pl.when(pl.program_id(0) == 0)
-    def _():
-        own_first = scalars[Z_AT] == 0
-        unit = lax.broadcasted_iota(jnp.int32, (chunk, own.shape[1]), 1)
-        for at in range(4):
-            part = slice(at % 2 * chunk, (at % 2 + 1) * chunk)
-            here, there = own[part, :].astype(F32), other[part, :].astype(F32)
-            values = jnp.where(own_first == (at < 2), here, there)
-            for c in range(8):
-                kept = jnp.where(unit >= scalars[LIVES_AT + c], values, 0.0).astype(BF)
-                rows[(c * 4 + at) * chunk : (c * 4 + at + 1) * chunk, :] = kept
-
-    block = 2 * (1 - scalars[0] if flip else scalars[0]) + pl.program_id(0)
-    total = jnp.dot(rows[...], down[block], preferred_element_type=F32)
-    out[:, 0] = total.astype(BF).reshape(cands, chunks, chunk, width)
-
-
-def dropped_output(scalars, own, other, down_four, flip):
-    tok_cand, ff_dev = own.shape
-    width = down_four.shape[2]
-    chunk = tok_cand // 2
-
-    return pl.pallas_call(
-        functools.partial(dropped_kernel, flip),
-        out_shape=jax.ShapeDtypeStruct((8, 2, 4, chunk, width), BF),
-        grid_spec=pltpu.PrefetchScalarGridSpec(
-            num_scalar_prefetch=1,
-            grid=(2,),
-            in_specs=[
-                whole(own),
-                whole(other),
-                VMEM,
-            ],
-            out_specs=pl.BlockSpec(
-                (8, 1, 4, chunk, width), lambda i, scalars: (0, i, 0, 0, 0)
-            ),
-            scratch_shapes=[pltpu.VMEM((32 * chunk, ff_dev), BF)],
-        ),
-        compiler_params=params(20),
-        cost_estimate=cost(4 * 32 * chunk * ff_dev * width, 4 * (ff_dev + 32 * chunk) * width),
-        name="dropped_output",
-    )(scalars, own, other, down_four)
+SUMS_TILES = 2 * CAND_DEV // LANES + 2
 
 
 def tiles_of(block, first, count, rows):
     tiles = [block[..., first + i * rows : first + (i + 1) * rows, :] for i in range(count)]
     return jnp.concatenate([tile.reshape(-1, LANES) for tile in tiles], axis=1)
+
+
+def dropped_kernel(flip, scalars, own, across, down, out, rows):
+    cands, blocks, chunks, chunk, width = out.shape
+    own_first = scalars[Z_AT] == 0
+    unit = lax.broadcasted_iota(jnp.int32, own.shape, 1)
+    count = own.shape[0]
+    tiles = CAND_DEV // LANES
+    gate = tiles_of(across[...], 0, tiles, count).astype(F32)
+    up = tiles_of(across[...], tiles * count, tiles, count).astype(F32)
+    rest = tiles_of(across[...], (2 * tiles + 1) * count, 1, count).astype(F32)
+    here = own[...].astype(F32)
+    there = jnp.concatenate([-(gate * jax.nn.sigmoid(gate) * up), rest], axis=1)
+    for z in range(2):
+        values = jnp.where(own_first == (z == 0), here, there)
+        for c in range(cands):
+            dropped = jnp.where(unit >= scalars[LIVES_AT + c], values, 0.0).astype(BF)
+            rows[(2 * c + z) * count : (2 * c + z + 1) * count, :] = dropped
+    core = 1 - scalars[0] if flip else scalars[0]
+    for i in range(blocks):
+        total = jnp.dot(rows[...], down[blocks * core + i], preferred_element_type=F32)
+        out[:, i] = total.astype(BF).reshape(cands, chunks, chunk, width)
+
+
+def dropped_output(scalars, own, across, down_four, flip):
+    tok_cand, ff_dev = own.shape
+    width = down_four.shape[2]
+    return pl.pallas_call(
+        functools.partial(dropped_kernel, flip),
+        out_shape=jax.ShapeDtypeStruct((8, 2, 4, tok_cand // 2, width), BF),
+        in_specs=[pl.BlockSpec(memory_space=pltpu.SMEM), VMEM, VMEM, VMEM],
+        out_specs=VMEM,
+        scratch_shapes=[pltpu.VMEM((16 * tok_cand, ff_dev), BF)],
+        compiler_params=pltpu.CompilerParams(vmem_limit_bytes=11 << 20),
+        cost_estimate=cost(64 * tok_cand * ff_dev * width, 8 * (ff_dev + 8 * tok_cand) * width),
+        name="dropped_output",
+    )(scalars, own, across, down_four)
 
 
 def factors_kernel(rows, scalars, own_sums, across_sums, gate_factor, up_factor, used_t):
@@ -358,39 +340,28 @@
         out_shape=jax.ShapeDtypeStruct((tok_count, CAND_DEV), F32),
         in_specs=[pl.BlockSpec(memory_space=pltpu.SMEM), VMEM, VMEM, VMEM],
         out_specs=VMEM,
-        compiler_params=pltpu.CompilerParams(vmem_limit_bytes=16 << 20),
+        compiler_params=pltpu.CompilerParams(vmem_limit_bytes=12 << 20),
         cost_estimate=cost(8 * tok_count * width * CAND_DEV, 10 << 20),
         name="own_back",
     )(scalars, grad_own, own_four, across_four)
 
 
-def res_order_kernel(half, first_row, scalars, first, second, out):
-    at = pl.program_id(0)
-    tiles = out.shape[2] // LANES
-    for part in range(2):
-        z = jnp.where(scalars[Z_AT] == 0, part, 1 - part)
-        start = first_row + part * half * tiles
-        for row, ref in ((0, first), (half, second)):
-            out[4 * z + at, row : row + half, :] = tiles_of(ref[0], start, tiles, half)
-
-
-def res_order(scalars, gathered, gathered_other, first_row, half, width):
-    blocks = gathered.shape[0]
-    spec = pl.BlockSpec((1,) + gathered.shape[1:], lambda i, scalars: (i, 0, 0))
-    return pl.pallas_call(
-        functools.partial(res_order_kernel, half, first_row),
-        out_shape=jax.ShapeDtypeStruct((2 * blocks, 2 * half, width), BF),
-        grid_spec=pltpu.PrefetchScalarGridSpec(
-            num_scalar_prefetch=1, grid=(blocks,), in_specs=[spec, spec], out_specs=VMEM
-        ),
-        compiler_params=params(16),
-        cost_estimate=cost(0, 4 * gathered.size + 8 * blocks * half * width),
-        name="res_order",
-    )(scalars, gathered, gathered_other)
-
-
 def gradient_kernel(
-    scalars, own, other, own_four, across_four, res, start, gate_factor, up_factor, used_t, gate_out, up_out, down_out, terms
+    scalars,
+    res_1,
+    res_2,
+    own,
+    other,
+    own_four,
+    across_four,
+    start,
+    gate_factor,
+    up_factor,
+    used_t,
+    gate_out,
+    up_out,
+    down_out,
+    terms,
 ):
     step = pl.program_id(0)
 
@@ -411,22 +382,38 @@
 
     @pl.when(step >= 5)
     def _():
-        both = contract(res[jnp.maximum(step - 5, 0)], terms[...], 0, 0).astype(BF)
+        tok_count, width = terms.shape[0], gate_out.shape[1]
+        half, tiles = tok_count // 2, width // LANES
+        at = pl.multiple_of((step - 5) % 2 * half * tiles, half * tiles)
+        res = [
+            tiles_of(ref[0, pl.ds(at, half * tiles), :], 0, tiles, half) for ref in (res_1, res_2)
+        ]
+        both = contract(jnp.concatenate(res, axis=0), terms[...], 0, 0).astype(BF)
         gate_out[0] = both[:, :CAND_DEV]
         up_out[0] = both[:, CAND_DEV:]
 
 
 def gradients(
-    scalars, grad_own, grad_other, own_four, across_four, res, start, gate_factor, up_factor, used_t
+    scalars, gathered, gathered_other, grad_own, grad_other, own_four, across_four, start, *factor
 ):
-    groups, tok_count, width = res.shape
+    tok_count, width = start.shape[0], own_four.shape[2]
+    groups = 2 * own_four.shape[0]
 
     def late_pair(i, scalars):
         at = jnp.clip(i - 1, 0, 3)
         return at % 2 * 2 + jnp.where(at < 2, scalars[0], 1 - scalars[0])
 
     out = jax.ShapeDtypeStruct((1, groups * width, CAND_DEV), BF)
-    out_spec = pl.BlockSpec((1, width, CAND_DEV), lambda i, scalars: (0, jnp.maximum(i - 5, 0), 0))
+
+    def late(i, scalars):
+        at = jnp.maximum(i - 5, 0)
+        return 4 * ((scalars[Z_AT] + at) % 2) + at // 2
+
+    out_spec = pl.BlockSpec((1, width, CAND_DEV), lambda i, scalars: (0, late(i, scalars), 0))
+    res_spec = pl.BlockSpec(
+        (1, tok_count * width // LANES, LANES),
+        lambda i, scalars: (jnp.maximum(i - 5, 0) // 2, 0, 0),
+    )
     product = 2 * tok_count * groups * width * CAND_DEV
     return pl.pallas_call(
         gradient_kernel,
@@ -434,7 +421,7 @@
         grid_spec=pltpu.PrefetchScalarGridSpec(
             num_scalar_prefetch=1,
             grid=(5 + groups,),
-            in_specs=[VMEM] * 9,
+            in_specs=[res_spec, res_spec] + [VMEM] * 8,
             out_specs=[
                 out_spec,
                 out_spec,
@@ -444,20 +431,19 @@
             ],
             scratch_shapes=[pltpu.VMEM((tok_count, 2 * CAND_DEV), BF)],
         ),
-        compiler_params=params(28),
+        compiler_params=params(20),
         cost_estimate=cost(7 * product // 2, 40 << 20),
         name="gradients",
     )(
         scalars,
+        gathered,
+        gathered_other,
         grad_own,
         grad_other,
         own_four,
         across_four,
-        res,
         start,
-        gate_factor,
-        up_factor,
-        used_t,
+        *factor,
     )
 
 
@@ -486,9 +472,6 @@
     tok_tp = tok_count // tps
     nothing = jnp.zeros((1,), jnp.int32)
 
-    own_four = lax.all_gather(w_down, "cand", axis=0, axis_index_groups=SAME_Z)
-    down_across = lax.ppermute(w_down[:CAND_DEV], "cand", ACROSS_Z)
-
     heads_dev = w_query.shape[1] // HEAD_DIM
     kv_index = tp_index * heads_dev // (HEADS // KV_HEADS)
     zero = jnp.zeros_like(kv_index)
@@ -503,8 +486,9 @@
         "project_qkv",
     )
     received = exchange(part.reshape(cands, tok_cand, part.shape[1]), "cand")
-    received, down_across = lax.optimization_barrier((received, down_across))
-    across_four = lax.all_gather(down_across, "cand", axis=0, axis_index_groups=SAME_Z)
+    received, w_down = lax.optimization_barrier((received, w_down))
+    own_four = lax.all_gather(w_down, "cand", axis=0, axis_index_groups=SAME_Z)
+    down_across = lax.ppermute(w_down[:CAND_DEV], "cand", ACROSS_Z)
     qkv_width = part.shape[1] - LANES
     copies = summed_copies(
         qkv_body, (received,), [whole(received)], nothing, cands, tok_cand, qkv_width, "sum_qkv"
@@ -527,6 +511,7 @@
     attended = attended.astype(BF).reshape(tok_count, heads_dev * HEAD_DIM)
     out_part = jnp.dot(attended, w_out, preferred_element_type=F32).astype(BF)
     received = exchange(out_part.reshape(tps, tok_tp, width), "tp")
+    received, down_across = lax.optimization_barrier((received, down_across))
     copies = summed_copies(
         residual_body,
         (received, tokens),
@@ -548,43 +533,46 @@
         residual, ffn_gain, (w_gate, w_up), (ff_dev, ff_dev), (zero, zero), 16, "project_gate_up"
     )
     tok_half = tok_count // 2
+    scaled_res, down_across = lax.optimization_barrier((scaled_res, down_across))
+    across_four = lax.all_gather(down_across, "cand", axis=0, axis_index_groups=SAME_Z)
     res_half = lax.dynamic_slice_in_dim(scaled_res, core * tok_half, tok_half, 0)
     res_across = lax.ppermute(res_half, "cand", ACROSS_Z)
     received = exchange(part.reshape(cands, tok_cand, part.shape[1]), "cand")
     received, own_four, res_across = lax.optimization_barrier((received, own_four, res_across))
-    payload, minus_hidden = gate_up_sums(core[None], received, scaled_res, res_across)
-    sums_rows = tok_cand * SUMS_TILES
-    sums_across = lax.ppermute(payload[:sums_rows], "cand", ACROSS_Z)
-    minus_hidden_across = lax.ppermute(minus_hidden, "cand", ACROSS_Z)
+    res_tiles, sums, minus_hidden = gate_up_sums(received, res_half, res_across)
+    sums_across = lax.ppermute(sums, "cand", ACROSS_Z)
 
     live = (widths // tps).astype(jnp.int32)
     own_live = jnp.sum(jnp.where(lax.iota(jnp.int32, widths.shape[0]) == cand_index, live, 0))
     z_index = (cand_index // 4).astype(jnp.int32)
     scalars = jnp.concatenate([core[None], own_live[None], live, z_index[None]])
-    minus_hidden, across_four = lax.optimization_barrier((minus_hidden, across_four))
-    for_other = dropped_output(scalars, minus_hidden, minus_hidden_across, own_four, True)
-    away = lax.ppermute(for_other, "tp", CORE_PAIRS)
-    mine = dropped_output(scalars, minus_hidden, minus_hidden_across, own_four, False)
-    pair_sum = (mine.astype(F32) + away.astype(F32)).astype(BF)
-    pair_sum, sums_across = lax.optimization_barrier((pair_sum, sums_across))
-    payload = jnp.concatenate([payload, sums_across], axis=0)
+    sent = dropped_output(scalars, minus_hidden, sums_across, own_four, True)
+    away = lax.ppermute(sent, "tp", CORE_PAIRS)
+    kept = dropped_output(scalars, minus_hidden, sums_across, own_four, False)
+    parts = (kept.astype(F32) + away.astype(F32)).astype(BF)
+    payload = jnp.concatenate([res_tiles, sums, sums_across], axis=0)
+    payload, across_four = lax.optimization_barrier((payload, across_four))
     gathered = lax.all_gather(payload, "cand", axis=0, axis_index_groups=SAME_Z)
     chunk = tok_cand // 2
-    parts = pair_sum.reshape(cands * tps // 2, chunk, width)
+    parts = parts.reshape(cands * tps // 2, chunk, width)
     received = exchange(parts, ("cand", "tp"), SAME_CORE_ALL)
     copies = sum_error(received.reshape(cands, tps // 2, chunk, width))
     gathered_other = lax.ppermute(gathered, "tp", CORE_PAIRS)
     grad_own = exchange(copies, "tp", SAME_CORE).reshape(2, 4, 2, 4, chunk, width)
-    grad_other = lax.ppermute(grad_own, "tp", CORE_PAIRS)
-
-    res = res_order(scalars, gathered, gathered_other, sums_rows, tok_half, width)
-    factor = factors(scalars, gathered[:, :sums_rows], gathered[:, -sums_rows:], tok_cand)
+
+    factor = factors(
+        scalars,
+        gathered[:, -2 * sums.shape[0] : -sums.shape[0]],
+        gathered[:, -sums.shape[0] :],
+        tok_cand,
+    )
     across_four = to_vmem(across_four)
     grad_own, across_four, *factor = lax.optimization_barrier((grad_own, across_four, *factor))
+    grad_other = lax.ppermute(grad_own, "tp", CORE_PAIRS)
     start = own_back(scalars, grad_own, own_four, across_four)
     return tuple(
         gradients(
-            scalars, grad_own, grad_other, own_four, across_four, res, start, *factor
+            scalars, gathered, gathered_other, grad_own, grad_other, own_four, across_four, start, *factor
         )
     )
 

time: 275 us -> 269 us (0.978)
  blocking collectives: 88.5 us -> 76.3 us
  local copies, waits for them, and re-layouts: 11.5 us -> 18.8 us
  waiting for transfers between devices: 73.8 us -> 79.4 us
  starting transfers between devices: 36 us -> 31.8 us
  Pallas kernels: 43.6 us -> 40.8 us
    all_to_all x4 -> x3, blocking collectives: 88.5 us -> 76.3 us  [exchange(): return lax.all_to_all(blocks, axis, 0, 0, axis_index_groups=groups)]
    all_gather x1, waiting for transfers between devices: 17.5 us -> 9.33 us  [shards(): gathered = lax.all_gather(payload, 'cand', axis=0, axis_index_groups=SAME_Z)]
    ppermute x1, waiting for transfers between devices: 5.95 us -> 12.5 us  [shards(): res_across = lax.ppermute(res_half, 'cand', ACROSS_Z)]
    unnamed x32 -> x48, local copies, waits for them, and re-layouts: 10 us -> 16.1 us
    all_gather x1, waiting for transfers between devices: 0.01 us -> 6.03 us  [shards(): lax.all_gather(down_across, 'cand', axis=0, axis_index_groups=SAME_Z)]
    pallas_call x2 -> x1, Pallas kernels: 4.73 us -> 0.51 us  [gate_up_sums(): pl.pallas_call(sums_kernel, out_shape=[jax.ShapeDtypeStruct((2 * half * (...]
    ppermute x1, waiting for transfers between devices: 0.01 us -> 3.81 us  [shards(): down_across = lax.ppermute(w_down[:CAND_DEV], 'cand', ACROSS_Z)]
    pallas_call x1, Pallas kernels: 17 us -> 20.2 us  [gradients(): pl.pallas_call(gradient_kernel, out_shape=[out, out, jax.ShapeDtypeStruct...]
  transfers between devices with their start and end apart: 13 -> 13, of which waited for: 7 -> 10; matrix products, arithmetic and copies ran while one was open for 3% -> 3% of each run, Pallas kernels for 8% -> 6%
where the time goes in v4:
time: 269 us; the launch traced here: 268 us
  waiting for transfers between devices  79.4 us (30%)
  blocking collectives  76.3 us (28%)
  Pallas kernels  40.8 us (15%)
  starting transfers between devices  31.8 us (12%)
  local copies, waits for them, and re-layouts  18.8 us (7%)
  between operations  14.1 us (5%)
  other arithmetic  4.11 us (2%)
  matrix products  3.15 us (1%)
    all_to_all x3, blocking collectives, exchange(): return lax.all_to_all(blocks, axis, 0, 0, axis_index_groups=groups)  76.3 us
    all_to_all x4, waiting for transfers between devices, exchange(): return lax.all_to_all(blocks, axis, 0, 0, axis_index_groups=groups)  41.8 us
    all_to_all x4, starting transfers between devices, exchange(): return lax.all_to_all(blocks, axis, 0, 0, axis_index_groups=groups)  21.4 us
    pallas_call x1, Pallas kernels, gradients(): pl.pallas_call(gradient_kernel, out_shape=[out, out, jax.ShapeDtypeStruct...  20.2 us
    unnamed x48, local copies, waits for them, and re-layouts  16.1 us
    ppermute x1, waiting for transfers between devices, shards(): res_across = lax.ppermute(res_half, 'cand', ACROSS_Z)  12.5 us
    all_gather x1, waiting for transfers between devices, shards(): gathered = lax.all_gather(payload, 'cand', axis=0, axis_index_groups=SAME_Z)  9.33 us
    all_gather x1, waiting for transfers between devices, shards(): lax.all_gather(down_across, 'cand', axis=0, axis_index_groups=SAME_Z)  6.03 us
  transfers between devices with their start and end apart: 13, of which 10 were waited for; matrix products, arithmetic and copies ran while one was open for 3% of the time, Pallas kernels for 6%

profile of v4, /device:TPU:1, one launch (start us, length us, event | category | flops | bytes accessed | tf_op | source)
XLA Modules:
  0.0 268.4 jit_solution(12762030072832423236)
XLA Ops:
  7.9 3.3 %project_qkv.1 = (bf16[512,640]{1,0:T(8,128)(2,1)}, bf16[512,512]{1,0:T(8,128)(2,1)}) custom-call(s32[3]{0:T(128)} %pad_add_fusion.1.scalars, bf16[512,512]{1,0:T(8,128)(2,1)} %refs_1_.4, f32[1,512]{1,0:T(1,128)} %bitcast.70, bf16[512,256]{1,0:T(8,128)(2,1)} %refs_0_.2, bf16[512,1024]{1,0:T(8,128)(2,1)} %refs_1_.3, bf16[512,1024]{1,0:T(8,128)(2,1)} %refs_2_.1), custom_call_target="tpu_custom_call" | custom-call | flops 335544320 | bytes 1310720 | tf_op jit(solution)/shard_map/project_qkv/pallas_call | solution.py:77
  11.2 20.8 %all_to_all.35.refs_0_ = bf16[8,64,640]{2,1,0:T(8,128)(2,1)S(1)} all-to-all(bf16[8,64,640]{2,1,0:T(8,128)(2,1)} %bitcast.66), channel_id=1, replica_groups=mesh['cand'=8,'tp'=16] {'cand'}, dimensions={0} | all-to-all | bytes 1310720 | tf_op jit(solution)/shard_map/all_to_all | solution.py:29
  33.0 3.5 %all-to-all-start.1 = ((bf16[8,64,512]{2,1,0:T(8,128)(2,1)}), bf16[8,64,512]{2,1,0:T(8,128)(2,1)S(1)}, u32[]{:S(2)}, u32[]{:S(2)}) async-start(bf16[8,64,512]{2,1,0:T(8,128)(2,1)} %sum_qkv.1), calls=%async_computation.1 | async-start | bytes 1048576 | tf_op jit(solution)/shard_map/all_to_all | solution.py:29
  37.7 2.9 %collective-permute-start = (bf16[768,512]{1,0:T(8,128)(2,1)}, bf16[768,512]{1,0:T(8,128)(2,1)S(1)}, u32[]{:S(2)}, u32[]{:S(2)}) collective-permute-start(bf16[768,512]{1,0:T(8,128)(2,1)} %slice.21), channel_id=1, source_target_pairs={{0,64},{16,80},{32,96},{48,112},{64,0},{80,16},{96,32},{112,48},{1... | collective-permute-start | bytes 2359304 | tf_op jit(solution)/shard_map/ppermute | solution.py:491
  40.5 7.3 %all-to-all-done.1 = bf16[8,64,512]{2,1,0:T(8,128)(2,1)S(1)} async-done(((bf16[8,64,512]{2,1,0:T(8,128)(2,1)}), bf16[8,64,512]{2,1,0:T(8,128)(2,1)S(1)}, u32[]{:S(2)}, u32[]{:S(2)}) %all-to-all-start.1) | async-done | bytes 524320 | tf_op jit(solution)/shard_map/all_to_all | solution.py:29
  51.2 7.7 %all-to-all-start.2 = ((bf16[16,32,512]{2,1,0:T(8,128)(2,1)}), bf16[16,32,512]{2,1,0:T(8,128)(2,1)S(1)}, u32[]{:S(2)}, u32[]{:S(2)}) async-start(bf16[16,32,512]{2,1,0:T(8,128)(2,1)} %bitcast.14), calls=%async_computation.2 | async-start | bytes 1048576 | tf_op jit(solution)/shard_map/all_to_all | solution.py:29
  58.9 3.8 %collective-permute-done = bf16[768,512]{1,0:T(8,128)(2,1)S(1)} collective-permute-done((bf16[768,512]{1,0:T(8,128)(2,1)}, bf16[768,512]{1,0:T(8,128)(2,1)S(1)}, u32[]{:S(2)}, u32[]{:S(2)}) %collective-permute-start) | collective-permute-done | bytes 786464 | tf_op jit(solution)/shard_map/ppermute | solution.py:491
  62.7 5.8 %all-to-all-done.2.refs_0_ = bf16[16,32,512]{2,1,0:T(8,128)(2,1)S(1)} async-done(((bf16[16,32,512]{2,1,0:T(8,128)(2,1)}), bf16[16,32,512]{2,1,0:T(8,128)(2,1)S(1)}, u32[]{:S(2)}, u32[]{:S(2)}) %all-to-all-start.2) | async-done | bytes 524320 | tf_op jit(solution)/shard_map/all_to_all | solution.py:29
  68.6 14.9 %all_to_all.36 = bf16[16,32,512]{2,1,0:T(8,128)(2,1)S(1)} all-to-all(bf16[16,32,512]{2,1,0:T(8,128)(2,1)S(1)} %sum_attention.1), channel_id=1, replica_groups=mesh['cand'=8,'tp'=16] {'tp'}, dimensions={0} | all-to-all | bytes 1048576 | tf_op jit(solution)/shard_map/all_to_all | solution.py:29
  88.0 4.6 %all-to-all-start.4 = ((bf16[8,64,1920]{2,1,0:T(8,128)(2,1)}), bf16[8,64,1920]{2,1,0:T(8,128)(2,1)S(1)}, u32[]{:S(2)}, u32[]{:S(2)}) async-start(bf16[8,64,1920]{2,1,0:T(8,128)(2,1)} %bitcast.56), calls=%async_computation.4 | async-start | bytes 3932160 | tf_op jit(solution)/shard_map/all_to_all | solution.py:29
  92.7 3.0 %collective-permute-start.1 = (bf16[256,512]{1,0:T(8,128)(2,1)S(1)}, bf16[256,512]{1,0:T(8,128)(2,1)S(1)}, u32[]{:S(2)}, u32[]{:S(2)}) collective-permute-start(bf16[256,512]{1,0:T(8,128)(2,1)S(1)} %constant_dynamic-slice_fusion.res_half), channel_id=1, source_target_pairs={{0,64},{16,80},{32,96},{48,112},{64,0},{80,16},{96,32},{112,48},{1... | collective-permute-start | bytes 786440 | tf_op jit(solution)/shard_map/ppermute | solution.py:539
  95.7 2.3 copy-done.6
  100.0 12.5 %collective-permute-done.1.res_across = bf16[256,512]{1,0:T(8,128)(2,1)S(1)} collective-permute-done((bf16[256,512]{1,0:T(8,128)(2,1)S(1)}, bf16[256,512]{1,0:T(8,128)(2,1)S(1)}, u32[]{:S(2)}, u32[]{:S(2)}) %collective-permute-start.1) | collective-permute-done | bytes 262176 | tf_op jit(solution)/shard_map/ppermute | solution.py:539
  112.6 16.7 %all-to-all-done.4.received = bf16[8,64,1920]{2,1,0:T(8,128)(2,1)S(1)} async-done(((bf16[8,64,1920]{2,1,0:T(8,128)(2,1)}), bf16[8,64,1920]{2,1,0:T(8,128)(2,1)S(1)}, u32[]{:S(2)}, u32[]{:S(2)}) %all-to-all-start.4) | async-done | bytes 1966112 | tf_op jit(solution)/shard_map/all_to_all | solution.py:29
  131.3 5.0 %collective-permute-done.2.across = bf16[896,128]{1,0:T(8,128)(2,1)S(1)} collective-permute-done((bf16[896,128]{1,0:T(8,128)(2,1)S(1)}, bf16[896,128]{1,0:T(8,128)(2,1)S(1)}, u32[]{:S(2)}, u32[]{:S(2)}) %collective-permute-start.2) | collective-permute-done | bytes 229408 | tf_op jit(solution)/shard_map/ppermute | solution.py:543
  137.3 6.0 %all-gather.9.cloned.1.call-done = bf16[3072,512]{1,0:T(8,128)(2,1)} async-done(((bf16[768,512]{1,0:T(8,128)(2,1)}), bf16[3072,512]{1,0:T(8,128)(2,1)}) %all-gather.9.cloned.1.call-update) | async-done | bytes 3145744 | tf_op jit(solution)/shard_map/all_gather | solution.py:537
  146.8 2.9 %dropped_output.3 = bf16[8,2,4,32,512]{4,3,2,1,0:T(8,128)(2,1)S(1)} custom-call(s32[11]{0:T(128)S(1)} %pad_add_fusion.scalars, bf16[64,896]{1,0:T(8,128)(2,1)S(1)} %get-tuple-element.46.own, bf16[896,128]{1,0:T(8,128)(2,1)S(1)} %collective-permute-done.2.across, bf16[4,896,512]{2,1,0:T(8,128)(2,1)S(1)} %copy-done.3), custom_call_target="tpu_custom_call" | custom-call | flops 1879048192 | bytes 5767168 | tf_op jit(solution)/shard_map/dropped_output/pallas_call | solution.py:231
  150.2 2.9 %dropped_output.2 = bf16[8,2,4,32,512]{4,3,2,1,0:T(8,128)(2,1)S(1)} custom-call(s32[11]{0:T(128)S(1)} %pad_add_fusion.scalars, bf16[64,896]{1,0:T(8,128)(2,1)S(1)} %get-tuple-element.46.own, bf16[896,128]{1,0:T(8,128)(2,1)S(1)} %collective-permute-done.2.across, bf16[4,896,512]{2,1,0:T(8,128)(2,1)S(1)} %copy-done.3), custom_call_target="tpu_custom_call" | custom-call | flops 1879048192 | bytes 5767168 | tf_op jit(solution)/shard_map/dropped_output/pallas_call | solution.py:231
  155.0 40.6 %all_to_all.37 = bf16[64,32,512]{2,1,0:T(8,128)(2,1)S(1)} all-to-all(bf16[64,32,512]{2,1,0:T(8,128)(2,1)S(1)} %bitcast.62), channel_id=1, replica_groups={{0,2,4,6,8,10,12,14,16,18,20,22,24,26,28,30,32,34,36,38,40,42,44,46,48,..., dimensions={0} | all-to-all | bytes 4194304 | tf_op jit(solution)/shard_map/all_to_all | solution.py:29
  197.5 5.6 %all-to-all-start.6 = ((bf16[8,8,32,512]{3,2,1,0:T(8,128)(2,1)}), bf16[8,8,32,512]{3,2,1,0:T(8,128)(2,1)}, u32[]{:S(2)}, u32[]{:S(2)}) async-start(bf16[8,8,32,512]{3,2,1,0:T(8,128)(2,1)} %sum_error.1), calls=%async_computation.6 | async-start | bytes 4194304 | tf_op jit(solution)/shard_map/all_to_all | solution.py:29
  203.1 9.3 %all-gather.11.cloned.1.call-done = bf16[15360,128]{1,0:T(8,128)(2,1)} async-done(((bf16[3840,128]{1,0:T(8,128)(2,1)}), bf16[15360,128]{1,0:T(8,128)(2,1)}) %all-gather.11.cloned.1.call-update) | async-done | bytes 3932176 | tf_op jit(solution)/shard_map/all_gather | solution.py:555
  221.4 12.0 %all-to-all-done.6 = bf16[8,8,32,512]{3,2,1,0:T(8,128)(2,1)} async-done(((bf16[8,8,32,512]{3,2,1,0:T(8,128)(2,1)}), bf16[8,8,32,512]{3,2,1,0:T(8,128)(2,1)}, u32[]{:S(2)}, u32[]{:S(2)}) %all-to-all-start.6) | async-done | bytes 2097184 | tf_op jit(solution)/shard_map/all_to_all | solution.py:29
  237.2 3.6 %own_back.1.start = f32[512,768]{1,0:T(8,128)S(1)} custom-call(s32[11]{0:T(128)S(1)} %pad_add_fusion.scalars, bf16[2,4,2,4,32,512]{5,4,3,2,1,0:T(8,128)(2,1)} %bitcast.23.grad.own, bf16[4,896,512]{2,1,0:T(8,128)(2,1)S(1)} %copy-done.4, bf16[4,768,512]{2,1,0:T(8,128)(2,1)S(1)} %to_vmem.3.across_four), custom_call_target="tpu_custom_call" | custom-call | flops 1610612736 | bytes 10485760 | tf_op jit(solution)/shard_map/own_back/pallas_call | solution.py:338
  241.7 20.2 %gradients.1 = (bf16[1,4096,768]{2,1,0:T(8,128)(2,1)}, bf16[1,4096,768]{2,1,0:T(8,128)(2,1)}, bf16[1,768,4096]{2,1,0:T(8,128)(2,1)}) custom-call(s32[11]{0:T(128)S(1)} %pad_add_fusion.scalars, bf16[4,3840,128]{2,1,0:T(8,128)(2,1)S(1)} %bitcast.59, bf16[4,3840,128]{2,1,0:T(8,128)(2,1)} %collective-permute-done.3.res_2, ...), custom_call_target="tpu_custom_call" | custom-call | flops 11274289152 | bytes 41943040 | tf_op jit(solution)/shard_map/gradients/pallas_call | solution.py:418
  (84 shorter events, 37.2 us)
Async XLA Ops:
  7.2 42.9 %copy-start = (bf16[256,512]{1,0:T(8,128)(2,1)S(1)}, bf16[256,512]{1,0:T(8,128)(2,1)}, u32[]{:S(2)}) copy-start(bf16[256,512]{1,0:T(8,128)(2,1)} %param.18) | copy-start | bytes 786436
  7.2 76.3 %all-gather.7.cloned.1.call-start = ((), (), s32[]{:S(2)}) async-start(), calls=%async_computation.7 | async-start | bytes 4587520 | tf_op jit(solution)/shard_map/all_gather | solution.py:490
  11.2 25.4 %copy-start.22 = (s32[512]{0:T(512)S(1)}, s32[512]{0:T(512)}, u32[]{:S(2)}) copy-start(s32[512]{0:T(512)} %param.22) | copy-start | bytes 6148
  11.2 25.6 %copy-start.20 = (bf16[896,512]{1,0:T(8,128)(2,1)S(1)}, bf16[896,512]{1,0:T(8,128)(2,1)}, u32[]{:S(2)}) copy-start(bf16[896,512]{1,0:T(8,128)(2,1)} %param.21) | copy-start | bytes 2752516
  33.0 14.8 %all-to-all-start.1 = ((bf16[8,64,512]{2,1,0:T(8,128)(2,1)}), bf16[8,64,512]{2,1,0:T(8,128)(2,1)S(1)}, u32[]{:S(2)}, u32[]{:S(2)}) async-start(bf16[8,64,512]{2,1,0:T(8,128)(2,1)} %sum_qkv.1), calls=%async_computation.1 | async-start | bytes 1048576 | tf_op jit(solution)/shard_map/all_to_all | solution.py:29
  37.7 25.1 %collective-permute-start = (bf16[768,512]{1,0:T(8,128)(2,1)}, bf16[768,512]{1,0:T(8,128)(2,1)S(1)}, u32[]{:S(2)}, u32[]{:S(2)}) collective-permute-start(bf16[768,512]{1,0:T(8,128)(2,1)} %slice.21), channel_id=1, source_target_pairs={{0,64},{16,80},{32,96},{48,112},{64,0},{80,16},{96,32},{112,48},{1... | collective-permute-start | bytes 2359304 | tf_op jit(solution)/shard_map/ppermute | solution.py:491
  50.0 18.5 %copy-start.8 = (bf16[512,512]{1,0:T(8,128)(2,1)S(1)}, bf16[512,512]{1,0:T(8,128)(2,1)}, u32[]{:S(2)}) copy-start(bf16[512,512]{1,0:T(8,128)(2,1)} %refs_1_.4) | copy-start | bytes 1572868
  51.2 32.3 %copy-start.11 = (bf16[512,896]{1,0:T(8,128)(2,1)S(1)}, bf16[512,896]{1,0:T(8,128)(2,1)}, u32[]{:S(2)}) copy-start(bf16[512,896]{1,0:T(8,128)(2,1)} %refs_0_.3) | copy-start | bytes 2752516
  51.2 32.3 %copy-start.19 = (f32[512]{0:T(512)S(1)}, f32[512]{0:T(512)}, u32[]{:S(2)}) copy-start(f32[512]{0:T(512)} %param.14) | copy-start | bytes 6148
  51.2 17.4 %all-to-all-start.2 = ((bf16[16,32,512]{2,1,0:T(8,128)(2,1)}), bf16[16,32,512]{2,1,0:T(8,128)(2,1)S(1)}, u32[]{:S(2)}, u32[]{:S(2)}) async-start(bf16[16,32,512]{2,1,0:T(8,128)(2,1)} %bitcast.14), calls=%async_computation.2 | async-start | bytes 1048576 | tf_op jit(solution)/shard_map/all_to_all | solution.py:29
  58.9 84.5 %all-gather.9.cloned.1.call-start = ((), (), s32[]{:S(2)}) async-start(), calls=%async_computation.8 | async-start | bytes 3932160 | tf_op jit(solution)/shard_map/all_gather | solution.py:537
  62.7 24.0 %copy-start.21 = (bf16[768,512]{1,0:T(8,128)(2,1)}, bf16[768,512]{1,0:T(8,128)(2,1)S(1)}, u32[]{:S(2)}) copy-start(bf16[768,512]{1,0:T(8,128)(2,1)S(1)} %collective-permute-done) | copy-start | bytes 2359300
  88.0 41.3 %all-to-all-start.4 = ((bf16[8,64,1920]{2,1,0:T(8,128)(2,1)}), bf16[8,64,1920]{2,1,0:T(8,128)(2,1)S(1)}, u32[]{:S(2)}, u32[]{:S(2)}) async-start(bf16[8,64,1920]{2,1,0:T(8,128)(2,1)} %bitcast.56), calls=%async_computation.4 | async-start | bytes 3932160 | tf_op jit(solution)/shard_map/all_to_all | solution.py:29
  92.6 119.8 %all-gather.11.cloned.1.call-start = ((), (), s32[]{:S(2)}) async-start(), calls=%async_computation.9 | async-start | bytes 4915200 | tf_op jit(solution)/shard_map/all_gather | solution.py:555
  92.7 19.9 %collective-permute-start.1 = (bf16[256,512]{1,0:T(8,128)(2,1)S(1)}, bf16[256,512]{1,0:T(8,128)(2,1)S(1)}, u32[]{:S(2)}, u32[]{:S(2)}) collective-permute-start(bf16[256,512]{1,0:T(8,128)(2,1)S(1)} %constant_dynamic-slice_fusion.res_half), channel_id=1, source_target_pairs={{0,64},{16,80},{32,96},{48,112},{64,0},{80,16},{96,32},{112,48},{1... | collective-permute-start | bytes 786440 | tf_op jit(solution)/shard_map/ppermute | solution.py:539
  129.8 13.6 %copy-start.23 = (s32[8]{0:T(128)S(1)}, s32[8]{0:T(128)}, u32[]{:S(2)}) copy-start(s32[8]{0:T(128)} %param.23) | copy-start | bytes 100
  129.9 6.5 %collective-permute-start.2 = (bf16[896,128]{1,0:T(8,128)(2,1)S(1)}, bf16[896,128]{1,0:T(8,128)(2,1)S(1)}, u32[]{:S(2)}, u32[]{:S(2)}) collective-permute-start(bf16[896,128]{1,0:T(8,128)(2,1)S(1)} %get-tuple-element.43), channel_id=1, source_target_pairs={{0,64},{16,80},{32,96},{48,112},{64,0},{80,16},{96,32},{112,48},{1... | collective-permute-start | bytes 688136 | tf_op jit(solution)/shard_map/ppermute | solution.py:543
  149.7 4.3 %collective-permute-start.4 = (bf16[8,2,4,32,512]{4,3,2,1,0:T(8,128)(2,1)S(1)}, bf16[8,2,4,32,512]{4,3,2,1,0:T(8,128)(2,1)S(1)}, u32[]{:S(2)}, u32[]{:S(2)}) collective-permute-start(bf16[8,2,4,32,512]{4,3,2,1,0:T(8,128)(2,1)S(1)} %dropped_output.3), channel_id=1, source_target_pairs={{0,1},{1,0},{2,3},{3,2},{4,5},{5,4},{6,7},{7,6},{8,9},{9,8},{10,11... | collective-permute-start | bytes 6291464 | tf_op jit(solution)/shard_map/ppermute | solution.py:550
  197.5 36.0 %all-to-all-start.6 = ((bf16[8,8,32,512]{3,2,1,0:T(8,128)(2,1)}), bf16[8,8,32,512]{3,2,1,0:T(8,128)(2,1)}, u32[]{:S(2)}, u32[]{:S(2)}) async-start(bf16[8,8,32,512]{3,2,1,0:T(8,128)(2,1)} %sum_error.1), calls=%async_computation.6 | async-start | bytes 4194304 | tf_op jit(solution)/shard_map/all_to_all | solution.py:29
  212.4 28.4 %collective-permute-start.3 = (bf16[4,3840,128]{2,1,0:T(8,128)(2,1)}, bf16[4,3840,128]{2,1,0:T(8,128)(2,1)}, u32[]{:S(2)}, u32[]{:S(2)}) collective-permute-start(bf16[4,3840,128]{2,1,0:T(8,128)(2,1)} %bitcast.57), channel_id=1, source_target_pairs={{0,1},{1,0},{2,3},{3,2},{4,5},{5,4},{6,7},{7,6},{8,9},{9,8},{10,11... | collective-permute-start | bytes 11796488 | tf_op jit(solution)/shard_map/ppermute | solution.py:560
  233.5 7.3 %collective-permute-start.5 = (bf16[2,4,2,4,32,512]{5,4,3,2,1,0:T(8,128)(2,1)}, bf16[2,4,2,4,32,512]{5,4,3,2,1,0:T(8,128)(2,1)S(1)}, u32[]{:S(2)}, u32[]{:S(2)}) collective-permute-start(bf16[2,4,2,4,32,512]{5,4,3,2,1,0:T(8,128)(2,1)} %bitcast.23.grad.own), channel_id=1, source_target_pairs={{0,1},{1,0},{2,3},{3,2},{4,5},{5,4},{6,7},{7,6},{8,9},{9,8},{10,11... | collective-permute-start | bytes 6291464 | tf_op jit(solution)/shard_map/ppermute | solution.py:571
  237.2 4.2 %copy-start.16 = (bf16[512,768]{1,0:T(8,128)(2,1)S(1)}, bf16[512,768]{1,0:T(8,128)(2,1)}, u32[]{:S(2)}) copy-start(bf16[512,768]{1,0:T(8,128)(2,1)} %copy-done.15) | copy-start | bytes 2359300
  237.2 4.4 %copy-start.18 = (bf16[768,512]{1,0:T(8,128)(2,1)S(1)}, bf16[768,512]{1,0:T(8,128)(2,1)}, u32[]{:S(2)}) copy-start(bf16[768,512]{1,0:T(8,128)(2,1)} %copy-done.17) | copy-start | bytes 2359300
  241.6 20.2 %copy-start.1 = (bf16[256,512]{1,0:T(8,128)(2,1)S(1)}, bf16[256,512]{1,0:T(8,128)(2,1)}, u32[]{:S(2)}) copy-start(bf16[256,512]{1,0:T(8,128)(2,1)} %param.18) | copy-start | bytes 786436
  (13 other events, 26.7 us)
Sparse Core Ops, SparseCore 0:
  32.1 43.8 all-gather.6
  88.1 55.1 all-gather.8
  145.6 66.7 all-gather.10

commit v5 on v4

--- a/solution.py
+++ b/solution.py
@@ -318,18 +318,18 @@
     return jnp.concatenate(rows, axis=0)
 
 
-def back_product(scalars, grad, own_four, across_four, core):
+def back_product(scalars, grad, own_two, across_two):
     total = None
-    for z, down in ((scalars[Z_AT], own_four), (1 - scalars[Z_AT], across_four)):
+    for z, down in ((scalars[Z_AT], own_two), (1 - scalars[Z_AT], across_two)):
         rows = [grad_rows_of(scalars, grad, block, z) for block in range(2)]
-        units = [down[2 * core + block, :CAND_DEV] for block in range(2)]
+        units = [down[block] for block in range(2)]
         product = contract(jnp.concatenate(rows, axis=1), jnp.concatenate(units, axis=1), 1, 1)
         total = product if total is None else total + product
     return total
 
 
 def back_kernel(scalars, grad, own_four, across_four, out):
-    out[...] = back_product(scalars, grad, own_four, across_four, scalars[0])
+    out[...] = back_product(scalars, grad, own_four, across_four)
 
 
 def own_back(scalars, grad_own, own_four, across_four):
@@ -367,7 +367,7 @@
 
     @pl.when(step == 0)
     def _():
-        total = start[...] + back_product(scalars, other, own_four, across_four, 1 - scalars[0])
+        total = start[...] + back_product(scalars, other, own_four, across_four)
         terms[:, :CAND_DEV] = (total * gate_factor[...].astype(F32)).astype(BF)
         terms[:, CAND_DEV:] = (total * up_factor[...].astype(F32)).astype(BF)
 
@@ -397,7 +397,7 @@
     scalars, gathered, gathered_other, grad_own, grad_other, own_four, across_four, start, *factor
 ):
     tok_count, width = start.shape[0], own_four.shape[2]
-    groups = 2 * own_four.shape[0]
+    groups = 4 * own_four.shape[0]
 
     def late_pair(i, scalars):
         at = jnp.clip(i - 1, 0, 3)
@@ -566,13 +566,20 @@
         gathered[:, -sums.shape[0] :],
         tok_cand,
     )
-    across_four = to_vmem(across_four)
-    grad_own, across_four, *factor = lax.optimization_barrier((grad_own, across_four, *factor))
+    near, far = (
+        [
+            lax.dynamic_slice(four, (2 * which, 0, 0), (2, CAND_DEV, width))
+            for four in (own_four, across_four)
+        ]
+        for which in (core, 1 - core)
+    )
+    grad_own, *held = lax.optimization_barrier((grad_own, *near, *far, *factor))
+    near, far, factor = held[:2], held[2:4], held[4:]
     grad_other = lax.ppermute(grad_own, "tp", CORE_PAIRS)
-    start = own_back(scalars, grad_own, own_four, across_four)
+    start = own_back(scalars, grad_own, *near)
     return tuple(
         gradients(
-            scalars, gathered, gathered_other, grad_own, grad_other, own_four, across_four, start, *factor
+            scalars, gathered, gathered_other, grad_own, grad_other, *far, start, *factor
         )
     )
 

time: 269 us -> 269 us (level)
  local copies, waits for them, and re-layouts: 18.8 us -> 25.2 us
  Pallas kernels: 40.8 us -> 37.1 us
  waiting for transfers between devices: 79.4 us -> 76.5 us
    dynamic_slice x0 -> x2, local copies, waits for them, and re-layouts: none -> 5.88 us  [shards(): lax.dynamic_slice(four, (2 * which, 0, 0), (2, CAND_DEV, width))]
    all_to_all x4, waiting for transfers between devices: 41.8 us -> 38.8 us  [exchange(): return lax.all_to_all(blocks, axis, 0, 0, axis_index_groups=groups)]
    unnamed x48 -> x50, local copies, waits for them, and re-layouts: 16.1 us -> 16.7 us
  transfers between devices with their start and end apart: 13 -> 13, of which waited for: 10 -> 10; matrix products, arithmetic and copies ran while one was open for 3% -> 6% of each run, Pallas kernels for 6% -> 5%
where the time goes in v5:
time: 269 us; the launch traced here: 268 us
  waiting for transfers between devices  76.5 us (28%)
  blocking collectives  76.3 us (28%)
  Pallas kernels  37.1 us (14%)
  starting transfers between devices  31.8 us (12%)
  local copies, waits for them, and re-layouts  25.2 us (9%)
  between operations  14.1 us (5%)
  other arithmetic  4.11 us (2%)
  matrix products  3.15 us (1%)
    all_to_all x3, blocking collectives, exchange(): return lax.all_to_all(blocks, axis, 0, 0, axis_index_groups=groups)  76.3 us
    all_to_all x4, waiting for transfers between devices, exchange(): return lax.all_to_all(blocks, axis, 0, 0, axis_index_groups=groups)  38.8 us
    all_to_all x4, starting transfers between devices, exchange(): return lax.all_to_all(blocks, axis, 0, 0, axis_index_groups=groups)  21.4 us
    pallas_call x1, Pallas kernels, gradients(): pl.pallas_call(gradient_kernel, out_shape=[out, out, jax.ShapeDtypeStruct...  19.4 us
    unnamed x50, local copies, waits for them, and re-layouts  16.7 us
    ppermute x1, waiting for transfers between devices, shards(): res_across = lax.ppermute(res_half, 'cand', ACROSS_Z)  12.5 us
    all_gather x1, waiting for transfers between devices, shards(): gathered = lax.all_gather(payload, 'cand', axis=0, axis_index_groups=SAME_Z)  9.41 us
    all_gather x1, waiting for transfers between devices, shards(): lax.all_gather(down_across, 'cand', axis=0, axis_index_groups=SAME_Z)  6.03 us
  transfers between devices with their start and end apart: 13, of which 10 were waited for; matrix products, arithmetic and copies ran while one was open for 6% of the time, Pallas kernels for 5%

profile of v5, /device:TPU:1, one launch (start us, length us, event | category | flops | bytes accessed | tf_op | source)
XLA Modules:
  0.0 268.3 jit_solution(3381128086312551830)
XLA Ops:
  7.8 3.3 %project_qkv.1 = (bf16[512,640]{1,0:T(8,128)(2,1)}, bf16[512,512]{1,0:T(8,128)(2,1)}) custom-call(s32[3]{0:T(128)} %pad_add_fusion.1.scalars, bf16[512,512]{1,0:T(8,128)(2,1)} %refs_1_.4, f32[1,512]{1,0:T(1,128)} %bitcast.73, bf16[512,256]{1,0:T(8,128)(2,1)} %refs_0_.2, bf16[512,1024]{1,0:T(8,128)(2,1)} %refs_1_.3, bf16[512,1024]{1,0:T(8,128)(2,1)} %refs_2_.1), custom_call_target="tpu_custom_call" | custom-call | flops 335544320 | bytes 1310720 | tf_op jit(solution)/shard_map/project_qkv/pallas_call | solution.py:77
  11.1 20.8 %all_to_all.35.refs_0_ = bf16[8,64,640]{2,1,0:T(8,128)(2,1)S(1)} all-to-all(bf16[8,64,640]{2,1,0:T(8,128)(2,1)} %bitcast.69), channel_id=1, replica_groups=mesh['cand'=8,'tp'=16] {'cand'}, dimensions={0} | all-to-all | bytes 1310720 | tf_op jit(solution)/shard_map/all_to_all | solution.py:29
  33.0 3.5 %all-to-all-start.1 = ((bf16[8,64,512]{2,1,0:T(8,128)(2,1)}), bf16[8,64,512]{2,1,0:T(8,128)(2,1)S(1)}, u32[]{:S(2)}, u32[]{:S(2)}) async-start(bf16[8,64,512]{2,1,0:T(8,128)(2,1)} %sum_qkv.1), calls=%async_computation.1 | async-start | bytes 1048576 | tf_op jit(solution)/shard_map/all_to_all | solution.py:29
  37.6 2.9 %collective-permute-start = (bf16[768,512]{1,0:T(8,128)(2,1)}, bf16[768,512]{1,0:T(8,128)(2,1)S(1)}, u32[]{:S(2)}, u32[]{:S(2)}) collective-permute-start(bf16[768,512]{1,0:T(8,128)(2,1)} %slice.21), channel_id=1, source_target_pairs={{0,64},{16,80},{32,96},{48,112},{64,0},{80,16},{96,32},{112,48},{1... | collective-permute-start | bytes 2359304 | tf_op jit(solution)/shard_map/ppermute | solution.py:491
  40.5 7.2 %all-to-all-done.1 = bf16[8,64,512]{2,1,0:T(8,128)(2,1)S(1)} async-done(((bf16[8,64,512]{2,1,0:T(8,128)(2,1)}), bf16[8,64,512]{2,1,0:T(8,128)(2,1)S(1)}, u32[]{:S(2)}, u32[]{:S(2)}) %all-to-all-start.1) | async-done | bytes 524320 | tf_op jit(solution)/shard_map/all_to_all | solution.py:29
  51.1 7.8 %all-to-all-start.2 = ((bf16[16,32,512]{2,1,0:T(8,128)(2,1)}), bf16[16,32,512]{2,1,0:T(8,128)(2,1)S(1)}, u32[]{:S(2)}, u32[]{:S(2)}) async-start(bf16[16,32,512]{2,1,0:T(8,128)(2,1)} %bitcast.14), calls=%async_computation.2 | async-start | bytes 1048576 | tf_op jit(solution)/shard_map/all_to_all | solution.py:29
  58.9 3.8 %collective-permute-done = bf16[768,512]{1,0:T(8,128)(2,1)S(1)} collective-permute-done((bf16[768,512]{1,0:T(8,128)(2,1)}, bf16[768,512]{1,0:T(8,128)(2,1)S(1)}, u32[]{:S(2)}, u32[]{:S(2)}) %collective-permute-start) | collective-permute-done | bytes 786464 | tf_op jit(solution)/shard_map/ppermute | solution.py:491
  62.7 5.8 %all-to-all-done.2.refs_0_ = bf16[16,32,512]{2,1,0:T(8,128)(2,1)S(1)} async-done(((bf16[16,32,512]{2,1,0:T(8,128)(2,1)}), bf16[16,32,512]{2,1,0:T(8,128)(2,1)S(1)}, u32[]{:S(2)}, u32[]{:S(2)}) %all-to-all-start.2) | async-done | bytes 524320 | tf_op jit(solution)/shard_map/all_to_all | solution.py:29
  68.6 14.8 %all_to_all.36 = bf16[16,32,512]{2,1,0:T(8,128)(2,1)S(1)} all-to-all(bf16[16,32,512]{2,1,0:T(8,128)(2,1)S(1)} %sum_attention.1), channel_id=1, replica_groups=mesh['cand'=8,'tp'=16] {'tp'}, dimensions={0} | all-to-all | bytes 1048576 | tf_op jit(solution)/shard_map/all_to_all | solution.py:29
  88.0 4.6 %all-to-all-start.4 = ((bf16[8,64,1920]{2,1,0:T(8,128)(2,1)}), bf16[8,64,1920]{2,1,0:T(8,128)(2,1)S(1)}, u32[]{:S(2)}, u32[]{:S(2)}) async-start(bf16[8,64,1920]{2,1,0:T(8,128)(2,1)} %bitcast.58), calls=%async_computation.4 | async-start | bytes 3932160 | tf_op jit(solution)/shard_map/all_to_all | solution.py:29
  92.6 3.0 %collective-permute-start.1 = (bf16[256,512]{1,0:T(8,128)(2,1)S(1)}, bf16[256,512]{1,0:T(8,128)(2,1)S(1)}, u32[]{:S(2)}, u32[]{:S(2)}) collective-permute-start(bf16[256,512]{1,0:T(8,128)(2,1)S(1)} %constant_dynamic-slice_fusion.4.res_half), channel_id=1, source_target_pairs={{0,64},{16,80},{32,96},{48,112},{64,0},{80,16},{96,32},{112,48},{1... | collective-permute-start | bytes 786440 | tf_op jit(solution)/shard_map/ppermute | solution.py:539
  100.0 12.5 %collective-permute-done.1.res_across = bf16[256,512]{1,0:T(8,128)(2,1)S(1)} collective-permute-done((bf16[256,512]{1,0:T(8,128)(2,1)S(1)}, bf16[256,512]{1,0:T(8,128)(2,1)S(1)}, u32[]{:S(2)}, u32[]{:S(2)}) %collective-permute-start.1) | collective-permute-done | bytes 262176 | tf_op jit(solution)/shard_map/ppermute | solution.py:539
  112.5 16.8 %all-to-all-done.4.received = bf16[8,64,1920]{2,1,0:T(8,128)(2,1)S(1)} async-done(((bf16[8,64,1920]{2,1,0:T(8,128)(2,1)}), bf16[8,64,1920]{2,1,0:T(8,128)(2,1)S(1)}, u32[]{:S(2)}, u32[]{:S(2)}) %all-to-all-start.4) | async-done | bytes 1966112 | tf_op jit(solution)/shard_map/all_to_all | solution.py:29
  131.3 5.0 %collective-permute-done.2.across = bf16[896,128]{1,0:T(8,128)(2,1)S(1)} collective-permute-done((bf16[896,128]{1,0:T(8,128)(2,1)S(1)}, bf16[896,128]{1,0:T(8,128)(2,1)S(1)}, u32[]{:S(2)}, u32[]{:S(2)}) %collective-permute-start.2) | collective-permute-done | bytes 229408 | tf_op jit(solution)/shard_map/ppermute | solution.py:543
  137.3 6.0 %all-gather.9.cloned.1.call-done = bf16[3072,512]{1,0:T(8,128)(2,1)} async-done(((bf16[768,512]{1,0:T(8,128)(2,1)}), bf16[3072,512]{1,0:T(8,128)(2,1)}) %all-gather.9.cloned.1.call-update) | async-done | bytes 3145744 | tf_op jit(solution)/shard_map/all_gather | solution.py:537
  146.8 2.9 %dropped_output.3 = bf16[8,2,4,32,512]{4,3,2,1,0:T(8,128)(2,1)S(1)} custom-call(s32[11]{0:T(128)S(1)} %pad_add_fusion.scalars, bf16[64,896]{1,0:T(8,128)(2,1)S(1)} %get-tuple-element.49.own, bf16[896,128]{1,0:T(8,128)(2,1)S(1)} %collective-permute-done.2.across, bf16[4,896,512]{2,1,0:T(8,128)(2,1)S(1)} %copy-done.3), custom_call_target="tpu_custom_call" | custom-call | flops 1879048192 | bytes 5767168 | tf_op jit(solution)/shard_map/dropped_output/pallas_call | solution.py:231
  150.2 2.9 %dropped_output.2 = bf16[8,2,4,32,512]{4,3,2,1,0:T(8,128)(2,1)S(1)} custom-call(s32[11]{0:T(128)S(1)} %pad_add_fusion.scalars, bf16[64,896]{1,0:T(8,128)(2,1)S(1)} %get-tuple-element.49.own, bf16[896,128]{1,0:T(8,128)(2,1)S(1)} %collective-permute-done.2.across, bf16[4,896,512]{2,1,0:T(8,128)(2,1)S(1)} %copy-done.3), custom_call_target="tpu_custom_call" | custom-call | flops 1879048192 | bytes 5767168 | tf_op jit(solution)/shard_map/dropped_output/pallas_call | solution.py:231
  154.9 40.6 %all_to_all.37 = bf16[64,32,512]{2,1,0:T(8,128)(2,1)S(1)} all-to-all(bf16[64,32,512]{2,1,0:T(8,128)(2,1)S(1)} %bitcast.64), channel_id=1, replica_groups={{0,2,4,6,8,10,12,14,16,18,20,22,24,26,28,30,32,34,36,38,40,42,44,46,48,..., dimensions={0} | all-to-all | bytes 4194304 | tf_op jit(solution)/shard_map/all_to_all | solution.py:29
  197.4 5.6 %all-to-all-start.6 = ((bf16[8,8,32,512]{3,2,1,0:T(8,128)(2,1)}), bf16[8,8,32,512]{3,2,1,0:T(8,128)(2,1)S(1)}, u32[]{:S(2)}, u32[]{:S(2)}) async-start(bf16[8,8,32,512]{3,2,1,0:T(8,128)(2,1)} %copy-done.4), calls=%async_computation.6 | async-start | bytes 4194304 | tf_op jit(solution)/shard_map/all_to_all | solution.py:29
  202.9 9.4 %all-gather.11.cloned.1.call-done = bf16[15360,128]{1,0:T(8,128)(2,1)} async-done(((bf16[3840,128]{1,0:T(8,128)(2,1)}), bf16[15360,128]{1,0:T(8,128)(2,1)}) %all-gather.11.cloned.1.call-update) | async-done | bytes 3932176 | tf_op jit(solution)/shard_map/all_gather | solution.py:555
  213.0 4.0 %constant_dynamic-slice_fusion.1 = (bf16[2,768,512]{2,1,0:T(8,128)(2,1)}, bf16[2,768,512]{2,1,0:T(8,128)(2,1)}) fusion(bf16[4,896,512]{2,1,0:T(8,128)(2,1)} %copy-done.2, s32[]{:T(128)S(6)} %select_n.46, s32[]{:T(128)S(6)} %select_n.45), kind=kLoop, calls=%fused_computation.21 | loop fusion | bytes 6291464 | tf_op jit(solution)/shard_map/dynamic_slice | solution.py:571
  224.2 9.0 %all-to-all-done.6 = bf16[8,8,32,512]{3,2,1,0:T(8,128)(2,1)S(1)} async-done(((bf16[8,8,32,512]{3,2,1,0:T(8,128)(2,1)}), bf16[8,8,32,512]{3,2,1,0:T(8,128)(2,1)S(1)}, u32[]{:S(2)}, u32[]{:S(2)}) %all-to-all-start.6) | async-done | bytes 2097184 | tf_op jit(solution)/shard_map/all_to_all | solution.py:29
  237.8 2.4 own_back.1.start
  242.3 19.4 %gradients.1 = (bf16[1,4096,768]{2,1,0:T(8,128)(2,1)}, bf16[1,4096,768]{2,1,0:T(8,128)(2,1)}, bf16[1,768,4096]{2,1,0:T(8,128)(2,1)}) custom-call(s32[11]{0:T(128)S(1)} %pad_add_fusion.scalars, bf16[4,3840,128]{2,1,0:T(8,128)(2,1)S(1)} %bitcast.61, bf16[4,3840,128]{2,1,0:T(8,128)(2,1)} %collective-permute-done.3.res_2, ...), custom_call_target="tpu_custom_call" | custom-call | flops 11274289152 | bytes 41943040 | tf_op jit(solution)/shard_map/gradients/pallas_call | solution.py:418
  (87 shorter events, 40.3 us)
Async XLA Ops:
  7.2 42.8 %copy-start = (bf16[256,512]{1,0:T(8,128)(2,1)S(1)}, bf16[256,512]{1,0:T(8,128)(2,1)}, u32[]{:S(2)}) copy-start(bf16[256,512]{1,0:T(8,128)(2,1)} %param.18) | copy-start | bytes 786436
  7.2 76.3 %all-gather.7.cloned.1.call-start = ((), (), s32[]{:S(2)}) async-start(), calls=%async_computation.7 | async-start | bytes 4587520 | tf_op jit(solution)/shard_map/all_gather | solution.py:490
  11.1 25.3 %copy-start.23 = (s32[512]{0:T(512)S(1)}, s32[512]{0:T(512)}, u32[]{:S(2)}) copy-start(s32[512]{0:T(512)} %param.22) | copy-start | bytes 6148
  11.1 25.6 %copy-start.20 = (bf16[896,512]{1,0:T(8,128)(2,1)S(1)}, bf16[896,512]{1,0:T(8,128)(2,1)}, u32[]{:S(2)}) copy-start(bf16[896,512]{1,0:T(8,128)(2,1)} %param.21) | copy-start | bytes 2752516
  33.0 14.8 %all-to-all-start.1 = ((bf16[8,64,512]{2,1,0:T(8,128)(2,1)}), bf16[8,64,512]{2,1,0:T(8,128)(2,1)S(1)}, u32[]{:S(2)}, u32[]{:S(2)}) async-start(bf16[8,64,512]{2,1,0:T(8,128)(2,1)} %sum_qkv.1), calls=%async_computation.1 | async-start | bytes 1048576 | tf_op jit(solution)/shard_map/all_to_all | solution.py:29
  37.6 25.1 %collective-permute-start = (bf16[768,512]{1,0:T(8,128)(2,1)}, bf16[768,512]{1,0:T(8,128)(2,1)S(1)}, u32[]{:S(2)}, u32[]{:S(2)}) collective-permute-start(bf16[768,512]{1,0:T(8,128)(2,1)} %slice.21), channel_id=1, source_target_pairs={{0,64},{16,80},{32,96},{48,112},{64,0},{80,16},{96,32},{112,48},{1... | collective-permute-start | bytes 2359304 | tf_op jit(solution)/shard_map/ppermute | solution.py:491
  49.9 18.6 %copy-start.8 = (bf16[512,512]{1,0:T(8,128)(2,1)S(1)}, bf16[512,512]{1,0:T(8,128)(2,1)}, u32[]{:S(2)}) copy-start(bf16[512,512]{1,0:T(8,128)(2,1)} %refs_1_.4) | copy-start | bytes 1572868
  51.1 32.4 %copy-start.13 = (bf16[512,896]{1,0:T(8,128)(2,1)S(1)}, bf16[512,896]{1,0:T(8,128)(2,1)}, u32[]{:S(2)}) copy-start(bf16[512,896]{1,0:T(8,128)(2,1)} %refs_0_.3) | copy-start | bytes 2752516
  51.1 32.4 %copy-start.19 = (f32[512]{0:T(512)S(1)}, f32[512]{0:T(512)}, u32[]{:S(2)}) copy-start(f32[512]{0:T(512)} %param.14) | copy-start | bytes 6148
  51.1 17.4 %all-to-all-start.2 = ((bf16[16,32,512]{2,1,0:T(8,128)(2,1)}), bf16[16,32,512]{2,1,0:T(8,128)(2,1)S(1)}, u32[]{:S(2)}, u32[]{:S(2)}) async-start(bf16[16,32,512]{2,1,0:T(8,128)(2,1)} %bitcast.14), calls=%async_computation.2 | async-start | bytes 1048576 | tf_op jit(solution)/shard_map/all_to_all | solution.py:29
  58.9 84.4 %all-gather.9.cloned.1.call-start = ((), (), s32[]{:S(2)}) async-start(), calls=%async_computation.8 | async-start | bytes 3932160 | tf_op jit(solution)/shard_map/all_gather | solution.py:537
  62.7 24.0 %copy-start.22 = (bf16[768,512]{1,0:T(8,128)(2,1)}, bf16[768,512]{1,0:T(8,128)(2,1)S(1)}, u32[]{:S(2)}) copy-start(bf16[768,512]{1,0:T(8,128)(2,1)S(1)} %collective-permute-done) | copy-start | bytes 2359300
  88.0 41.3 %all-to-all-start.4 = ((bf16[8,64,1920]{2,1,0:T(8,128)(2,1)}), bf16[8,64,1920]{2,1,0:T(8,128)(2,1)S(1)}, u32[]{:S(2)}, u32[]{:S(2)}) async-start(bf16[8,64,1920]{2,1,0:T(8,128)(2,1)} %bitcast.58), calls=%async_computation.4 | async-start | bytes 3932160 | tf_op jit(solution)/shard_map/all_to_all | solution.py:29
  92.5 119.8 %all-gather.11.cloned.1.call-start = ((), (), s32[]{:S(2)}) async-start(), calls=%async_computation.9 | async-start | bytes 4915200 | tf_op jit(solution)/shard_map/all_gather | solution.py:555
  92.6 19.9 %collective-permute-start.1 = (bf16[256,512]{1,0:T(8,128)(2,1)S(1)}, bf16[256,512]{1,0:T(8,128)(2,1)S(1)}, u32[]{:S(2)}, u32[]{:S(2)}) collective-permute-start(bf16[256,512]{1,0:T(8,128)(2,1)S(1)} %constant_dynamic-slice_fusion.4.res_half), channel_id=1, source_target_pairs={{0,64},{16,80},{32,96},{48,112},{64,0},{80,16},{96,32},{112,48},{1... | collective-permute-start | bytes 786440 | tf_op jit(solution)/shard_map/ppermute | solution.py:539
  129.8 13.6 %copy-start.24 = (s32[8]{0:T(128)S(1)}, s32[8]{0:T(128)}, u32[]{:S(2)}) copy-start(s32[8]{0:T(128)} %param.23) | copy-start | bytes 100
  129.8 6.5 %collective-permute-start.2 = (bf16[896,128]{1,0:T(8,128)(2,1)S(1)}, bf16[896,128]{1,0:T(8,128)(2,1)S(1)}, u32[]{:S(2)}, u32[]{:S(2)}) collective-permute-start(bf16[896,128]{1,0:T(8,128)(2,1)S(1)} %get-tuple-element.46), channel_id=1, source_target_pairs={{0,64},{16,80},{32,96},{48,112},{64,0},{80,16},{96,32},{112,48},{1... | collective-permute-start | bytes 688136 | tf_op jit(solution)/shard_map/ppermute | solution.py:543
  149.7 4.4 %collective-permute-start.4 = (bf16[8,2,4,32,512]{4,3,2,1,0:T(8,128)(2,1)S(1)}, bf16[8,2,4,32,512]{4,3,2,1,0:T(8,128)(2,1)S(1)}, u32[]{:S(2)}, u32[]{:S(2)}) collective-permute-start(bf16[8,2,4,32,512]{4,3,2,1,0:T(8,128)(2,1)S(1)} %dropped_output.3), channel_id=1, source_target_pairs={{0,1},{1,0},{2,3},{3,2},{4,5},{5,4},{6,7},{7,6},{8,9},{9,8},{10,11... | collective-permute-start | bytes 6291464 | tf_op jit(solution)/shard_map/ppermute | solution.py:550
  197.4 35.9 %all-to-all-start.6 = ((bf16[8,8,32,512]{3,2,1,0:T(8,128)(2,1)}), bf16[8,8,32,512]{3,2,1,0:T(8,128)(2,1)S(1)}, u32[]{:S(2)}, u32[]{:S(2)}) async-start(bf16[8,8,32,512]{3,2,1,0:T(8,128)(2,1)} %copy-done.4), calls=%async_computation.6 | async-start | bytes 4194304 | tf_op jit(solution)/shard_map/all_to_all | solution.py:29
  212.4 27.8 %collective-permute-start.3 = (bf16[4,3840,128]{2,1,0:T(8,128)(2,1)}, bf16[4,3840,128]{2,1,0:T(8,128)(2,1)}, u32[]{:S(2)}, u32[]{:S(2)}) collective-permute-start(bf16[4,3840,128]{2,1,0:T(8,128)(2,1)} %bitcast.59), channel_id=1, source_target_pairs={{0,1},{1,0},{2,3},{3,2},{4,5},{5,4},{6,7},{7,6},{8,9},{9,8},{10,11... | collective-permute-start | bytes 11796488 | tf_op jit(solution)/shard_map/ppermute | solution.py:560
  213.0 4.0 %copy-start.21 = (bf16[3072,512]{1,0:T(8,128)(2,1)S(1)}, bf16[3072,512]{1,0:T(8,128)(2,1)}, u32[]{:S(2)}) copy-start(bf16[3072,512]{1,0:T(8,128)(2,1)} %all-gather.9.cloned.1.call-done) | copy-start | bytes 9437188
  233.3 6.9 %collective-permute-start.5 = (bf16[2,4,2,4,32,512]{5,4,3,2,1,0:T(8,128)(2,1)S(1)}, bf16[2,4,2,4,32,512]{5,4,3,2,1,0:T(8,128)(2,1)S(1)}, u32[]{:S(2)}, u32[]{:S(2)}) collective-permute-start(bf16[2,4,2,4,32,512]{5,4,3,2,1,0:T(8,128)(2,1)S(1)} %bitcast.53), channel_id=1, source_target_pairs={{0,1},{1,0},{2,3},{3,2},{4,5},{5,4},{6,7},{7,6},{8,9},{9,8},{10,11... | collective-permute-start | bytes 6291464 | tf_op jit(solution)/shard_map/ppermute | solution.py:578
  237.8 2.4 copy-start.18
  242.3 19.5 %copy-start.1 = (bf16[256,512]{1,0:T(8,128)(2,1)S(1)}, bf16[256,512]{1,0:T(8,128)(2,1)}, u32[]{:S(2)}) copy-start(bf16[256,512]{1,0:T(8,128)(2,1)} %param.18) | copy-start | bytes 786436
  (14 other events, 23.9 us)
Sparse Core Ops, SparseCore 0:
  32.1 43.8 all-gather.6
  88.1 55.1 all-gather.8
  145.6 66.7 all-gather.10
